TPU v7x, 32 devices: a whole 2x2x4 slice. The times are simulated.
32 devices in a mesh: dp: 16 (over z, x, core), tensor: 2 (over y).
Axes of the slice: x: 2, y: 2, z: 4, core: 2. Of those that a mesh axis runs over, the one named last changes fastest.
Arguments:
- text_rows: bfloat16 [32, 512, 768], P('dp'), may hold values from -6 to 6
- vision_rows: bfloat16 [32, 256, 768], P('dp'), may hold values from -6 to 6
- segment_ids: int32 [32, 512], P('dp'), may hold values from 0 to 63, never falling along the last dimension, each value on 1 to 256 neighbouring positions
- text_keep: int32 [32, 512], P('dp'), may hold values 0 or 1
- segment_box: int32 [32, 64, 2], P('dp'), may hold values from 0 to 15
- patch_keep: int32 [32, 256], P('dp'), may hold values 0 or 1
- attn_qkv_a: bfloat16 [768, 3, 768], P('dp', None, 'tensor'), may hold values from -0.21875 to 0.21875
- attn_out_a: bfloat16 [768, 768], P('tensor', 'dp'), may hold values from -1.75 to 1.75
- mlp_in_a: bfloat16 [768, 3072], P('dp', 'tensor'), may hold values from -0.21875 to 0.21875
- mlp_out_a: bfloat16 [3072, 768], P('tensor', 'dp'), may hold values from -0.109375 to 0.109375
- norm_gain_a: bfloat16 [2, 768], P(None, 'dp'), may hold values from 0.5 to 1.5
- norm_shift_a: bfloat16 [2, 768], P(None, 'dp'), may hold values from -4 to 4
- box_table_a: bfloat16 [12, 2, 31], P('tensor'), may hold values from -6 to 6
- attn_query_b: bfloat16 [768, 768], P('dp', 'tensor'), may hold values from -0.21875 to 0.21875
- attn_kv_b: bfloat16 [768, 2, 768], P('dp', None, 'tensor'), may hold values from -0.21875 to 0.21875
- attn_out_b: bfloat16 [768, 768], P('tensor', 'dp'), may hold values from -1.75 to 1.75
- mlp_in_b: bfloat16 [768, 3072], P('dp', 'tensor'), may hold values from -0.21875 to 0.21875
- mlp_out_b: bfloat16 [3072, 768], P('tensor', 'dp'), may hold values from -0.109375 to 0.109375
- norm_gain_b: bfloat16 [2, 768], P(None, 'dp'), may hold values from 0.5 to 1.5
- norm_shift_b: bfloat16 [2, 768], P(None, 'dp'), may hold values from -4 to 4
- box_table_b: bfloat16 [12, 2, 31], P('tensor'), may hold values from -6 to 6
- out_grad: bfloat16 [32, 512, 768], P('dp', 'tensor'), may hold values from -6 to 6
Outputs:
- layer_out: bfloat16 [32, 512, 768], P('dp', 'tensor')
- text_grad: float32 [32, 512, 768], P('dp', 'tensor')
- vision_grad: float32 [32, 256, 768], P('dp', 'tensor')
- grad_qkv_a: float32 [768, 3, 768], P('dp', None, 'tensor')
- grad_out_a: float32 [768, 768], P('tensor', 'dp')
- grad_in_a: float32 [768, 3072], P('dp', 'tensor')
- grad_mlp_a: float32 [3072, 768], P('tensor', 'dp')
- grad_gain_a: float32 [2, 768], P(None, 'dp')
- grad_shift_a: float32 [2, 768], P(None, 'dp')
- grad_table_a: float32 [12, 2, 31], P('tensor')
- grad_query_b: float32 [768, 768], P('dp', 'tensor')
- grad_kv_b: float32 [768, 2, 768], P('dp', None, 'tensor')
- grad_out_b: float32 [768, 768], P('tensor', 'dp')
- grad_in_b: float32 [768, 3072], P('dp', 'tensor')
- grad_mlp_b: float32 [3072, 768], P('tensor', 'dp')
- grad_gain_b: float32 [2, 768], P(None, 'dp')
- grad_shift_b: float32 [2, 768], P(None, 'dp')
- grad_table_b: float32 [12, 2, 31], P('tensor')
Inputs may be any that keep to these rules, and one draw needn't show every extreme that they name: `segment_ids`: each page's segment numbers never fall, every one of the 64 segments has a token, and one segment holds 512 // 2 tokens.
All inputs are finite; a program needn't handle non-finite values. No bound on the sum of `text_keep` or of `patch_keep` on one device may be relied on, other than what follows from the above.
Results may differ from a plain program's by a relative error of at most 0.025.
Values may be sent and summed in bfloat16 or wider, within the bound.
No kernel may reach another device: no remote copies, remote signals or barrier semaphores. Data moves between devices by JAX's collectives and lax.ppermute only.
A program may use at most 192 MiB of HBM per device.

v0:
```python
import jax
import jax.numpy as jnp
from jax import lax
from jax.sharding import PartitionSpec as P

HD = 64
GRID = 16
MICRO = 2


highest = lax.Precision.HIGHEST
epsilon = 1e-06
masked_score = -30000.0


def cast_low(values):
    return values.astype(jnp.bfloat16)


def matmul(left_side, right_side):
    return jnp.dot(left_side, right_side, preferred_element_type=jnp.float32)


def matmul_tn(left_side, right_side):
    return lax.dot_general(
        left_side, right_side, (((0,), (0,)), ((), ())), preferred_element_type=jnp.float32
    )


def matmul_nt(left_side, right_side):
    return lax.dot_general(
        left_side, right_side, (((1,), (1,)), ((), ())), preferred_element_type=jnp.float32
    )


def norm_rows(values, norm_gain, norm_shift):
    center = values - jnp.mean(values, axis=-1, keepdims=True)
    spread = jnp.mean(center * center, axis=-1, keepdims=True)
    return center * lax.rsqrt(spread + epsilon) * norm_gain + norm_shift


def gelu_exact(values):
    return jax.nn.gelu(values, approximate=False)


def grid_hot(coords):
    return (coords[..., None] == jnp.arange(GRID, dtype=jnp.int32)).astype(jnp.float32)


def relation():
    offset = (
        jnp.arange(GRID, dtype=jnp.int32)[:, None]
        - jnp.arange(GRID, dtype=jnp.int32)[None, :]
        + GRID
        - 1
    )
    return (offset[:, :, None] == jnp.arange(2 * GRID - 1, dtype=jnp.int32)[None, None, :]).astype(
        jnp.float32
    )


def box_bias(bias_table, row_hot, col_hot):
    pairwise = jnp.einsum("hcr,abr->hcab", bias_table, relation(), precision=highest)
    row_part = jnp.einsum("pcia,hcab->phcib", row_hot, pairwise, precision=highest)
    return jnp.einsum("phcib,pcjb->phij", row_part, col_hot, precision=highest)


def box_bias_grad(score_grad, row_hot, col_hot):
    right_part = jnp.einsum(
        "phij,pcjb->phcib", score_grad, cast_low(col_hot), preferred_element_type=jnp.float32
    )
    pair_grad = jnp.einsum("phcib,pcia->hcab", right_part, row_hot, precision=highest)
    return jnp.einsum("hcab,abr->hcr", pair_grad, relation(), precision=highest)


def masked_scores(queries, key_rows, page_bias, key_keep):
    score_scale = queries.shape[-1] ** (-0.5)
    scores = (
        jnp.einsum("pqhd,pkhd->phqk", queries, key_rows, preferred_element_type=jnp.float32)
        * score_scale
        + page_bias
    )
    return jnp.where(key_keep[:, None, None, :] > 0, scores, masked_score)


def attend_forward(queries, key_rows, values, page_bias, key_keep):
    scores = masked_scores(queries, key_rows, page_bias, key_keep)
    row_max = jnp.max(scores, axis=-1, keepdims=True)
    exponent = jnp.exp(scores - row_max)
    row_total = jnp.sum(exponent, axis=-1, keepdims=True)
    attn_probs = cast_low(exponent / row_total)
    context = jnp.einsum("phqk,pkhd->pqhd", attn_probs, values, preferred_element_type=jnp.float32)
    log_total = row_max[..., 0] + jnp.log(row_total[..., 0])
    return (cast_low(context), log_total)


def attend_backward(queries, key_rows, values, page_bias, key_keep, log_total, context_grad):
    score_scale = queries.shape[-1] ** (-0.5)
    scores = masked_scores(queries, key_rows, page_bias, key_keep)
    attn_probs = jnp.exp(scores - log_total[..., None])
    prob_grad = jnp.einsum(
        "pqhd,pkhd->phqk", context_grad, values, preferred_element_type=jnp.float32
    )
    row_dot = jnp.sum(attn_probs * prob_grad, axis=-1, keepdims=True)
    score_grad = cast_low(attn_probs * (prob_grad - row_dot))
    query_grad = (
        jnp.einsum("phqk,pkhd->pqhd", score_grad, key_rows, preferred_element_type=jnp.float32)
        * score_scale
    )
    key_grad = (
        jnp.einsum("phqk,pqhd->pkhd", score_grad, queries, preferred_element_type=jnp.float32)
        * score_scale
    )
    value_grad = jnp.einsum(
        "phqk,pqhd->pkhd", cast_low(attn_probs), context_grad, preferred_element_type=jnp.float32
    )
    return (query_grad, key_grad, value_grad, score_grad)


def shards(
    text_rows,
    vision_rows,
    segment_ids,
    text_keep,
    segment_box,
    patch_keep,
    attn_qkv_a,
    attn_out_a,
    mlp_in_a,
    mlp_out_a,
    norm_gain_a,
    norm_shift_a,
    box_table_a,
    attn_query_b,
    attn_kv_b,
    attn_out_b,
    mlp_in_b,
    mlp_out_b,
    norm_gain_b,
    norm_shift_b,
    box_table_b,
    out_grad,
):
    page_count = text_rows.shape[0]
    length = text_rows.shape[1]
    patches = vision_rows.shape[1]
    model_width = text_rows.shape[2]
    local_width = attn_out_a.shape[0]
    local_heads = local_width // HD
    micro_pages = page_count // MICRO
    micro_rows = micro_pages * length
    micro_patches = micro_pages * patches
    share_len = length // lax.axis_size("tensor")
    share_start = lax.axis_index("tensor") * share_len
    token_box = jax.vmap(lambda page_box, page_ids: page_box[page_ids])(segment_box, segment_ids)
    text_hot = grid_hot(jnp.transpose(token_box, (0, 2, 1)))
    grid_index = jnp.arange(patches, dtype=jnp.int32)
    patch_hot = grid_hot(jnp.stack([grid_index % GRID, grid_index // GRID]))
    table_first_local = box_table_a.astype(jnp.float32)
    table_second_local = box_table_b.astype(jnp.float32)

    def branch_share(partial_rows):
        return lax.psum_scatter(partial_rows, "tensor", scatter_dimension=1, tiled=True)

    def input_share(partial_rows):
        return lax.psum_scatter(partial_rows, "tensor", scatter_dimension=1, tiled=True)

    def row_gather(share_rows):
        return lax.all_gather(share_rows, "tensor", axis=1, tiled=True)

    def grad_gather(share_rows):
        return lax.all_gather(share_rows, "tensor", axis=1, tiled=True)

    outputs = []
    text_grads = []
    vision_grads = []
    running = None
    for micro_index in range(MICRO):
        page_slice = slice(micro_index * micro_pages, (micro_index + 1) * micro_pages)
        first_weights = (
            lax.all_gather(attn_qkv_a, "dp", axis=0, tiled=True),
            lax.all_gather(attn_out_a, "dp", axis=1, tiled=True),
            lax.all_gather(mlp_in_a, "dp", axis=0, tiled=True),
            lax.all_gather(mlp_out_a, "dp", axis=1, tiled=True),
            lax.all_gather(norm_gain_a, "dp", axis=1, tiled=True),
            lax.all_gather(norm_shift_a, "dp", axis=1, tiled=True),
        )
        qkv_full, out_full_a, in_full_a, mlp_full_a, gain_pair_a, shift_pair_a = first_weights
        text_micro = text_rows[page_slice]
        keep_micro = text_keep[page_slice]
        hot_micro = text_hot[page_slice]
        text_share = lax.dynamic_slice_in_dim(text_micro, share_start, share_len, 1).astype(
            jnp.float32
        )
        text_flat = text_micro.reshape(micro_rows, model_width)
        mix_qkv = cast_low(matmul(text_flat, qkv_full.reshape(model_width, 3 * local_width)))
        mix_qkv = mix_qkv.reshape(micro_pages, length, 3, local_heads, HD)
        queries_a, key_rows_a, values_a = (mix_qkv[:, :, 0], mix_qkv[:, :, 1], mix_qkv[:, :, 2])
        bias_a = box_bias(table_first_local, hot_micro, hot_micro)
        context_a, lse_a = attend_forward(queries_a, key_rows_a, values_a, bias_a, keep_micro)
        context_a = context_a.reshape(micro_rows, local_width)
        attn_share_a = branch_share(
            matmul(context_a, out_full_a).reshape(micro_pages, length, model_width)
        )
        mixed_a, norm_back_a = jax.vjp(
            norm_rows,
            text_share + attn_share_a,
            gain_pair_a[0].astype(jnp.float32),
            shift_pair_a[0].astype(jnp.float32),
        )
        mixed_full_a = row_gather(cast_low(mixed_a)).reshape(micro_rows, model_width)
        hidden_a, gelu_back_a = jax.vjp(gelu_exact, matmul(mixed_full_a, in_full_a))
        gelu_rows_a = cast_low(hidden_a)
        mlp_share_a = branch_share(
            matmul(gelu_rows_a, mlp_full_a).reshape(micro_pages, length, model_width)
        )
        middle, norm2_back_a = jax.vjp(
            norm_rows,
            mixed_a + mlp_share_a,
            gain_pair_a[1].astype(jnp.float32),
            shift_pair_a[1].astype(jnp.float32),
        )
        second_weights = (
            lax.all_gather(attn_query_b, "dp", axis=0, tiled=True),
            lax.all_gather(attn_kv_b, "dp", axis=0, tiled=True),
            lax.all_gather(attn_out_b, "dp", axis=1, tiled=True),
            lax.all_gather(mlp_in_b, "dp", axis=0, tiled=True),
            lax.all_gather(mlp_out_b, "dp", axis=1, tiled=True),
            lax.all_gather(norm_gain_b, "dp", axis=1, tiled=True),
            lax.all_gather(norm_shift_b, "dp", axis=1, tiled=True),
        )
        query_full, kv_full, out_full_b, in_full_b, mlp_full_b, gain_pair_b, shift_pair_b = (
            second_weights
        )
        middle_full = row_gather(cast_low(middle)).reshape(micro_rows, model_width)
        queries_b = cast_low(matmul(middle_full, query_full)).reshape(
            micro_pages, length, local_heads, HD
        )
        vision_micro = vision_rows[page_slice].reshape(micro_patches, model_width)
        mix_kv = cast_low(matmul(vision_micro, kv_full.reshape(model_width, 2 * local_width)))
        mix_kv = mix_kv.reshape(micro_pages, patches, 2, local_heads, HD)
        key_rows_b, values_b = (mix_kv[:, :, 0], mix_kv[:, :, 1])
        patch_micro = jnp.broadcast_to(patch_hot, (micro_pages,) + patch_hot.shape)
        bias_b = box_bias(table_second_local, hot_micro, patch_micro)
        keep_patch = patch_keep[page_slice]
        context_b, lse_b = attend_forward(queries_b, key_rows_b, values_b, bias_b, keep_patch)
        context_b = context_b.reshape(micro_rows, local_width)
        attn_share_b = branch_share(
            matmul(context_b, out_full_b).reshape(micro_pages, length, model_width)
        )
        mixed_b, norm_back_b = jax.vjp(
            norm_rows,
            middle + attn_share_b,
            gain_pair_b[0].astype(jnp.float32),
            shift_pair_b[0].astype(jnp.float32),
        )
        mixed_full_b = row_gather(cast_low(mixed_b)).reshape(micro_rows, model_width)
        hidden_b, gelu_back_b = jax.vjp(gelu_exact, matmul(mixed_full_b, in_full_b))
        gelu_rows_b = cast_low(hidden_b)
        mlp_share_b = branch_share(
            matmul(gelu_rows_b, mlp_full_b).reshape(micro_pages, length, model_width)
        )
        final_rows, norm2_back_b = jax.vjp(
            norm_rows,
            mixed_b + mlp_share_b,
            gain_pair_b[1].astype(jnp.float32),
            shift_pair_b[1].astype(jnp.float32),
        )
        outputs.append(cast_low(final_rows))
        back_second = (
            lax.all_gather(attn_query_b, "dp", axis=0, tiled=True),
            lax.all_gather(attn_kv_b, "dp", axis=0, tiled=True),
            lax.all_gather(attn_out_b, "dp", axis=1, tiled=True),
            lax.all_gather(mlp_in_b, "dp", axis=0, tiled=True),
            lax.all_gather(mlp_out_b, "dp", axis=1, tiled=True),
        )
        query_back, kv_back, out_back_b, in_back_b, mlp_back_b = back_second
        pre_grad_b, gain_grad_b1, shift_grad_b1 = norm2_back_b(
            out_grad[page_slice].astype(jnp.float32)
        )
        branch_grad_b = grad_gather(cast_low(pre_grad_b)).reshape(micro_rows, model_width)
        grad_mlp_b = matmul_tn(gelu_rows_b, branch_grad_b)
        (hidden_grad_b,) = gelu_back_b(matmul_nt(branch_grad_b, mlp_back_b))
        hidden_grad_b = cast_low(hidden_grad_b)
        grad_in_b = matmul_tn(mixed_full_b, hidden_grad_b)
        mixed_grad_b = pre_grad_b + input_share(
            matmul_nt(hidden_grad_b, in_back_b).reshape(micro_pages, length, model_width)
        )
        attn_pre_b, gain_grad_b0, shift_grad_b0 = norm_back_b(mixed_grad_b)
        attn_grad_b = grad_gather(cast_low(attn_pre_b)).reshape(micro_rows, model_width)
        grad_out_b = matmul_tn(context_b, attn_grad_b)
        context_grad_b = cast_low(matmul_nt(attn_grad_b, out_back_b)).reshape(
            micro_pages, length, local_heads, HD
        )
        query_grad_b, key_grad_b, value_grad_b, score_grad_b = attend_backward(
            queries_b, key_rows_b, values_b, bias_b, keep_patch, lse_b, context_grad_b
        )
        query_grad_b = cast_low(query_grad_b).reshape(micro_rows, local_width)
        kv_grad_b = cast_low(jnp.stack([key_grad_b, value_grad_b], axis=2)).reshape(
            micro_patches, 2 * local_width
        )
        grad_query_b = matmul_tn(middle_full, query_grad_b)
        grad_kv_b = matmul_tn(vision_micro, kv_grad_b).reshape(model_width, 2, local_width)
        table_grad_b = box_bias_grad(score_grad_b, hot_micro, patch_micro)
        text_part, vision_part = (
            lax.psum_scatter(
                matmul_nt(query_grad_b, query_back)
                .reshape(micro_pages, length, model_width)
                .astype(jnp.bfloat16),
                "tensor",
                scatter_dimension=1,
                tiled=True,
            ).astype(jnp.float32),
            lax.psum_scatter(
                matmul_nt(kv_grad_b, kv_back.reshape(model_width, 2 * local_width))
                .reshape(micro_pages, patches, model_width)
                .astype(jnp.bfloat16),
                "tensor",
                scatter_dimension=1,
                tiled=True,
            ).astype(jnp.float32),
        )
        middle_grad = attn_pre_b + text_part
        vision_grads.append(vision_part)
        back_first = (
            lax.all_gather(attn_qkv_a, "dp", axis=0, tiled=True),
            lax.all_gather(attn_out_a, "dp", axis=1, tiled=True),
            lax.all_gather(mlp_in_a, "dp", axis=0, tiled=True),
            lax.all_gather(mlp_out_a, "dp", axis=1, tiled=True),
        )
        qkv_back, out_back_a, in_back_a, mlp_back_a = back_first
        pre_grad_a, gain_grad_a1, shift_grad_a1 = norm2_back_a(middle_grad)
        branch_grad_a = grad_gather(cast_low(pre_grad_a)).reshape(micro_rows, model_width)
        grad_mlp_a = matmul_tn(gelu_rows_a, branch_grad_a)
        (hidden_grad_a,) = gelu_back_a(matmul_nt(branch_grad_a, mlp_back_a))
        hidden_grad_a = cast_low(hidden_grad_a)
        grad_in_a = matmul_tn(mixed_full_a, hidden_grad_a)
        mixed_grad_a = pre_grad_a + input_share(
            matmul_nt(hidden_grad_a, in_back_a).reshape(micro_pages, length, model_width)
        )
        attn_pre_a, gain_grad_a0, shift_grad_a0 = norm_back_a(mixed_grad_a)
        attn_grad_a = grad_gather(cast_low(attn_pre_a)).reshape(micro_rows, model_width)
        grad_out_a = matmul_tn(context_a, attn_grad_a)
        context_grad_a = cast_low(matmul_nt(attn_grad_a, out_back_a)).reshape(
            micro_pages, length, local_heads, HD
        )
        query_grad_a, key_grad_a, value_grad_a, score_grad_a = attend_backward(
            queries_a, key_rows_a, values_a, bias_a, keep_micro, lse_a, context_grad_a
        )
        qkv_grad = cast_low(jnp.stack([query_grad_a, key_grad_a, value_grad_a], axis=2)).reshape(
            micro_rows, 3 * local_width
        )
        grad_qkv_a = matmul_tn(text_flat, qkv_grad).reshape(model_width, 3, local_width)
        table_grad_a = box_bias_grad(score_grad_a, hot_micro, hot_micro)
        text_grads.append(
            attn_pre_a
            + input_share(
                matmul_nt(qkv_grad, qkv_back.reshape(model_width, 3 * local_width)).reshape(
                    micro_pages, length, model_width
                )
            )
        )
        grads_first = (
            grad_qkv_a,
            grad_out_a,
            grad_in_a,
            grad_mlp_a,
            jnp.stack([gain_grad_a0, gain_grad_a1]),
            jnp.stack([shift_grad_a0, shift_grad_a1]),
        )
        grads_second = (
            grad_query_b,
            grad_kv_b,
            grad_out_b,
            grad_in_b,
            grad_mlp_b,
            jnp.stack([gain_grad_b0, gain_grad_b1]),
            jnp.stack([shift_grad_b0, shift_grad_b1]),
        )
        table_grads = (table_grad_a, table_grad_b)
        gain_first, shift_first, gain_second, shift_second = lax.psum(
            (grads_first[4], grads_first[5], grads_second[5], grads_second[6]), "tensor"
        )
        shared_first = (
            lax.psum_scatter(grads_first[0], "dp", scatter_dimension=0, tiled=True),
            lax.psum_scatter(grads_first[1], "dp", scatter_dimension=1, tiled=True),
            lax.psum_scatter(grads_first[2], "dp", scatter_dimension=0, tiled=True),
            lax.psum_scatter(grads_first[3], "dp", scatter_dimension=1, tiled=True),
            lax.psum_scatter(gain_first, "dp", scatter_dimension=1, tiled=True),
            lax.psum_scatter(shift_first, "dp", scatter_dimension=1, tiled=True),
        )
        shared_second = (
            lax.psum_scatter(grads_second[0], "dp", scatter_dimension=0, tiled=True),
            lax.psum_scatter(grads_second[1], "dp", scatter_dimension=0, tiled=True),
            lax.psum_scatter(grads_second[2], "dp", scatter_dimension=1, tiled=True),
            lax.psum_scatter(grads_second[3], "dp", scatter_dimension=0, tiled=True),
            lax.psum_scatter(grads_second[4], "dp", scatter_dimension=1, tiled=True),
            lax.psum_scatter(gain_second, "dp", scatter_dimension=1, tiled=True),
            lax.psum_scatter(shift_second, "dp", scatter_dimension=1, tiled=True),
        )
        table_first, table_second = lax.psum((table_grads[0], table_grads[1]), "dp")
        grads_first = tuple(shared_first)
        grads_second = tuple(shared_second)
        table_grads = (table_first, table_second)
        if running is None:
            running = (grads_first, grads_second, table_grads)
        else:
            running = jax.tree.map(jnp.add, running, (grads_first, grads_second, table_grads))
    grads_first, grads_second, table_grads = running
    return (
        jnp.concatenate(outputs, axis=0),
        jnp.concatenate(text_grads, axis=0),
        jnp.concatenate(vision_grads, axis=0),
        grads_first[0],
        grads_first[1],
        grads_first[2],
        grads_first[3],
        grads_first[4],
        grads_first[5],
        table_grads[0],
        grads_second[0],
        grads_second[1],
        grads_second[2],
        grads_second[3],
        grads_second[4],
        grads_second[5],
        grads_second[6],
        table_grads[1],
    )


def solution(mesh):
    return jax.shard_map(
        shards,
        mesh=mesh,
        in_specs=(
            P("dp", None, None),
            P("dp", None, None),
            P("dp", None),
            P("dp", None),
            P("dp", None, None),
            P("dp", None),
            P("dp", None, "tensor"),
            P("tensor", "dp"),
            P("dp", "tensor"),
            P("tensor", "dp"),
            P(None, "dp"),
            P(None, "dp"),
            P("tensor", None, None),
            P("dp", "tensor"),
            P("dp", None, "tensor"),
            P("tensor", "dp"),
            P("dp", "tensor"),
            P("tensor", "dp"),
            P(None, "dp"),
            P(None, "dp"),
            P("tensor", None, None),
            P("dp", "tensor", None),
        ),
        out_specs=(
            P("dp", "tensor", None),
            P("dp", "tensor", None),
            P("dp", "tensor", None),
            P("dp", None, "tensor"),
            P("tensor", "dp"),
            P("dp", "tensor"),
            P("tensor", "dp"),
            P(None, "dp"),
            P(None, "dp"),
            P("tensor", None, None),
            P("dp", "tensor"),
            P("dp", None, "tensor"),
            P("tensor", "dp"),
            P("dp", "tensor"),
            P("tensor", "dp"),
            P(None, "dp"),
            P(None, "dp"),
            P("tensor", None, None),
        ),
        check_vma=False,
    )
```

profile of v0, /device:TPU:0, one launch (start us, length us, event | category | flops | bytes accessed | tf_op | source)
XLA Modules:
  0.0 1808.4 jit_solution(7097482248224523781)
XLA Ops:
  19.4 26.7 %all_gather.55 = bf16[384,768]{0,1:T(8,128)(2,1)} all-gather(bf16[384,48]{0,1:T(8,128)(2,1)S(1)} %copy-done.149), channel_id=1, replica_groups=mesh['dp'=16,'tensor'=2] {'dp'}, dimensions={1}, use_global_device_ids=true | all-gather | bytes 626688 | tf_op jit(solution)/shard_map/all_gather | solution.py:182
  46.1 7.7 all-gather.11.cloned.1.call-done
  76.8 19.2 %all-gather = bf16[16,48,2]{1,2,0:T(2,128)(2,1)S(1)} all-gather(bf16[1,48,2]{1,2,0:T(2,128)(2,1)S(1)} %bitcast.713), channel_id=1, replica_groups=mesh['dp'=16,'tensor'=2] {'dp'}, dimensions={0}, use_global_device_ids=true | all-gather | bytes 3264 | tf_op jit(solution)/shard_map/all_gather | solution.py:185
  96.2 17.8 all-gather.1
  131.6 12.2 all_gather.116
  143.8 11.1 multiply_convert_fusion.7
  154.9 31.1 %all-gather.15.cloned.1.call-done = bf16[1536,768]{0,1:T(8,128)(2,1)} async-done(((bf16[1536,48]{0,1:T(8,128)(2,1)}), bf16[1536,768]{0,1:T(8,128)(2,1)}) %all-gather.15.cloned.1.call-update) | async-done | bytes 2359312 | tf_op jit(solution)/shard_map/all_gather | solution.py:184
  193.5 22.4 %all_gather.121 = bf16[768,384]{1,0:T(8,128)(2,1)} all-gather(bf16[48,384]{1,0:T(8,128)(2,1)S(1)} %copy-done.150), channel_id=1, replica_groups=mesh['dp'=16,'tensor'=2] {'dp'}, dimensions={0}, use_global_device_ids=true | all-gather | bytes 626688 | tf_op jit(solution)/shard_map/all_gather | solution.py:224
  215.9 21.2 %all_gather.122 = bf16[384,768]{0,1:T(8,128)(2,1)} all-gather(bf16[384,48]{0,1:T(8,128)(2,1)S(1)} %copy-done.151), channel_id=1, replica_groups=mesh['dp'=16,'tensor'=2] {'dp'}, dimensions={1}, use_global_device_ids=true | all-gather | bytes 626688 | tf_op jit(solution)/shard_map/all_gather | solution.py:226
  238.6 15.3 reduce-scatter.47.cloned.1.call-done
  256.1 26.2 %reduce-scatter.41.cloned.1.call-done = f32[1,256,768]{2,1,0:T(8,128)} async-done(((f32[1,512,768]{2,1,0:T(8,128)}), f32[1,256,768]{2,1,0:T(8,128)}) %reduce-scatter.41.cloned.1.call-update) | async-done | bytes 786448 | tf_op jit(solution)/shard_map/reduce_scatter | solution.py:163
  284.7 11.5 all_gather.128
  296.2 9.7 multiply_convert_fusion.5
  312.8 19.0 %all_gather.120 = bf16[1,512,768]{2,1,0:T(8,128)(2,1)S(1)} all-gather(bf16[1,256,768]{2,1,0:T(8,128)(2,1)S(1)} %fusion.187), channel_id=1, replica_groups=mesh['dp'=16,'tensor'=2] {'tensor'}, dimensions={1}, use_global_device_ids=true | all-gather | bytes 1179648 | tf_op jit(solution)/shard_map/all_gather | solution.py:169
  340.2 21.3 %all-gather.2 = bf16[16,48,2]{1,2,0:T(2,128)(2,1)S(1)} all-gather(bf16[1,48,2]{1,2,0:T(2,128)(2,1)} %bitcast.715), channel_id=1, replica_groups=mesh['dp'=16,'tensor'=2] {'dp'}, dimensions={0}, use_global_device_ids=true | all-gather | bytes 3264 | tf_op jit(solution)/shard_map/all_gather | solution.py:229
  363.5 17.4 all-gather.3
  399.2 12.1 all_gather.129
  421.5 11.8 all_gather.125
  433.3 11.1 multiply_convert_fusion.6
  444.4 14.2 all-gather.21.cloned.1.call-done
  463.4 22.3 %reduce-scatter.51.cloned.1.call-done = f32[1,256,768]{2,1,0:T(8,128)} async-done(((f32[1,512,768]{2,1,0:T(8,128)}), f32[1,256,768]{2,1,0:T(8,128)}) %reduce-scatter.51.cloned.1.call-update) | async-done | bytes 786448 | tf_op jit(solution)/shard_map/reduce_scatter | solution.py:163
  489.7 24.4 %reduce-scatter.45.cloned.1.call-done = f32[1,256,768]{2,1,0:T(8,128)} async-done(((f32[1,512,768]{2,1,0:T(8,128)}), f32[1,256,768]{2,1,0:T(8,128)}) %reduce-scatter.45.cloned.1.call-update) | async-done | bytes 786448 | tf_op jit(solution)/shard_map/reduce_scatter | solution.py:163
  517.6 11.5 all_gather.130
  529.1 9.7 multiply_convert_fusion.4
  546.4 22.5 %reduce-scatter.53.cloned.1.call-done = f32[1,256,768]{2,1,0:T(8,128)} async-done(((f32[1,512,768]{2,1,0:T(8,128)}), f32[1,256,768]{2,1,0:T(8,128)}) %reduce-scatter.53.cloned.1.call-update) | async-done | bytes 786448 | tf_op jit(solution)/shard_map/reduce_scatter | solution.py:163
  575.8 11.7 all_gather.131
  595.5 17.1 all_gather.135
  624.5 28.0 %reduce-scatter.63.cloned.1.call-done = f32[1,256,768]{2,1,0:T(8,128)} async-done(((f32[1,512,768]{2,1,0:T(8,128)}), f32[1,256,768]{2,1,0:T(8,128)}) %reduce-scatter.63.cloned.1.call-update) | async-done | bytes 786448 | tf_op jit(solution)/shard_map/reduce_scatter | solution.py:166
  658.6 11.5 all_gather.132
  677.4 17.0 all_gather.136
  702.0 17.5 reduce-scatter.65.cloned.1.call-done
  726.7 11.5 all_gather.137
  748.5 17.1 all_gather.133
  827.5 8.5 all_gather.134
  858.9 8.6 all_gather.138
  955.0 100.8 %all-reduce.5.cloned.1.call-done = f32[768,2,384]{2,1,0:T(2,128)} async-done(((f32[768,2,384]{2,1,0:T(2,128)}), f32[768,2,384]{2,1,0:T(2,128)}) %all-reduce.5.cloned.1.call-update) | async-done | bytes 2359312
  1062.9 57.9 %all-reduce.1 = (f32[6,2,31]{2,0,1:T(8,128)S(1)}, f32[6,2,31]{2,0,1:T(8,128)S(1)}) all-reduce(f32[6,2,31]{2,0,1:T(8,128)S(1)} %fusion.118, f32[6,2,31]{2,0,1:T(8,128)S(1)} %fusion.119), channel_id=1, replica_groups=mesh['dp'=16,'tensor'=2] {'dp'}, use_global_device_ids=true, to_apply=%region_86.87 | all-reduce | flops 744 | bytes 5952 | tf_op jit(solution)/shard_map/psum | solution.py:401
  1122.9 49.3 %reduce-scatter.93.cloned.1.call-done = f32[48,2]{1,0:T(8,128)} async-done(((f32[768,2]{1,0:T(8,128)}), f32[48,2]{1,0:T(8,128)}) %reduce-scatter.93.cloned.1.call-update) | async-done | bytes 400
  1178.5 21.1 %reduce-scatter.61.cloned.1.call-done = f32[1,256,768]{2,1,0:T(8,128)} async-done(((f32[1,512,768]{2,1,0:T(8,128)}), f32[1,256,768]{2,1,0:T(8,128)}) %reduce-scatter.61.cloned.1.call-update) | async-done | bytes 786448 | tf_op jit(solution)/shard_map/reduce_scatter | solution.py:166
  1201.1 26.9 %reduce-scatter.69.cloned.1.call-done = f32[1,256,768]{2,1,0:T(8,128)} async-done(((f32[1,512,768]{2,1,0:T(8,128)}), f32[1,256,768]{2,1,0:T(8,128)}) %reduce-scatter.69.cloned.1.call-update) | async-done | bytes 786448 | tf_op jit(solution)/shard_map/reduce_scatter | solution.py:166
  1230.5 59.6 %reduce-scatter.85.cloned.1.call-done = f32[384,48]{0,1:T(8,128)} async-done(((f32[384,768]{0,1:T(8,128)}), f32[384,48]{0,1:T(8,128)}) %reduce-scatter.85.cloned.1.call-update) | async-done | bytes 73744 | tf_op jit(solution)/shard_map/reduce_scatter | solution.py:395
  1290.2 61.3 %reduce-scatter.83.cloned.1.call-done = f32[48,384]{1,0:T(8,128)} async-done(((f32[768,384]{1,0:T(8,128)}), f32[48,384]{1,0:T(8,128)}) %reduce-scatter.83.cloned.1.call-update) | async-done | bytes 73744 | tf_op jit(solution)/shard_map/reduce_scatter | solution.py:393
  1351.5 79.0 %reduce-scatter.87.cloned.1.call-done = f32[48,1536]{1,0:T(8,128)} async-done(((f32[768,1536]{1,0:T(8,128)}), f32[48,1536]{1,0:T(8,128)}) %reduce-scatter.87.cloned.1.call-update) | async-done | bytes 294928 | tf_op jit(solution)/shard_map/reduce_scatter | solution.py:396
  1430.5 79.4 %reduce-scatter.89.cloned.1.call-done = f32[1536,48]{0,1:T(8,128)} async-done(((f32[1536,768]{0,1:T(8,128)}), f32[1536,48]{0,1:T(8,128)}) %reduce-scatter.89.cloned.1.call-update) | async-done | bytes 294928 | tf_op jit(solution)/shard_map/reduce_scatter | solution.py:397
  1509.9 61.3 %reduce-scatter.77.cloned.1.call-done = f32[384,48]{0,1:T(8,128)} async-done(((f32[384,768]{0,1:T(8,128)}), f32[384,48]{0,1:T(8,128)}) %reduce-scatter.77.cloned.1.call-update) | async-done | bytes 73744 | tf_op jit(solution)/shard_map/reduce_scatter | solution.py:386
  1571.2 79.0 %reduce-scatter.79.cloned.1.call-done = f32[48,1536]{1,0:T(8,128)} async-done(((f32[768,1536]{1,0:T(8,128)}), f32[48,1536]{1,0:T(8,128)}) %reduce-scatter.79.cloned.1.call-update) | async-done | bytes 294928 | tf_op jit(solution)/shard_map/reduce_scatter | solution.py:387
  1650.2 79.4 %reduce-scatter.81.cloned.1.call-done = f32[1536,48]{0,1:T(8,128)} async-done(((f32[1536,768]{0,1:T(8,128)}), f32[1536,48]{0,1:T(8,128)}) %reduce-scatter.81.cloned.1.call-update) | async-done | bytes 294928 | tf_op jit(solution)/shard_map/reduce_scatter | solution.py:388
  1729.6 71.4 %reduce-scatter.75.cloned.1.call-done = f32[48,3,384]{2,0,1:T(8,128)} async-done(((f32[768,3,384]{2,0,1:T(8,128)}), f32[48,3,384]{2,0,1:T(8,128)}) %reduce-scatter.75.cloned.1.call-update) | async-done | bytes 221200 | tf_op jit(solution)/shard_map/reduce_scatter | solution.py:385
  (796 shorter events, 385.2 us)
Async XLA Ops:
  7.2 46.6 %all-gather.11.cloned.1.call-start = ((), (), s32[]{:S(2)}) async-start(), calls=%async_computation.30 | async-start | bytes 1880064 | tf_op jit(solution)/shard_map/all_gather | solution.py:181
  7.9 121.8 %reduce-scatter.39.cloned.1.call-start = ((), (), s32[]{:S(2)}) async-start(), calls=%async_computation.31 | async-start | bytes 2359296 | tf_op jit(solution)/shard_map/reduce_scatter | solution.py:163
  9.5 181.3 %copy-start.119 = (s32[16,16]{1,0:T(8,128)}, s32[16,16]{1,0:T(8,128)S(1)}, u32[]{:S(2)}) copy-start(s32[16,16]{1,0:T(8,128)S(1)} %subtract_add_fusion) | copy-start | bytes 3076
  18.3 174.1 %copy-start.113 = (pred[2,2,512,16]{2,3,1,0:T(8,128)(4,1)}, pred[2,2,512,16]{2,3,1,0:T(8,128)(4,1)S(1)}, u32[]{:S(2)}) copy-start(pred[2,2,512,16]{2,3,1,0:T(8,128)(4,1)S(1)} %get-tuple-element.172) | copy-start | bytes 98308
  72.6 71.2 %all-gather.13.cloned.1.call-start = ((), (), s32[]{:S(2)}) async-start(), calls=%async_computation.32 | async-start | bytes 2506752 | tf_op jit(solution)/shard_map/all_gather | solution.py:183
  73.3 112.7 %all-gather.15.cloned.1.call-start = ((), (), s32[]{:S(2)}) async-start(), calls=%async_computation.33 | async-start | bytes 2506752 | tf_op jit(solution)/shard_map/all_gather | solution.py:184
  73.9 163.3 %all-gather.17.cloned.1.call-start = ((), (), s32[]{:S(2)}) async-start(), calls=%async_computation.35 | async-start | bytes 1253376 | tf_op jit(solution)/shard_map/all_gather | solution.py:225
  74.5 179.5 %reduce-scatter.47.cloned.1.call-start = ((), (), s32[]{:S(2)}) async-start(), calls=%async_computation.40 | async-start | bytes 2359296 | tf_op jit(solution)/shard_map/reduce_scatter | solution.py:163
  96.1 186.2 %copy-start.131 = (f32[768]{0:T(1024)}, f32[768]{0:T(1024)S(1)}, u32[]{:S(2)}) copy-start(f32[768]{0:T(1024)S(1)} %get-tuple-element.109) | copy-start | bytes 9220
  96.2 216.4 %copy-start.129 = (f32[768]{0:T(1024)}, f32[768]{0:T(1024)S(1)}, u32[]{:S(2)}) copy-start(f32[768]{0:T(1024)S(1)} %get-tuple-element.108) | copy-start | bytes 9220
  114.1 168.2 %copy-start.135 = (f32[768]{0:T(1024)}, f32[768]{0:T(1024)S(1)}, u32[]{:S(2)}) copy-start(f32[768]{0:T(1024)S(1)} %get-tuple-element.111) | copy-start | bytes 9220
  114.1 198.4 %copy-start.134 = (f32[768]{0:T(1024)}, f32[768]{0:T(1024)S(1)}, u32[]{:S(2)}) copy-start(f32[768]{0:T(1024)S(1)} %get-tuple-element.110) | copy-start | bytes 9220
  129.7 152.6 %reduce-scatter.41.cloned.1.call-start = ((), (), s32[]{:S(2)}) async-start(), calls=%async_computation.34 | async-start | bytes 2359296 | tf_op jit(solution)/shard_map/reduce_scatter | solution.py:163
  131.1 151.2 %copy-start.14 = (f32[1,256,768]{2,1,0:T(8,128)}, f32[1,256,768]{2,1,0:T(8,128)S(1)}, u32[]{:S(2)}) copy-start(f32[1,256,768]{2,1,0:T(8,128)S(1)} %get-tuple-element.151) | copy-start | bytes 2359300
  190.8 201.4 %reduce-scatter.49.cloned.1.call-start = ((), (), s32[]{:S(2)}) async-start(), calls=%async_computation.41 | async-start | bytes 2359296 | tf_op jit(solution)/shard_map/reduce_scatter | solution.py:163
  309.7 86.5 %reduce-scatter.43.cloned.1.call-start = ((), (), s32[]{:S(2)}) async-start(), calls=%async_computation.36 | async-start | bytes 2359296 | tf_op jit(solution)/shard_map/reduce_scatter | solution.py:163
  312.2 358.9 %copy-start.80 = (bf16[256,768]{0,1:T(8,128)(2,1)}, bf16[256,768]{0,1:T(8,128)(2,1)S(1)}, u32[]{:S(2)}) copy-start(bf16[256,768]{0,1:T(8,128)(2,1)S(1)} %copy.140) | copy-start | bytes 1179652
  338.9 94.5 %all-gather.19.cloned.1.call-start = ((), (), s32[]{:S(2)}) async-start(), calls=%async_computation.37 | async-start | bytes 2506752 | tf_op jit(solution)/shard_map/all_gather | solution.py:227
  339.5 119.2 %all-gather.21.cloned.1.call-start = ((), (), s32[]{:S(2)}) async-start(), calls=%async_computation.38 | async-start | bytes 2506752 | tf_op jit(solution)/shard_map/all_gather | solution.py:228
  340.2 145.5 %reduce-scatter.51.cloned.1.call-start = ((), (), s32[]{:S(2)}) async-start(), calls=%async_computation.42 | async-start | bytes 2359296 | tf_op jit(solution)/shard_map/reduce_scatter | solution.py:163
  418.9 95.1 %reduce-scatter.45.cloned.1.call-start = ((), (), s32[]{:S(2)}) async-start(), calls=%async_computation.39 | async-start | bytes 2359296 | tf_op jit(solution)/shard_map/reduce_scatter | solution.py:163
  463.3 105.5 %reduce-scatter.53.cloned.1.call-start = ((), (), s32[]{:S(2)}) async-start(), calls=%async_computation.43 | async-start | bytes 2359296 | tf_op jit(solution)/shard_map/reduce_scatter | solution.py:163
  542.6 81.9 %reduce-scatter.55.cloned.1.call-start = ((), (), s32[]{:S(2)}) async-start(), calls=%async_computation.44 | async-start | bytes 2359296 | tf_op jit(solution)/shard_map/reduce_scatter | solution.py:166
  593.5 59.0 %reduce-scatter.63.cloned.1.call-start = ((), (), s32[]{:S(2)}) async-start(), calls=%async_computation.48 | async-start | bytes 2359296 | tf_op jit(solution)/shard_map/reduce_scatter | solution.py:166
  622.4 79.6 %reduce-scatter.57.cloned.1.call-start = ((), (), s32[]{:S(2)}) async-start(), calls=%async_computation.45 | async-start | bytes 1179648 | tf_op jit(solution)/shard_map/reduce_scatter | solution.py:306
  675.9 43.6 %reduce-scatter.65.cloned.1.call-start = ((), (), s32[]{:S(2)}) async-start(), calls=%async_computation.49 | async-start | bytes 1179648 | tf_op jit(solution)/shard_map/reduce_scatter | solution.py:306
  701.9 117.1 %reduce-scatter.67.cloned.1.call-start = ((), (), s32[]{:S(2)}) async-start(), calls=%async_computation.50 | async-start | bytes 2359296 | tf_op jit(solution)/shard_map/reduce_scatter | solution.py:166
  746.5 72.6 %reduce-scatter.59.cloned.1.call-start = ((), (), s32[]{:S(2)}) async-start(), calls=%async_computation.46 | async-start | bytes 2359296 | tf_op jit(solution)/shard_map/reduce_scatter | solution.py:166
  775.4 173.2 %reduce-scatter.95.cloned.1.call-start = ((), (), s32[]{:S(2)}) async-start(), calls=%async_computation.64 | async-start | bytes 417792
  791.9 157.4 %reduce-scatter.97.cloned.1.call-start = ((), (), s32[]{:S(2)}) async-start(), calls=%async_computation.65 | async-start | bytes 417792
  795.1 155.1 %reduce-scatter.71.cloned.1.call-start = ((), (), s32[]{:S(2)}) async-start(), calls=%async_computation.52 | async-start | bytes 589824 | tf_op jit(solution)/shard_map/reduce_scatter | solution.py:314
  799.6 153.4 %reduce-scatter.73.cloned.1.call-start = ((), (), s32[]{:S(2)}) async-start(), calls=%async_computation.53 | async-start | bytes 589824 | tf_op jit(solution)/shard_map/reduce_scatter | solution.py:314
  805.4 250.4 %all-reduce.5.cloned.1.call-start = ((), (), s32[]{:S(2)}) async-start(), calls=%async_computation.66 | async-start | bytes 4718592
  813.9 308.1 %reduce-scatter.91.cloned.1.call-start = ((), (), s32[]{:S(2)}) async-start(), calls=%async_computation.62 | async-start | bytes 417792
  854.5 317.6 %reduce-scatter.93.cloned.1.call-start = ((), (), s32[]{:S(2)}) async-start(), calls=%async_computation.63 | async-start | bytes 417792
  856.3 343.3 %reduce-scatter.61.cloned.1.call-start = ((), (), s32[]{:S(2)}) async-start(), calls=%async_computation.47 | async-start | bytes 2359296 | tf_op jit(solution)/shard_map/reduce_scatter | solution.py:166
  857.6 370.4 %reduce-scatter.69.cloned.1.call-start = ((), (), s32[]{:S(2)}) async-start(), calls=%async_computation.51 | async-start | bytes 2359296 | tf_op jit(solution)/shard_map/reduce_scatter | solution.py:166
  885.0 405.1 %reduce-scatter.85.cloned.1.call-start = ((), (), s32[]{:S(2)}) async-start(), calls=%async_computation.59 | async-start | bytes 1253376 | tf_op jit(solution)/shard_map/reduce_scatter | solution.py:395
  889.9 461.6 %reduce-scatter.83.cloned.1.call-start = ((), (), s32[]{:S(2)}) async-start(), calls=%async_computation.58 | async-start | bytes 1253376 | tf_op jit(solution)/shard_map/reduce_scatter | solution.py:393
  894.6 535.9 %reduce-scatter.87.cloned.1.call-start = ((), (), s32[]{:S(2)}) async-start(), calls=%async_computation.60 | async-start | bytes 5013504 | tf_op jit(solution)/shard_map/reduce_scatter | solution.py:396
  901.7 608.2 %reduce-scatter.89.cloned.1.call-start = ((), (), s32[]{:S(2)}) async-start(), calls=%async_computation.61 | async-start | bytes 5013504 | tf_op jit(solution)/shard_map/reduce_scatter | solution.py:397
  909.0 662.2 %reduce-scatter.77.cloned.1.call-start = ((), (), s32[]{:S(2)}) async-start(), calls=%async_computation.55 | async-start | bytes 1253376 | tf_op jit(solution)/shard_map/reduce_scatter | solution.py:386
  914.6 735.6 %reduce-scatter.79.cloned.1.call-start = ((), (), s32[]{:S(2)}) async-start(), calls=%async_computation.56 | async-start | bytes 5013504 | tf_op jit(solution)/shard_map/reduce_scatter | solution.py:387
  921.7 807.9 %reduce-scatter.81.cloned.1.call-start = ((), (), s32[]{:S(2)}) async-start(), calls=%async_computation.57 | async-start | bytes 5013504 | tf_op jit(solution)/shard_map/reduce_scatter | solution.py:388
  928.7 872.3 %reduce-scatter.75.cloned.1.call-start = ((), (), s32[]{:S(2)}) async-start(), calls=%async_computation.54 | async-start | bytes 3760128 | tf_op jit(solution)/shard_map/reduce_scatter | solution.py:385
  1059.9 139.6 %copy-start.195 = (f32[256]{0:T(256)S(1)}, f32[256]{0:T(256)}, u32[]{:S(2)}) copy-start(f32[256]{0:T(256)} %copy-done.194) | copy-start | bytes 3076
  1061.1 166.9 %copy-start.196 = (f32[256]{0:T(256)S(1)}, f32[256]{0:T(256)}, u32[]{:S(2)}) copy-start(f32[256]{0:T(256)} %negate_multiply_fusion.4) | copy-start | bytes 3076
  1061.8 166.3 %copy-start.37 = (f32[1,256,768]{2,1,0:T(8,128)S(1)}, f32[1,256,768]{2,1,0:T(8,128)}, u32[]{:S(2)}) copy-start(f32[1,256,768]{2,1,0:T(8,128)} %get-tuple-element.177) | copy-start | bytes 2359300
  (216 other events, 1853.3 us)
Sparse Core Ops, SparseCore 0:
  10.3 43.3 all-gather.10
  72.7 24.9 reduce-scatter.38
  100.3 42.2 all-gather.12
  144.9 41.0 all-gather.14
  188.4 38.2 all-gather.16
  228.9 25.0 reduce-scatter.46
  256.2 26.0 reduce-scatter.40
  309.8 32.0 reduce-scatter.48
  344.2 26.0 reduce-scatter.42
  372.6 42.2 all-gather.18
  417.5 41.0 all-gather.20
  460.8 24.8 reduce-scatter.50
  487.9 26.0 reduce-scatter.44
  542.7 26.0 reduce-scatter.52
  593.6 30.5 reduce-scatter.54
  626.4 26.0 reduce-scatter.62
  676.1 21.6 reduce-scatter.56
  702.0 17.4 reduce-scatter.64
  746.6 30.6 reduce-scatter.66
  779.4 26.1 reduce-scatter.58
  809.1 55.5 reduce-scatter.94
  868.6 54.5 reduce-scatter.96
  925.4 12.1 reduce-scatter.70
  939.9 13.1 reduce-scatter.72
  956.6 99.1 all-reduce.4
  1059.1 54.6 reduce-scatter.90
  1117.6 54.5 reduce-scatter.92
  1174.4 25.0 reduce-scatter.60
  1201.9 26.0 reduce-scatter.68
  1232.1 58.0 reduce-scatter.84
  1294.4 57.1 reduce-scatter.82
  1355.9 74.5 reduce-scatter.86
  1435.3 74.5 reduce-scatter.88
  1514.1 57.1 reduce-scatter.76
  1575.6 74.5 reduce-scatter.78
  1655.0 74.5 reduce-scatter.80
  1733.9 67.1 reduce-scatter.74
where the time goes:
time: 1820 us; the launch traced here: 1810 us
  waiting for transfers between devices  985 us (54%)
  blocking collectives  391 us (21%)
  matrix products  233 us (13%)
  local copies, waits for them, and re-layouts  92.9 us (5%)
  other arithmetic  85.8 us (5%)
  between operations  18.6 us (1%)
    unnamed x42, waiting for transfers between devices  154 us
    reduce_scatter x8, waiting for transfers between devices, branch_share(): lax.psum_scatter(partial_rows, 'tensor', scatter_dimension=1, tiled=True)  111 us
    all_gather x8, blocking collectives, grad_gather(): return lax.all_gather(share_rows, 'tensor', axis=1, tiled=True)  103 us
    reduce_scatter x1, waiting for transfers between devices, shards(): lax.psum_scatter(grads_first[3], 'dp', scatter_dimension=1, tiled=True)  79.4 us
    reduce_scatter x1, waiting for transfers between devices, shards(): lax.psum_scatter(grads_second[4], 'dp', scatter_dimension=1, tiled=True)  79.4 us
    reduce_scatter x1, waiting for transfers between devices, shards(): lax.psum_scatter(grads_first[2], 'dp', scatter_dimension=0, tiled=True)  79 us
    reduce_scatter x1, waiting for transfers between devices, shards(): lax.psum_scatter(grads_second[3], 'dp', scatter_dimension=0, tiled=True)  79 us
    all_gather x6, blocking collectives, row_gather(): return lax.all_gather(share_rows, 'tensor', axis=1, tiled=True)  78.2 us
  transfers between devices with their start and end apart: 37, of which 23 were waited for; matrix products, arithmetic and copies ran while one was open for 17% of the time, Pallas kernels for 0%

commit v1 on v0

v1 whole, which is shorter than its diff:
```python
import jax
import jax.numpy as jnp
from jax import lax
from jax.sharding import PartitionSpec as P

HD = 64
GRID = 16
RELS = 2 * GRID - 1
LANES = 128

highest = lax.Precision.HIGHEST
epsilon = 1e-06
masked_score = -30000.0
bf16 = jnp.bfloat16
f32 = jnp.float32


def cast_low(values):
    return values.astype(bf16)


def matmul(left_side, right_side):
    return jnp.dot(left_side, right_side, preferred_element_type=f32)


def matmul_tn(left_side, right_side):
    return lax.dot_general(
        left_side, right_side, (((0,), (0,)), ((), ())), preferred_element_type=f32
    )


def matmul_nt(left_side, right_side):
    return lax.dot_general(
        left_side, right_side, (((1,), (1,)), ((), ())), preferred_element_type=f32
    )


def norm_forward(values, gain, shift):
    center = values - jnp.mean(values, axis=-1, keepdims=True)
    scale = lax.rsqrt(jnp.mean(center * center, axis=-1, keepdims=True) + epsilon)
    normed = center * scale
    return normed * gain + shift, normed, scale


def norm_backward(grad, normed, scale, gain):
    scaled = grad * gain
    inner = scaled - jnp.mean(scaled, axis=-1, keepdims=True)
    inner = inner - normed * jnp.mean(scaled * normed, axis=-1, keepdims=True)
    return inner * scale, jnp.sum(grad * normed, axis=0), jnp.sum(grad, axis=0)


def gelu_pair(hidden):
    cdf = 0.5 * lax.erfc(-hidden * (0.5**0.5))
    slope = cdf + hidden * jnp.exp(-0.5 * hidden * hidden) * (0.3989422804014327)
    return cast_low(hidden * cdf), cast_low(slope)


def grid_hot(coords):
    hot = coords[:, :, None] == jnp.arange(GRID, dtype=jnp.int32)
    return hot.reshape(coords.shape[0], 2 * GRID)


def pair_tables(tables):
    offset = jnp.arange(GRID)[:, None] - jnp.arange(GRID)[None, :] + GRID - 1
    hot = (offset[:, :, None] == jnp.arange(RELS)).astype(f32)
    pairs = jnp.einsum("hcr,abr->cahb", tables.astype(f32), hot, precision=highest)
    same = jnp.eye(2, dtype=f32)
    spread = pairs[:, :, :, None, :] * same[:, None, None, :, None]
    return cast_low(spread.reshape(2 * GRID, -1))


def table_grad(own_hot, right_part):
    heads = right_part.shape[0]
    pairs = jnp.einsum(
        "na,hnb->hab", own_hot.astype(f32), right_part, precision=highest
    ).reshape(heads, 2, GRID, 2, GRID)
    pairs = jnp.stack([pairs[:, 0, :, 0], pairs[:, 1, :, 1]], axis=1)
    offset = jnp.arange(GRID)[:, None] - jnp.arange(GRID)[None, :] + GRID - 1
    hot = (offset[:, :, None] == jnp.arange(RELS)).astype(f32)
    return jnp.einsum("hcab,abr->hcr", pairs, hot, precision=highest)


def split_heads(rows):
    return jnp.transpose(rows.reshape(rows.shape[0], -1, HD), (1, 0, 2))


def merge_heads(heads):
    return jnp.transpose(heads, (1, 0, 2)).reshape(heads.shape[1], -1)


def scores_of(queries, keys, own_part, other_hot, keep):
    scores = jnp.einsum("hqd,hkd->hqk", queries, keys, preferred_element_type=f32) * HD**-0.5
    scores = scores + jnp.einsum("hqb,kb->hqk", own_part, other_hot, preferred_element_type=f32)
    return jnp.where(keep[None, None, :] > 0, scores, masked_score)


def attend_forward(queries, keys, values, own_part, other_hot, keep):
    scores = scores_of(split_heads(queries), split_heads(keys), own_part, other_hot, keep)
    top = jnp.max(scores, axis=-1, keepdims=True)
    weights = jnp.exp(scores - top)
    total = jnp.sum(weights, axis=-1, keepdims=True)
    probs = cast_low(weights / total)
    context = jnp.einsum("hqk,hkd->hqd", probs, split_heads(values), preferred_element_type=f32)
    return merge_heads(cast_low(context)), top + jnp.log(total)


def attend_backward(queries, keys, values, own_part, other_hot, keep, log_total, context_grad):
    queries, keys, values = split_heads(queries), split_heads(keys), split_heads(values)
    context_grad = split_heads(context_grad)
    scores = scores_of(queries, keys, own_part, other_hot, keep)
    probs = jnp.exp(scores - log_total)
    prob_grad = jnp.einsum("hqd,hkd->hqk", context_grad, values, preferred_element_type=f32)
    row_dot = jnp.sum(probs * prob_grad, axis=-1, keepdims=True)
    score_grad = cast_low(probs * (prob_grad - row_dot) * (keep[None, None, :] > 0))
    query_grad = jnp.einsum("hqk,hkd->hqd", score_grad, keys, preferred_element_type=f32)
    key_grad = jnp.einsum("hqk,hqd->hkd", score_grad, queries, preferred_element_type=f32)
    value_grad = jnp.einsum(
        "hqk,hqd->hkd", cast_low(probs), context_grad, preferred_element_type=f32
    )
    right_part = jnp.einsum("hqk,kb->hqb", score_grad, other_hot, preferred_element_type=f32)
    return (
        merge_heads(cast_low(query_grad * HD**-0.5)),
        merge_heads(cast_low(key_grad * HD**-0.5)),
        merge_heads(cast_low(value_grad)),
        right_part,
    )


def shards(
    text_rows,
    vision_rows,
    segment_ids,
    text_keep,
    segment_box,
    patch_keep,
    attn_qkv_a,
    attn_out_a,
    mlp_in_a,
    mlp_out_a,
    norm_gain_a,
    norm_shift_a,
    box_table_a,
    attn_query_b,
    attn_kv_b,
    attn_out_b,
    mlp_in_b,
    mlp_out_b,
    norm_gain_b,
    norm_shift_b,
    box_table_b,
    out_grad,
):
    pages, length, width = text_rows.shape
    patches = vision_rows.shape[1]
    ndp, nt = lax.axis_size("dp"), lax.axis_size("tensor")
    own, mine = lax.axis_index("dp"), lax.axis_index("tensor")
    block = width // ndp
    share = attn_out_a.shape[0]
    hidden = mlp_in_a.shape[1]
    nz = ndp // 4
    copies = nt // pages

    def swap(values, dp_mask, tensor_mask):
        pairs = [
            (d * nt + t, (d ^ dp_mask) * nt + (t ^ tensor_mask))
            for d in range(ndp)
            for t in range(nt)
        ]
        return lax.ppermute(values, ("dp", "tensor"), pairs)

    def in_order(relative):
        return [
            lax.select_n(mine, *[relative[a ^ m] for m in range(nt)])
            for a in range(nt)
        ]

    def gather_rows(piece):
        slab = jnp.concatenate([piece] + [swap(piece, 4 * k, 0) for k in range(1, nz)], axis=0)
        if nt == 2:
            half = slab.shape[0] // 2
            along_x, along_y = swap(slab, 2, 0), swap(slab, 0, 1)
            far = jnp.concatenate(
                [swap(along_y[:half], 2, 0), swap(along_x[half:], 0, 1)], axis=0
            )
            plane = [[slab, along_x], [along_y, far]]
        else:
            pair = [slab, swap(slab, 2, 0)]
            plane = [pair] + [[swap(p, 0, j) for p in pair] for j in range(1, nt)]
        whole = []
        for pair in plane:
            rows = jnp.concatenate(pair, axis=0)
            whole.append(jnp.concatenate([rows, swap(rows, 1, 0)], axis=0))
        return whole

    def columns(whole, start, size):
        return jnp.concatenate([rows[:, start : start + size] for rows in whole], axis=1)

    def scatter_rows(products, groups):
        high = width // 2
        sums = []
        for left_side, right_side in products:
            away = cast_low(matmul_tn(left_side[:, high:], right_side) * (1.0 / copies))
            sums.append(
                cast_low(
                    matmul_tn(left_side[:, :high], right_side) * (1.0 / copies)
                    + swap(away, 1, 0).astype(f32)
                )
            )
        rows = high // 2

        def part(x, j):
            out = []
            for total, count in zip(sums, groups):
                size = total.shape[1] // count
                own_size = size // nt
                for g in range(count):
                    start = g * size + j * own_size
                    out.append(total[x * rows : (x + 1) * rows, start : start + own_size])
            return jnp.concatenate(out, axis=1) if len(out) > 1 else out[0]

        if nt == 2:
            half = rows // 2
            far, near_x, near_y, here = part(1, 1), part(1, 0), part(0, 1), part(0, 0)
            from_x, from_y = swap(far[:half], 2, 0), swap(far[half:], 0, 1)
            near_y = jnp.concatenate([near_y[:half] + from_x, near_y[half:]], axis=0)
            near_x = jnp.concatenate([near_x[:half], near_x[half:] + from_y], axis=0)
            here = here.astype(f32) + swap(near_x, 2, 0) + swap(near_y, 0, 1)
        else:
            here = [part(0, j) + swap(part(1, j), 2, 0) for j in range(nt)]
            here = here[0].astype(f32) + sum(swap(here[j], 0, j).astype(f32) for j in range(1, nt))
        here = cast_low(here)
        out = here[:block].astype(f32)
        for k in range(1, nz):
            out = out + swap(here[k * block : (k + 1) * block], 4 * k, 0).astype(f32)
        return out

    def sum_all(values):
        total = values[0]
        for j in range(1, nt):
            total = total + swap(values[j], 0, j)
        for mask in (1, 2):
            total = total + swap(total, mask, 0)
        return sum([swap(total, 4 * k, 0) for k in range(1, nz)], total)

    def to_owners(rows):
        cut = rows.shape[0] // nt
        parts = [rows[a * cut : (a + 1) * cut] for a in range(nt)]
        relative = in_order(parts)
        arrived = [relative[0]] + [swap(relative[k], 0, k) for k in range(1, nt)]
        return jnp.stack(in_order(arrived)[::copies])

    def from_owners(shares):
        relative = in_order([shares[a // copies] for a in range(nt)])
        arrived = [relative[0]] + [swap(relative[k], 0, k) for k in range(1, nt)]
        return jnp.concatenate(in_order(arrived), axis=0)

    norms = jnp.concatenate([norm_gain_a, norm_shift_a, norm_gain_b, norm_shift_b], axis=0)
    norm_columns = jnp.pad(norms.T, ((0, 0), (0, LANES - norms.shape[0])))
    first = gather_rows(
        jnp.concatenate([attn_qkv_a.reshape(block, 3 * share), attn_out_a.T, norm_columns], axis=1)
    )
    in_a = gather_rows(mlp_in_a)
    back_a = gather_rows(mlp_out_a.T)
    second = gather_rows(
        jnp.concatenate([attn_query_b, attn_kv_b.reshape(block, 2 * share), attn_out_b.T], axis=1)
    )
    in_b = gather_rows(mlp_in_b)
    back_b = gather_rows(mlp_out_b.T)
    qkv_a = jnp.concatenate([columns(first, i * share, share) for i in range(3)], axis=1)
    out_a = columns(first, 3 * share, share)
    norms = first[0][:, 4 * share : 4 * share + 8].T.astype(f32)
    gains, shifts = [norms[0], norms[1], norms[4], norms[5]], [norms[2], norms[3], norms[6], norms[7]]
    query_b = columns(second, 0, share)
    kv_b = jnp.concatenate([columns(second, share, share), columns(second, 2 * share, share)], axis=1)
    out_b = columns(second, 3 * share, share)
    in_a, back_a = columns(in_a, 0, hidden), columns(back_a, 0, hidden)
    in_b, back_b = columns(in_b, 0, hidden), columns(back_b, 0, hidden)

    place = jnp.arange(width)
    relative = place // (2 * nz * block) + 2 * (place // (nz * block) % 2) + 4 * (place // block % nz)
    feature = (own ^ relative) * block + place % block
    order = cast_low(jnp.arange(width)[:, None] == feature[None, :])
    page = mine // copies

    def of_page(values):
        return lax.dynamic_index_in_dim(values, page, 0, keepdims=False)

    text = cast_low(matmul(of_page(text_rows), order))
    vision = cast_low(matmul(of_page(vision_rows), order))
    grad_in = matmul(from_owners(out_grad), order)
    keep_text, keep_patch = of_page(text_keep), of_page(patch_keep)
    segment_hot = (of_page(segment_ids)[:, None] == jnp.arange(segment_box.shape[1])).astype(f32)
    token_box = matmul(segment_hot, of_page(segment_box).astype(f32)).astype(jnp.int32)
    text_hot = cast_low(grid_hot(token_box))
    patch = jnp.arange(patches, dtype=jnp.int32)
    patch_hot = cast_low(grid_hot(jnp.stack([patch % GRID, patch // GRID], axis=1)))
    tables = jnp.stack([box_table_a, box_table_b])
    tables = [tables] + [swap(tables, 0, j) for j in range(1, nt)]
    tables = jnp.concatenate(tables, axis=1)
    heads = tables.shape[1]

    def own_parts(table):
        parts = cast_low(matmul(text_hot, pair_tables(table)))
        return jnp.transpose(parts.reshape(length, heads, 2 * GRID), (1, 0, 2))

    own_a, own_b = own_parts(tables[0]), own_parts(tables[1])

    qkv = cast_low(matmul(text, qkv_a))
    queries_a, keys_a, values_a = (qkv[:, i * width : (i + 1) * width] for i in range(3))
    context_a, lse_a = attend_forward(queries_a, keys_a, values_a, own_a, text_hot, keep_text)
    mixed_a, normed_a0, scale_a0 = norm_forward(
        text.astype(f32) + matmul_nt(context_a, out_a), gains[0], shifts[0]
    )
    mixed_low_a = cast_low(mixed_a)
    gelu_a, slope_a = gelu_pair(matmul(mixed_low_a, in_a))
    middle, normed_a1, scale_a1 = norm_forward(
        mixed_a + matmul_nt(gelu_a, back_a), gains[1], shifts[1]
    )
    middle_low = cast_low(middle)

    queries_b = cast_low(matmul(middle_low, query_b))
    kv = cast_low(matmul(vision, kv_b))
    keys_b, values_b = kv[:, :width], kv[:, width:]
    context_b, lse_b = attend_forward(queries_b, keys_b, values_b, own_b, patch_hot, keep_patch)
    mixed_b, normed_b0, scale_b0 = norm_forward(
        middle + matmul_nt(context_b, out_b), gains[2], shifts[2]
    )
    mixed_low_b = cast_low(mixed_b)
    gelu_b, slope_b = gelu_pair(matmul(mixed_low_b, in_b))
    final, normed_b1, scale_b1 = norm_forward(
        mixed_b + matmul_nt(gelu_b, back_b), gains[3], shifts[3]
    )
    layer_out = to_owners(cast_low(matmul_nt(cast_low(final), order)))

    pre_b, gain_b1, shift_b1 = norm_backward(grad_in, normed_b1, scale_b1, gains[3])
    branch_b = cast_low(pre_b)
    hidden_b = cast_low(matmul(branch_b, back_b) * slope_b.astype(f32))
    grad_mlp_b = scatter_rows([(branch_b, gelu_b)], [1])
    grad_in_b = scatter_rows([(mixed_low_b, hidden_b)], [1])
    mixed_grad_b = pre_b + matmul_nt(hidden_b, in_b)
    attn_pre_b, gain_b0, shift_b0 = norm_backward(mixed_grad_b, normed_b0, scale_b0, gains[2])
    attn_grad_b = cast_low(attn_pre_b)
    context_grad_b = cast_low(matmul(attn_grad_b, out_b))
    query_grad_b, key_grad_b, value_grad_b, right_b = attend_backward(
        queries_b, keys_b, values_b, own_b, patch_hot, keep_patch, lse_b, context_grad_b
    )
    kv_grad_b = jnp.concatenate([key_grad_b, value_grad_b], axis=1)
    grad_second = scatter_rows(
        [(middle_low, query_grad_b), (vision, kv_grad_b), (attn_grad_b, context_b)], [1, 2, 1]
    )
    middle_grad = attn_pre_b + matmul_nt(query_grad_b, query_b)
    vision_grad = matmul_nt(cast_low(matmul_nt(kv_grad_b, kv_b)), order)
    vision_grad = to_owners(cast_low(vision_grad)).astype(f32)

    pre_a, gain_a1, shift_a1 = norm_backward(middle_grad, normed_a1, scale_a1, gains[1])
    branch_a = cast_low(pre_a)
    hidden_a = cast_low(matmul(branch_a, back_a) * slope_a.astype(f32))
    grad_mlp_a = scatter_rows([(branch_a, gelu_a)], [1])
    grad_in_a = scatter_rows([(mixed_low_a, hidden_a)], [1])
    mixed_grad_a = pre_a + matmul_nt(hidden_a, in_a)
    attn_pre_a, gain_a0, shift_a0 = norm_backward(mixed_grad_a, normed_a0, scale_a0, gains[0])
    attn_grad_a = cast_low(attn_pre_a)
    context_grad_a = cast_low(matmul(attn_grad_a, out_a))
    query_grad_a, key_grad_a, value_grad_a, right_a = attend_backward(
        queries_a, keys_a, values_a, own_a, text_hot, keep_text, lse_a, context_grad_a
    )
    qkv_grad = jnp.concatenate([query_grad_a, key_grad_a, value_grad_a], axis=1)
    grad_first = scatter_rows([(text, qkv_grad), (attn_grad_a, context_a)], [3, 1])
    text_grad = cast_low(attn_pre_a + matmul_nt(qkv_grad, qkv_a))
    text_grad = to_owners(cast_low(matmul_nt(text_grad, order))).astype(f32)

    norm_grads = jnp.stack(
        [gain_a0, gain_a1, shift_a0, shift_a1, gain_b0, gain_b1, shift_b0, shift_b1]
    )
    norm_grads = jnp.transpose(norm_grads.reshape(8, 2, 2, nz, block), (1, 2, 3, 0, 4)) * (1.0 / copies)
    norm_sum = norm_grads[0] + swap(norm_grads[1], 1, 0)
    norm_sum = norm_sum[0] + swap(norm_sum[1], 2, 0)
    norm_sum = sum([swap(norm_sum[k], 4 * k, 0) for k in range(1, nz)], norm_sum[0])
    norm_sum = sum([swap(norm_sum, 0, j) for j in range(1, nt)], norm_sum)

    tables_grad = jnp.stack([table_grad(text_hot, right_a), table_grad(text_hot, right_b)])
    tables_grad = jnp.transpose(
        tables_grad.reshape(2, nt, heads // nt, 2, RELS) * (1.0 / copies), (1, 0, 2, 3, 4)
    )
    tables_grad = sum_all(tables_grad)

    return (
        layer_out,
        text_grad,
        vision_grad,
        grad_first[:, : 3 * share].reshape(block, 3, share),
        grad_first[:, 3 * share :].T,
        grad_in_a,
        grad_mlp_a.T,
        norm_sum[0:2],
        norm_sum[2:4],
        tables_grad[0],
        grad_second[:, :share],
        grad_second[:, share : 3 * share].reshape(block, 2, share),
        grad_second[:, 3 * share :].T,
        grad_in_b,
        grad_mlp_b.T,
        norm_sum[4:6],
        norm_sum[6:8],
        tables_grad[1],
    )


def solution(mesh):
    return jax.shard_map(
        shards,
        mesh=mesh,
        in_specs=(
            P("dp", None, None),
            P("dp", None, None),
            P("dp", None),
            P("dp", None),
            P("dp", None, None),
            P("dp", None),
            P("dp", None, "tensor"),
            P("tensor", "dp"),
            P("dp", "tensor"),
            P("tensor", "dp"),
            P(None, "dp"),
            P(None, "dp"),
            P("tensor", None, None),
            P("dp", "tensor"),
            P("dp", None, "tensor"),
            P("tensor", "dp"),
            P("dp", "tensor"),
            P("tensor", "dp"),
            P(None, "dp"),
            P(None, "dp"),
            P("tensor", None, None),
            P("dp", "tensor", None),
        ),
        out_specs=(
            P("dp", "tensor", None),
            P("dp", "tensor", None),
            P("dp", "tensor", None),
            P("dp", None, "tensor"),
            P("tensor", "dp"),
            P("dp", "tensor"),
            P("tensor", "dp"),
            P(None, "dp"),
            P(None, "dp"),
            P("tensor", None, None),
            P("dp", "tensor"),
            P("dp", None, "tensor"),
            P("tensor", "dp"),
            P("dp", "tensor"),
            P("tensor", "dp"),
            P(None, "dp"),
            P(None, "dp"),
            P("tensor", None, None),
        ),
        check_vma=False,
    )
```

time: 1820 us -> 803 us (0.44)
  waiting for transfers between devices: 985 us -> 206 us
  blocking collectives: 391 us -> 0 us
  starting transfers between devices: 2.39 us -> 150 us
  matrix products: 233 us -> 309 us
  other arithmetic: 85.8 us -> 36.4 us
    reduce_scatter x26 -> x0, waiting for transfers between devices: 778 us -> none  [the longest x8 111 us: branch_share(): lax.psum_scatter(partial_rows, 'tensor', scatter_dimension=1, tiled=True)]
    all_gather x21 -> x0, blocking collectives: 327 us -> none  [the longest x8 103 us: grad_gather(): return lax.all_gather(share_rows, 'tensor', axis=1, tiled=True)]
    ppermute x0 -> x122, waiting for transfers between devices: none -> 206 us  [swap(): return lax.ppermute(values, ('dp', 'tensor'), pairs)]
    unnamed x42 -> x0, waiting for transfers between devices: 154 us -> none
    ppermute x0 -> x122, starting transfers between devices: none -> 150 us  [swap(): return lax.ppermute(values, ('dp', 'tensor'), pairs)]
    dot_general x64 -> x37, matrix products: 138 us -> 227 us  [the longest x15 80.7 us: matmul(): return jnp.dot(left_side, right_side, preferred_element_type=f32)]
    psum x2 -> x0, blocking collectives: 63.4 us -> none  [the longest x1 57.9 us: shards(): table_first, table_second = lax.psum((table_grads[0], table_grads[1]), 'dp')]
    all_gather x6 -> x0, waiting for transfers between devices: 53 us -> none  [the longest x1 31.1 us: shards(): lax.all_gather(mlp_out_a, 'dp', axis=1, tiled=True)]
  transfers between devices with their start and end apart: 37 -> 122, of which waited for: 23 -> 51; matrix products, arithmetic and copies ran while one was open for 17% -> 27% of each run, Pallas kernels for 0% -> 0%
where the time goes in v1:
time: 803 us; the launch traced here: 792 us
  matrix products  309 us (38%)
  waiting for transfers between devices  206 us (26%)
  starting transfers between devices  150 us (19%)
  local copies, waits for them, and re-layouts  87.5 us (11%)
  other arithmetic  36.4 us (5%)
    ppermute x122, waiting for transfers between devices, swap(): return lax.ppermute(values, ('dp', 'tensor'), pairs)  206 us
    ppermute x122, starting transfers between devices, swap(): return lax.ppermute(values, ('dp', 'tensor'), pairs)  150 us
    dot_general x15, matrix products, matmul(): return jnp.dot(left_side, right_side, preferred_element_type=f32)  80.7 us
    unnamed x435, local copies, waits for them, and re-layouts  43.5 us
    dot_general x18, matrix products, matmul_tn(): lax.dot_general(left_side, right_side, (((0,), (0,)), ((), ())), preferre...  41.2 us
    dot_general x10, matrix products, matmul_nt(): lax.dot_general(left_side, right_side, (((1,), (1,)), ((), ())), preferre...  40.5 us
    dot_general x2, matrix products, attend_backward(): jnp.einsum('hqk,kb->hqb', score_grad, other_hot, preferred_element_type=f32)  31.8 us
    dot_general x2, matrix products, attend_backward(): jnp.einsum('hqk,hqd->hkd', score_grad, queries, preferred_element_type=f32)  31.3 us
  transfers between devices with their start and end apart: 122, of which 51 were waited for; matrix products, arithmetic and copies ran while one was open for 27% of the time, Pallas kernels for 0%

profile of v1, /device:TPU:0, one launch (start us, length us, event | category | flops | bytes accessed | tf_op | source)
XLA Modules:
  0.0 792.5 jit_solution(17293776644508556222)
XLA Ops:
  0.7 5.1 collective-permute-start.21
  42.6 4.0 collective-permute-done.46
  52.0 9.0 %collective-permute-start.12 = (bf16[48,1536]{1,0:T(8,128)(2,1)}, bf16[48,1536]{1,0:T(8,128)(2,1)S(1)}, u32[]{:S(2)}, u32[]{:S(2)}) collective-permute-start(bf16[48,1536]{1,0:T(8,128)(2,1)} %param.30), channel_id=1, source_target_pairs={{0,24},{1,25},{2,26},{3,27},{4,28},{5,29},{6,30},{7,31},{8,16},{9,... | collective-permute-start | bytes 442376 | tf_op jit(solution)/shard_map/ppermute | solution.py:169
  64.2 8.6 %collective-permute-start.39 = (bf16[48,1536]{1,0:T(8,128)(2,1)S(1)}, bf16[48,1536]{1,0:T(8,128)(2,1)S(1)}, u32[]{:S(2)}, u32[]{:S(2)}) collective-permute-start(bf16[48,1536]{1,0:T(8,128)(2,1)S(1)} %copy-done.117), channel_id=1, source_target_pairs={{0,24},{1,25},{2,26},{3,27},{4,28},{5,29},{6,30},{7,31},{8,16},{9,... | collective-permute-start | bytes 442376 | tf_op jit(solution)/shard_map/ppermute | solution.py:169
  96.8 5.3 collective-permute-done.22
  103.7 11.0 %collective-permute-done.49 = bf16[192,1536]{1,0:T(8,128)(2,1)S(1)} collective-permute-done((bf16[192,1536]{1,0:T(8,128)(2,1)S(1)}, bf16[192,1536]{1,0:T(8,128)(2,1)S(1)}, u32[]{:S(2)}, u32[]{:S(2)}) %collective-permute-start.49) | collective-permute-done | bytes 589856 | tf_op jit(solution)/shard_map/ppermute | solution.py:169
  117.4 10.0 %collective-permute-done.31 = bf16[192,1536]{1,0:T(8,128)(2,1)S(1)} collective-permute-done((bf16[192,1536]{1,0:T(8,128)(2,1)S(1)}, bf16[192,1536]{1,0:T(8,128)(2,1)S(1)}, u32[]{:S(2)}, u32[]{:S(2)}) %collective-permute-start.31) | collective-permute-done | bytes 589856 | tf_op jit(solution)/shard_map/ppermute | solution.py:169
  129.0 11.0 %collective-permute-done.13 = bf16[192,1536]{1,0:T(8,128)(2,1)S(1)} collective-permute-done((bf16[192,1536]{1,0:T(8,128)(2,1)S(1)}, bf16[192,1536]{1,0:T(8,128)(2,1)S(1)}, u32[]{:S(2)}, u32[]{:S(2)}) %collective-permute-start.13) | collective-permute-done | bytes 589856 | tf_op jit(solution)/shard_map/ppermute | solution.py:169
  145.2 11.1 %collective-permute-done.42 = bf16[192,1536]{1,0:T(8,128)(2,1)S(1)} collective-permute-done((bf16[192,1536]{1,0:T(8,128)(2,1)S(1)}, bf16[192,1536]{1,0:T(8,128)(2,1)S(1)}, u32[]{:S(2)}, u32[]{:S(2)}) %collective-permute-start.42) | collective-permute-done | bytes 589856 | tf_op jit(solution)/shard_map/ppermute | solution.py:169
  158.2 7.4 collective-permute-done.3
  195.6 6.2 collective-permute-done.6
  231.9 4.0 convolution_convert_fusion
  246.2 12.9 %fusion.90 = bf16[12,512,64]{1,2,0:T(8,128)(2,1)S(1)} fusion(bf16[12,512,64]{1,2,0:T(8,128)(2,1)S(1)} %bitcast.281, f32[12,512,512]{1,2,0:T(8,128)S(1)} %get-tuple-element.307, f32[12,512]{1,0:T(8,128)S(1)} %fusion.3, f32[12,512]{1,0:T(8,128)S(1)} %get-tuple-element.306), kind=kOutput, calls=%fused_computation.156 | convolution fusion | flops 412483584 | bytes 14204928 | tf_op jit(solution)/shard_map/hqk,hkd->hqd/dot_general | solution.py:103
  263.3 20.4 %multiply_convert_fusion.5 = (bf16[512,3072]{1,0:T(8,128)(2,1)S(1)}, f32[512,3072]{1,0:T(8,128)}, f32[512,3072]{1,0:T(8,128)}) fusion(bf16[512,768]{1,0:T(8,128)(2,1)S(1)} %fusion.91, bf16[384,1536]{1,0:T(8,128)(2,1)} %collective-permute-done.18, bf16[96,1536]{1,0:T(8,128)(2,1)S(1)} %copy-done.98, bf16[96,1536]{1,0:T(8,128)(2,1)S(1)} %copy-done.95, ...), kind=kOutput, calls=%fused_computation.55 | convolution fusion | flops 2541748224 | bytes 21233664 | tf_op jit(solution)/shard_map/dot_general | solution.py:23
  283.7 4.9 fusion.277
  306.7 20.9 %multiply_convert_fusion.4 = (bf16[512,3072]{1,0:T(8,128)(2,1)S(1)}, f32[512,3072]{1,0:T(8,128)}, f32[512,3072]{1,0:T(8,128)}) fusion(bf16[512,768]{1,0:T(8,128)(2,1)S(1)} %fusion.93, bf16[384,1536]{1,0:T(8,128)(2,1)} %collective-permute-done.45, bf16[96,1536]{1,0:T(8,128)(2,1)S(1)} %copy-done.107, bf16[96,1536]{1,0:T(8,128)(2,1)S(1)} %copy-done.105, ...), kind=kOutput, calls=%fused_computation.38 | convolution fusion | flops 2541748224 | bytes 21233664 | tf_op jit(solution)/shard_map/dot_general | solution.py:23
  329.4 4.1 fusion.280
  336.1 10.6 %multiply_convert_fusion.3 = bf16[512,3072]{1,0:T(8,128)(2,1)S(1)} fusion(bf16[512,768]{1,0:T(8,128)(2,1)S(1)} %get-tuple-element.102, f32[512,3072]{1,0:T(8,128)} %get-tuple-element.105, f32[512,3072]{1,0:T(8,128)} %get-tuple-element.317, bf16[384,1536]{1,0:T(8,128)(2,1)} %collective-permute-done.54, bf16[96,1536]{1,0:T(8,128)(2,1)S(1)} %copy-done.103, ...), kind=kOutput, calls=%fused_computation.37 | convolution fusion | flops 2453667840 | bytes 21233664 | tf_op jit(solution)/shard_map/dot_general | solution.py:23
  346.7 6.8 multiply_reduce_fusion.3
  366.3 4.8 fusion.283
  371.2 3.9 fusion.100
  375.1 12.2 %fusion.97 = bf16[12,256,64]{1,2,0:T(8,128)(2,1)} fusion(bf16[12,512,64]{1,2,0:T(8,128)(2,1)} %bitcast.284, f32[12,512,256]{1,2,0:T(8,128)} %fusion.283, f32[12,512,256]{1,2,0:T(8,128)} %copy-done.3, f32[256]{0:T(256)} %convert_element_type.514, f32[12,512]{1,0:T(8,128)} %log_add_fusion.1), kind=kOutput, calls=%fused_computation.169 | convolution fusion | flops 212736256 | bytes 13788160 | tf_op jit(solution)/shard_map/hqk,hqd->hkd/dot_general | solution.py:116
  387.3 12.3 %multiply_convert_fusion.8 = bf16[12,512,64]{1,2,0:T(8,128)(2,1)} fusion(bf16[12,256,64]{1,2,0:T(8,128)(2,1)} %bitcast.289, f32[12,512,256]{1,2,0:T(8,128)} %fusion.283, f32[12,512,256]{1,2,0:T(8,128)} %copy-done.3, f32[256]{0:T(256)} %convert_element_type.514, f32[12,512]{1,0:T(8,128)} %log_add_fusion.1), kind=kOutput, calls=%fused_computation.124 | convolution fusion | flops 213129472 | bytes 13788160 | tf_op jit(solution)/shard_map/hqk,hkd->hqd/dot_general | solution.py:115
  399.6 12.6 %fusion.55 = f32[12,512,32]{1,2,0:T(8,128)} fusion(f32[12,512,256]{1,2,0:T(8,128)} %fusion.283, f32[12,512,256]{1,2,0:T(8,128)} %copy-done.3, f32[256]{0:T(256)} %convert_element_type.514, f32[12,512]{1,0:T(8,128)} %log_add_fusion.1, pred[256,32]{0,1:T(32,128)(4,1)} %bitcast_compare_fusion.1), kind=kOutput, calls=%fused_computation.93 | convolution fusion | flops 111679744 | bytes 13403136 | tf_op jit(solution)/shard_map/hqk,kb->hqb/dot_general | solution.py:120
  412.2 4.0 multiply_reduce_fusion.4
  418.6 10.2 %multiply_convert_fusion.1 = bf16[512,3072]{1,0:T(8,128)(2,1)S(1)} fusion(bf16[512,768]{1,0:T(8,128)(2,1)S(1)} %get-tuple-element.98, f32[512,3072]{1,0:T(8,128)} %get-tuple-element.107, f32[512,3072]{1,0:T(8,128)} %get-tuple-element.310, bf16[384,1536]{1,0:T(8,128)(2,1)} %collective-permute-done.27, bf16[96,1536]{1,0:T(8,128)(2,1)S(1)} %copy-done.93, ...), kind=kOutput, calls=%fused_computation.32 | convolution fusion | flops 2453667840 | bytes 21233664 | tf_op jit(solution)/shard_map/dot_general | solution.py:23
  428.9 5.9 multiply_reduce_fusion.5
  445.8 4.9 convolution_convert_fusion.4
  455.0 6.4 fusion.284
  461.3 7.8 fusion.84
  469.1 19.0 %multiply_convert_fusion.7 = bf16[12,512,64]{1,2,0:T(8,128)(2,1)} fusion(bf16[12,512,64]{1,2,0:T(8,128)(2,1)S(1)} %bitcast.278, f32[12,512,512]{1,2,0:T(8,128)} %fusion.284, f32[12,512,512]{1,2,0:T(8,128)} %copy-done.2, f32[512]{0:T(512)S(1)} %copy-done.179, f32[12,512]{1,0:T(8,128)} %log_add_fusion), kind=kOutput, calls=%fused_computation.119 | convolution fusion | flops 425466368 | bytes 26765312 | tf_op jit(solution)/shard_map/hqk,hkd->hqd/dot_general | solution.py:115
  488.1 19.1 %multiply_convert_fusion.6 = bf16[12,512,64]{1,2,0:T(8,128)(2,1)} fusion(bf16[12,512,64]{1,2,0:T(8,128)(2,1)S(1)} %bitcast.280, f32[12,512,512]{1,2,0:T(8,128)} %fusion.284, f32[12,512,512]{1,2,0:T(8,128)} %copy-done.2, f32[512]{0:T(512)} %convert_element_type.524, f32[12,512]{1,0:T(8,128)} %log_add_fusion), kind=kOutput, calls=%fused_computation.118 | convolution fusion | flops 425466368 | bytes 26765312 | tf_op jit(solution)/shard_map/hqk,hqd->hkd/dot_general | solution.py:116
  507.3 19.1 %fusion.44 = f32[12,512,32]{1,2,0:T(8,128)} fusion(f32[12,512,512]{1,2,0:T(8,128)} %fusion.284, f32[12,512,512]{1,2,0:T(8,128)} %copy-done.2, f32[512]{0:T(512)} %convert_element_type.524, f32[12,512]{1,0:T(8,128)} %log_add_fusion, pred[512,32]{0,1:T(32,128)(4,1)S(1)} %copy-done.109), kind=kOutput, calls=%fused_computation.88 | convolution fusion | flops 223353344 | bytes 25995264 | tf_op jit(solution)/shard_map/hqk,kb->hqb/dot_general | solution.py:120
  546.7 6.7 fusion.89
  591.3 6.5 collective-permute-done.57
  608.8 7.7 collective-permute-done.101
  617.1 8.0 %collective-permute-done.99 = bf16[96,1536]{1,0:T(8,128)(2,1)S(1)} collective-permute-done((bf16[96,1536]{1,0:T(8,128)(2,1)S(1)}, bf16[96,1536]{1,0:T(8,128)(2,1)S(1)}, u32[]{:S(2)}, u32[]{:S(2)}) %collective-permute-start.99) | collective-permute-done | bytes 294944 | tf_op jit(solution)/shard_map/ppermute | solution.py:169
  629.5 9.6 %collective-permute-done.102 = bf16[192,1536]{1,0:T(8,128)(2,1)S(1)} collective-permute-done((bf16[192,1536]{1,0:T(8,128)(2,1)S(1)}, bf16[192,1536]{1,0:T(8,128)(2,1)S(1)}, u32[]{:S(2)}, u32[]{:S(2)}) %collective-permute-start.102) | collective-permute-done | bytes 589856 | tf_op jit(solution)/shard_map/ppermute | solution.py:169
  641.3 5.0 collective-permute-done.63
  656.3 4.4 collective-permute-done.104
  665.2 4.2 add_convert_fusion
  720.7 9.8 %collective-permute-done.110 = bf16[192,1536]{1,0:T(8,128)(2,1)S(1)} collective-permute-done((bf16[192,1536]{1,0:T(8,128)(2,1)S(1)}, bf16[192,1536]{1,0:T(8,128)(2,1)S(1)}, u32[]{:S(2)}, u32[]{:S(2)}) %collective-permute-start.110) | collective-permute-done | bytes 589856 | tf_op jit(solution)/shard_map/ppermute | solution.py:169
  731.8 11.4 %collective-permute-done.80 = bf16[192,1536]{1,0:T(8,128)(2,1)S(1)} collective-permute-done((bf16[192,1536]{1,0:T(8,128)(2,1)S(1)}, bf16[192,1536]{1,0:T(8,128)(2,1)S(1)}, u32[]{:S(2)}, u32[]{:S(2)}) %collective-permute-start.80) | collective-permute-done | bytes 589856 | tf_op jit(solution)/shard_map/ppermute | solution.py:169
  746.0 4.8 collective-permute-done.72
  762.2 5.7 collective-permute-start.73
  767.9 7.2 collective-permute-done.112
  778.6 7.7 collective-permute-done.82
  787.1 4.1 collective-permute-done.74
  (910 shorter events, 370.2 us)
Async XLA Ops:
  0.7 35.4 %collective-permute-start.21 = (bf16[48,1536]{1,0:T(8,128)(2,1)}, bf16[48,1536]{1,0:T(8,128)(2,1)S(1)}, u32[]{:S(2)}, u32[]{:S(2)}) collective-permute-start(bf16[48,1536]{1,0:T(8,128)(2,1)} %bitcast.302), channel_id=1, source_target_pairs={{0,24},{1,25},{2,26},{3,27},{4,28},{5,29},{6,30},{7,31},{8,16},{9,... | collective-permute-start | bytes 442376 | tf_op jit(solution)/shard_map/ppermute | solution.py:169
  5.8 31.0 %collective-permute-start.20 = (bf16[48,1536]{1,0:T(8,128)(2,1)}, bf16[48,1536]{1,0:T(8,128)(2,1)S(1)}, u32[]{:S(2)}, u32[]{:S(2)}) collective-permute-start(bf16[48,1536]{1,0:T(8,128)(2,1)} %bitcast.303), channel_id=1, source_target_pairs={{0,16},{1,17},{2,18},{3,19},{4,20},{5,21},{6,22},{7,23},{8,24},{9,... | collective-permute-start | bytes 442376 | tf_op jit(solution)/shard_map/ppermute | solution.py:169
  5.8 33.3 %collective-permute-start.19 = (bf16[48,1536]{1,0:T(8,128)(2,1)}, bf16[48,1536]{1,0:T(8,128)(2,1)S(1)}, u32[]{:S(2)}, u32[]{:S(2)}) collective-permute-start(bf16[48,1536]{1,0:T(8,128)(2,1)} %bitcast.304), channel_id=1, source_target_pairs={{0,8},{1,9},{2,10},{3,11},{4,12},{5,13},{6,14},{7,15},{8,0},{9,1},... | collective-permute-start | bytes 442376 | tf_op jit(solution)/shard_map/ppermute | solution.py:169
  7.1 24.3 %collective-permute-start.9 = (bf16[2,6,2,31]{3,1,2,0:T(8,128)(2,1)S(1)}, bf16[2,6,2,31]{3,1,2,0:T(8,128)(2,1)}, u32[]{:S(2)}, u32[]{:S(2)}) collective-permute-start(bf16[2,6,2,31]{3,1,2,0:T(8,128)(2,1)S(1)} %pad_maximum_fusion.53), channel_id=1, source_target_pairs={{0,1},{1,0},{2,3},{3,2},{4,5},{5,4},{6,7},{7,6},{8,9},{9,8},{10,11... | collective-permute-start | bytes 4472 | tf_op jit(solution)/shard_map/ppermute | solution.py:169
  8.9 32.9 %collective-permute-start.48 = (bf16[48,1536]{1,0:T(8,128)(2,1)}, bf16[48,1536]{1,0:T(8,128)(2,1)S(1)}, u32[]{:S(2)}, u32[]{:S(2)}) collective-permute-start(bf16[48,1536]{1,0:T(8,128)(2,1)} %bitcast.306), channel_id=1, source_target_pairs={{0,24},{1,25},{2,26},{3,27},{4,28},{5,29},{6,30},{7,31},{8,16},{9,... | collective-permute-start | bytes 442376 | tf_op jit(solution)/shard_map/ppermute | solution.py:169
  36.8 37.4 %collective-permute-start.11 = (bf16[48,1536]{1,0:T(8,128)(2,1)}, bf16[48,1536]{1,0:T(8,128)(2,1)S(1)}, u32[]{:S(2)}, u32[]{:S(2)}) collective-permute-start(bf16[48,1536]{1,0:T(8,128)(2,1)} %param.30), channel_id=1, source_target_pairs={{0,16},{1,17},{2,18},{3,19},{4,20},{5,21},{6,22},{7,23},{8,24},{9,... | collective-permute-start | bytes 442376 | tf_op jit(solution)/shard_map/ppermute | solution.py:169
  39.0 25.2 %collective-permute-start.10 = (bf16[48,1536]{1,0:T(8,128)(2,1)}, bf16[48,1536]{1,0:T(8,128)(2,1)S(1)}, u32[]{:S(2)}, u32[]{:S(2)}) collective-permute-start(bf16[48,1536]{1,0:T(8,128)(2,1)} %param.30), channel_id=1, source_target_pairs={{0,8},{1,9},{2,10},{3,11},{4,12},{5,13},{6,14},{7,15},{8,0},{9,1},... | collective-permute-start | bytes 442376 | tf_op jit(solution)/shard_map/ppermute | solution.py:169
  52.0 23.7 %collective-permute-start.12 = (bf16[48,1536]{1,0:T(8,128)(2,1)}, bf16[48,1536]{1,0:T(8,128)(2,1)S(1)}, u32[]{:S(2)}, u32[]{:S(2)}) collective-permute-start(bf16[48,1536]{1,0:T(8,128)(2,1)} %param.30), channel_id=1, source_target_pairs={{0,24},{1,25},{2,26},{3,27},{4,28},{5,29},{6,30},{7,31},{8,16},{9,... | collective-permute-start | bytes 442376 | tf_op jit(solution)/shard_map/ppermute | solution.py:169
  61.0 21.3 %collective-permute-start.38 = (bf16[48,1536]{1,0:T(8,128)(2,1)S(1)}, bf16[48,1536]{1,0:T(8,128)(2,1)S(1)}, u32[]{:S(2)}, u32[]{:S(2)}) collective-permute-start(bf16[48,1536]{1,0:T(8,128)(2,1)S(1)} %copy-done.117), channel_id=1, source_target_pairs={{0,16},{1,17},{2,18},{3,19},{4,20},{5,21},{6,22},{7,23},{8,24},{9,... | collective-permute-start | bytes 442376 | tf_op jit(solution)/shard_map/ppermute | solution.py:169
  83.5 31.5 %collective-permute-start.24 = (bf16[192,1536]{1,0:T(8,128)(2,1)S(1)}, bf16[192,1536]{1,0:T(8,128)(2,1)S(1)}, u32[]{:S(2)}, u32[]{:S(2)}) collective-permute-start(bf16[192,1536]{1,0:T(8,128)(2,1)S(1)} %pad_maximum_fusion.20), channel_id=1, source_target_pairs={{0,1},{1,0},{2,3},{3,2},{4,5},{5,4},{6,7},{7,6},{8,9},{9,8},{10,11... | collective-permute-start | bytes 1769480 | tf_op jit(solution)/shard_map/ppermute | solution.py:169
  88.9 28.5 %collective-permute-start.51 = (bf16[192,1536]{1,0:T(8,128)(2,1)S(1)}, bf16[192,1536]{1,0:T(8,128)(2,1)S(1)}, u32[]{:S(2)}, u32[]{:S(2)}) collective-permute-start(bf16[192,1536]{1,0:T(8,128)(2,1)S(1)} %pad_maximum_fusion.22), channel_id=1, source_target_pairs={{0,1},{1,0},{2,3},{3,2},{4,5},{5,4},{6,7},{7,6},{8,9},{9,8},{10,11... | collective-permute-start | bytes 1769480 | tf_op jit(solution)/shard_map/ppermute | solution.py:169
  89.4 25.3 %collective-permute-start.49 = (bf16[192,1536]{1,0:T(8,128)(2,1)S(1)}, bf16[192,1536]{1,0:T(8,128)(2,1)S(1)}, u32[]{:S(2)}, u32[]{:S(2)}) collective-permute-start(bf16[192,1536]{1,0:T(8,128)(2,1)S(1)} %pad_maximum_fusion.22), channel_id=1, source_target_pairs={{0,4},{1,5},{2,6},{3,7},{4,0},{5,1},{6,2},{7,3},{8,12},{9,13},{10,... | collective-permute-start | bytes 1769480 | tf_op jit(solution)/shard_map/ppermute | solution.py:169
  94.4 33.0 %collective-permute-start.31 = (bf16[192,1536]{1,0:T(8,128)(2,1)S(1)}, bf16[192,1536]{1,0:T(8,128)(2,1)S(1)}, u32[]{:S(2)}, u32[]{:S(2)}) collective-permute-start(bf16[192,1536]{1,0:T(8,128)(2,1)S(1)} %pad_maximum_fusion.21), channel_id=1, source_target_pairs={{0,4},{1,5},{2,6},{3,7},{4,0},{5,1},{6,2},{7,3},{8,12},{9,13},{10,... | collective-permute-start | bytes 1769480 | tf_op jit(solution)/shard_map/ppermute | solution.py:169
  102.1 37.9 %collective-permute-start.13 = (bf16[192,1536]{1,0:T(8,128)(2,1)S(1)}, bf16[192,1536]{1,0:T(8,128)(2,1)S(1)}, u32[]{:S(2)}, u32[]{:S(2)}) collective-permute-start(bf16[192,1536]{1,0:T(8,128)(2,1)S(1)} %get-tuple-element.276), channel_id=1, source_target_pairs={{0,4},{1,5},{2,6},{3,7},{4,0},{5,1},{6,2},{7,3},{8,12},{9,13},{10,... | collective-permute-start | bytes 1769480 | tf_op jit(solution)/shard_map/ppermute | solution.py:169
  114.7 26.9 %collective-permute-start.33 = (bf16[192,1536]{1,0:T(8,128)(2,1)S(1)}, bf16[192,1536]{1,0:T(8,128)(2,1)S(1)}, u32[]{:S(2)}, u32[]{:S(2)}) collective-permute-start(bf16[192,1536]{1,0:T(8,128)(2,1)S(1)} %pad_maximum_fusion.21), channel_id=1, source_target_pairs={{0,1},{1,0},{2,3},{3,2},{4,5},{5,4},{6,7},{7,6},{8,9},{9,8},{10,11... | collective-permute-start | bytes 1769480 | tf_op jit(solution)/shard_map/ppermute | solution.py:169
  115.1 28.5 %collective-permute-start.15 = (bf16[192,1536]{1,0:T(8,128)(2,1)S(1)}, bf16[192,1536]{1,0:T(8,128)(2,1)S(1)}, u32[]{:S(2)}, u32[]{:S(2)}) collective-permute-start(bf16[192,1536]{1,0:T(8,128)(2,1)S(1)} %get-tuple-element.276), channel_id=1, source_target_pairs={{0,1},{1,0},{2,3},{3,2},{4,5},{5,4},{6,7},{7,6},{8,9},{9,8},{10,11... | collective-permute-start | bytes 1769480 | tf_op jit(solution)/shard_map/ppermute | solution.py:169
  117.4 38.9 %collective-permute-start.42 = (bf16[192,1536]{1,0:T(8,128)(2,1)S(1)}, bf16[192,1536]{1,0:T(8,128)(2,1)S(1)}, u32[]{:S(2)}, u32[]{:S(2)}) collective-permute-start(bf16[192,1536]{1,0:T(8,128)(2,1)S(1)} %get-tuple-element.256), channel_id=1, source_target_pairs={{0,1},{1,0},{2,3},{3,2},{4,5},{5,4},{6,7},{7,6},{8,9},{9,8},{10,11... | collective-permute-start | bytes 1769480 | tf_op jit(solution)/shard_map/ppermute | solution.py:169
  127.4 29.2 %collective-permute-start.40 = (bf16[192,1536]{1,0:T(8,128)(2,1)S(1)}, bf16[192,1536]{1,0:T(8,128)(2,1)S(1)}, u32[]{:S(2)}, u32[]{:S(2)}) collective-permute-start(bf16[192,1536]{1,0:T(8,128)(2,1)S(1)} %get-tuple-element.256), channel_id=1, source_target_pairs={{0,4},{1,5},{2,6},{3,7},{4,0},{5,1},{6,2},{7,3},{8,12},{9,13},{10,... | collective-permute-start | bytes 1769480 | tf_op jit(solution)/shard_map/ppermute | solution.py:169
  140.0 25.7 %collective-permute-start.3 = (bf16[192,1664]{1,0:T(8,128)(2,1)S(1)}, bf16[192,1664]{1,0:T(8,128)(2,1)S(1)}, u32[]{:S(2)}, u32[]{:S(2)}) collective-permute-start(bf16[192,1664]{1,0:T(8,128)(2,1)S(1)} %pad_maximum_fusion.19), channel_id=1, source_target_pairs={{0,4},{1,5},{2,6},{3,7},{4,0},{5,1},{6,2},{7,3},{8,12},{9,13},{10,... | collective-permute-start | bytes 1916936 | tf_op jit(solution)/shard_map/ppermute | solution.py:169
  141.6 27.0 %collective-permute-start.5 = (bf16[192,1664]{1,0:T(8,128)(2,1)S(1)}, bf16[192,1664]{1,0:T(8,128)(2,1)S(1)}, u32[]{:S(2)}, u32[]{:S(2)}) collective-permute-start(bf16[192,1664]{1,0:T(8,128)(2,1)S(1)} %pad_maximum_fusion.19), channel_id=1, source_target_pairs={{0,1},{1,0},{2,3},{3,2},{4,5},{5,4},{6,7},{7,6},{8,9},{9,8},{10,11... | collective-permute-start | bytes 1916936 | tf_op jit(solution)/shard_map/ppermute | solution.py:169
  143.6 34.6 %collective-permute-start.25 = (bf16[96,1536]{1,0:T(8,128)(2,1)S(1)}, bf16[96,1536]{1,0:T(8,128)(2,1)S(1)}, u32[]{:S(2)}, u32[]{:S(2)}) collective-permute-start(bf16[96,1536]{1,0:T(8,128)(2,1)S(1)} %slice.819), channel_id=1, source_target_pairs={{0,4},{1,5},{2,6},{3,7},{4,0},{5,1},{6,2},{7,3},{8,12},{9,13},{10,... | collective-permute-start | bytes 884744 | tf_op jit(solution)/shard_map/ppermute | solution.py:169
  156.3 24.5 %collective-permute-start.26 = (bf16[96,1536]{1,0:T(8,128)(2,1)S(1)}, bf16[96,1536]{1,0:T(8,128)(2,1)S(1)}, u32[]{:S(2)}, u32[]{:S(2)}) collective-permute-start(bf16[96,1536]{1,0:T(8,128)(2,1)S(1)} %slice.820), channel_id=1, source_target_pairs={{0,1},{1,0},{2,3},{3,2},{4,5},{5,4},{6,7},{7,6},{8,9},{9,8},{10,11... | collective-permute-start | bytes 884744 | tf_op jit(solution)/shard_map/ppermute | solution.py:169
  168.6 34.6 %collective-permute-start.23 = (bf16[384,1536]{1,0:T(8,128)(2,1)S(1)}, bf16[384,1536]{1,0:T(8,128)(2,1)S(1)}, u32[]{:S(2)}, u32[]{:S(2)}) collective-permute-start(bf16[384,1536]{1,0:T(8,128)(2,1)S(1)} %get-tuple-element.225), channel_id=1, source_target_pairs={{0,2},{1,3},{2,0},{3,1},{4,6},{5,7},{6,4},{7,5},{8,10},{9,11},{10,... | collective-permute-start | bytes 3538952 | tf_op jit(solution)/shard_map/ppermute | solution.py:169
  204.6 79.1 %collective-permute-start.27 = (bf16[384,1536]{1,0:T(8,128)(2,1)}, bf16[384,1536]{1,0:T(8,128)(2,1)}, u32[]{:S(2)}, u32[]{:S(2)}) collective-permute-start(bf16[384,1536]{1,0:T(8,128)(2,1)} %pad_maximum_fusion.5), channel_id=1, source_target_pairs={{0,2},{1,3},{2,0},{3,1},{4,6},{5,7},{6,4},{7,5},{8,10},{9,11},{10,... | collective-permute-start | bytes 3538952 | tf_op jit(solution)/shard_map/ppermute | solution.py:169
  205.2 124.1 %collective-permute-start.54 = (bf16[384,1536]{1,0:T(8,128)(2,1)}, bf16[384,1536]{1,0:T(8,128)(2,1)}, u32[]{:S(2)}, u32[]{:S(2)}) collective-permute-start(bf16[384,1536]{1,0:T(8,128)(2,1)} %pad_maximum_fusion.10), channel_id=1, source_target_pairs={{0,2},{1,3},{2,0},{3,1},{4,6},{5,7},{6,4},{7,5},{8,10},{9,11},{10,... | collective-permute-start | bytes 3538952 | tf_op jit(solution)/shard_map/ppermute | solution.py:169
  208.6 53.1 %collective-permute-start.18 = (bf16[384,1536]{1,0:T(8,128)(2,1)}, bf16[384,1536]{1,0:T(8,128)(2,1)}, u32[]{:S(2)}, u32[]{:S(2)}) collective-permute-start(bf16[384,1536]{1,0:T(8,128)(2,1)} %pad_maximum_fusion.4), channel_id=1, source_target_pairs={{0,2},{1,3},{2,0},{3,1},{4,6},{5,7},{6,4},{7,5},{8,10},{9,11},{10,... | collective-permute-start | bytes 3538952 | tf_op jit(solution)/shard_map/ppermute | solution.py:169
  213.8 91.4 %collective-permute-start.45 = (bf16[384,1536]{1,0:T(8,128)(2,1)}, bf16[384,1536]{1,0:T(8,128)(2,1)}, u32[]{:S(2)}, u32[]{:S(2)}) collective-permute-start(bf16[384,1536]{1,0:T(8,128)(2,1)} %pad_maximum_fusion.9), channel_id=1, source_target_pairs={{0,2},{1,3},{2,0},{3,1},{4,6},{5,7},{6,4},{7,5},{8,10},{9,11},{10,... | collective-permute-start | bytes 3538952 | tf_op jit(solution)/shard_map/ppermute | solution.py:169
  532.2 68.6 %collective-permute-start.98 = (bf16[384,768]{1,0:T(8,128)(2,1)}, bf16[384,768]{1,0:T(8,128)(2,1)}, u32[]{:S(2)}, u32[]{:S(2)}) collective-permute-start(bf16[384,768]{1,0:T(8,128)(2,1)} %convolution_convert_fusion.11), channel_id=1, source_target_pairs={{0,2},{1,3},{2,0},{3,1},{4,6},{5,7},{6,4},{7,5},{8,10},{9,11},{10,... | collective-permute-start | bytes 1769480 | tf_op jit(solution)/shard_map/ppermute | solution.py:169
  537.8 31.6 %collective-permute-start.84 = (f32[2,4,8,48]{3,2,1,0:T(8,128)}, f32[2,4,8,48]{3,2,1,0:T(8,128)}, u32[]{:S(2)}, u32[]{:S(2)}) collective-permute-start(f32[2,4,8,48]{3,2,1,0:T(8,128)} %slice_bitcast_fusion.2), channel_id=1, source_target_pairs={{0,2},{1,3},{2,0},{3,1},{4,6},{5,7},{6,4},{7,5},{8,10},{9,11},{10,... | collective-permute-start | bytes 36872 | tf_op jit(solution)/shard_map/ppermute | solution.py:169
  563.4 35.8 %collective-permute-start.55 = (bf16[256,768]{1,0:T(8,128)(2,1)S(1)}, bf16[256,768]{1,0:T(8,128)(2,1)S(1)}, u32[]{:S(2)}, u32[]{:S(2)}) collective-permute-start(bf16[256,768]{1,0:T(8,128)(2,1)S(1)} %broadcast_select_fusion.3), channel_id=1, source_target_pairs={{0,1},{1,0},{2,3},{3,2},{4,5},{5,4},{6,7},{7,6},{8,9},{9,8},{10,11... | collective-permute-start | bytes 1179656 | tf_op jit(solution)/shard_map/ppermute | solution.py:169
  581.7 81.9 %collective-permute-start.114 = (bf16[384,3072]{1,0:T(8,128)(2,1)}, bf16[384,3072]{1,0:T(8,128)(2,1)}, u32[]{:S(2)}, u32[]{:S(2)}) collective-permute-start(bf16[384,3072]{1,0:T(8,128)(2,1)} %convolution_convert_fusion.1), channel_id=1, source_target_pairs={{0,2},{1,3},{2,0},{3,1},{4,6},{5,7},{6,4},{7,5},{8,10},{9,11},{10,... | collective-permute-start | bytes 7077896 | tf_op jit(solution)/shard_map/ppermute | solution.py:169
  590.3 79.1 %collective-permute-start.106 = (bf16[384,3072]{1,0:T(8,128)(2,1)}, bf16[384,3072]{1,0:T(8,128)(2,1)}, u32[]{:S(2)}, u32[]{:S(2)}) collective-permute-start(bf16[384,3072]{1,0:T(8,128)(2,1)} %convolution_convert_fusion.2), channel_id=1, source_target_pairs={{0,2},{1,3},{2,0},{3,1},{4,6},{5,7},{6,4},{7,5},{8,10},{9,11},{10,... | collective-permute-start | bytes 7077896 | tf_op jit(solution)/shard_map/ppermute | solution.py:169
  602.8 70.9 %collective-permute-start.76 = (bf16[384,3072]{1,0:T(8,128)(2,1)}, bf16[384,3072]{1,0:T(8,128)(2,1)}, u32[]{:S(2)}, u32[]{:S(2)}) collective-permute-start(bf16[384,3072]{1,0:T(8,128)(2,1)} %convolution_convert_fusion.3), channel_id=1, source_target_pairs={{0,2},{1,3},{2,0},{3,1},{4,6},{5,7},{6,4},{7,5},{8,10},{9,11},{10,... | collective-permute-start | bytes 7077896 | tf_op jit(solution)/shard_map/ppermute | solution.py:169
  604.2 21.5 %collective-permute-start.59 = (bf16[384,2304]{1,0:T(8,128)(2,1)S(1)}, bf16[384,2304]{1,0:T(8,128)(2,1)S(1)}, u32[]{:S(2)}, u32[]{:S(2)}) collective-permute-start(bf16[384,2304]{1,0:T(8,128)(2,1)S(1)} %copy-done.182), channel_id=1, source_target_pairs={{0,2},{1,3},{2,0},{3,1},{4,6},{5,7},{6,4},{7,5},{8,10},{9,11},{10,... | collective-permute-start | bytes 5308424 | tf_op jit(solution)/shard_map/ppermute | solution.py:169
  656.3 21.3 %collective-permute-start.68 = (bf16[384,3072]{1,0:T(8,128)(2,1)}, bf16[384,3072]{1,0:T(8,128)(2,1)}, u32[]{:S(2)}, u32[]{:S(2)}) collective-permute-start(bf16[384,3072]{1,0:T(8,128)(2,1)} %convolution_convert_fusion.4), channel_id=1, source_target_pairs={{0,2},{1,3},{2,0},{3,1},{4,6},{5,7},{6,4},{7,5},{8,10},{9,11},{10,... | collective-permute-start | bytes 7077896 | tf_op jit(solution)/shard_map/ppermute | solution.py:169
  660.6 21.9 %collective-permute-start.62 = (bf16[192,1536]{1,0:T(8,128)(2,1)}, bf16[192,1536]{1,0:T(8,128)(2,1)}, u32[]{:S(2)}, u32[]{:S(2)}) collective-permute-start(bf16[192,1536]{1,0:T(8,128)(2,1)} %pad_maximum_fusion.25), channel_id=1, source_target_pairs={{0,4},{1,5},{2,6},{3,7},{4,0},{5,1},{6,2},{7,3},{8,12},{9,13},{10,... | collective-permute-start | bytes 1769480 | tf_op jit(solution)/shard_map/ppermute | solution.py:169
  692.6 25.3 %collective-permute-start.118 = (bf16[192,1536]{1,0:T(8,128)(2,1)S(1)}, bf16[192,1536]{1,0:T(8,128)(2,1)S(1)}, u32[]{:S(2)}, u32[]{:S(2)}) collective-permute-start(bf16[192,1536]{1,0:T(8,128)(2,1)S(1)} %pad_maximum_fusion.40), channel_id=1, source_target_pairs={{0,1},{1,0},{2,3},{3,2},{4,5},{5,4},{6,7},{7,6},{8,9},{9,8},{10,11... | collective-permute-start | bytes 1769480 | tf_op jit(solution)/shard_map/ppermute | solution.py:169
  694.4 24.6 %collective-permute-start.116 = (bf16[192,1536]{1,0:T(8,128)(2,1)S(1)}, bf16[192,1536]{1,0:T(8,128)(2,1)S(1)}, u32[]{:S(2)}, u32[]{:S(2)}) collective-permute-start(bf16[192,1536]{1,0:T(8,128)(2,1)S(1)} %pad_maximum_fusion.39), channel_id=1, source_target_pairs={{0,4},{1,5},{2,6},{3,7},{4,0},{5,1},{6,2},{7,3},{8,12},{9,13},{10,... | collective-permute-start | bytes 1769480 | tf_op jit(solution)/shard_map/ppermute | solution.py:169
  706.2 24.3 %collective-permute-start.110 = (bf16[192,1536]{1,0:T(8,128)(2,1)S(1)}, bf16[192,1536]{1,0:T(8,128)(2,1)S(1)}, u32[]{:S(2)}, u32[]{:S(2)}) collective-permute-start(bf16[192,1536]{1,0:T(8,128)(2,1)S(1)} %pad_maximum_fusion.38), channel_id=1, source_target_pairs={{0,1},{1,0},{2,3},{3,2},{4,5},{5,4},{6,7},{7,6},{8,9},{9,8},{10,11... | collective-permute-start | bytes 1769480 | tf_op jit(solution)/shard_map/ppermute | solution.py:169
  707.8 23.8 %collective-permute-start.108 = (bf16[192,1536]{1,0:T(8,128)(2,1)S(1)}, bf16[192,1536]{1,0:T(8,128)(2,1)S(1)}, u32[]{:S(2)}, u32[]{:S(2)}) collective-permute-start(bf16[192,1536]{1,0:T(8,128)(2,1)S(1)} %pad_maximum_fusion.37), channel_id=1, source_target_pairs={{0,4},{1,5},{2,6},{3,7},{4,0},{5,1},{6,2},{7,3},{8,12},{9,13},{10,... | collective-permute-start | bytes 1769480 | tf_op jit(solution)/shard_map/ppermute | solution.py:169
  712.5 30.7 %collective-permute-start.80 = (bf16[192,1536]{1,0:T(8,128)(2,1)S(1)}, bf16[192,1536]{1,0:T(8,128)(2,1)S(1)}, u32[]{:S(2)}, u32[]{:S(2)}) collective-permute-start(bf16[192,1536]{1,0:T(8,128)(2,1)S(1)} %pad_maximum_fusion.31), channel_id=1, source_target_pairs={{0,1},{1,0},{2,3},{3,2},{4,5},{5,4},{6,7},{7,6},{8,9},{9,8},{10,11... | collective-permute-start | bytes 1769480 | tf_op jit(solution)/shard_map/ppermute | solution.py:169
  717.9 27.8 %collective-permute-start.78 = (bf16[192,1536]{1,0:T(8,128)(2,1)S(1)}, bf16[192,1536]{1,0:T(8,128)(2,1)S(1)}, u32[]{:S(2)}, u32[]{:S(2)}) collective-permute-start(bf16[192,1536]{1,0:T(8,128)(2,1)S(1)} %pad_maximum_fusion.30), channel_id=1, source_target_pairs={{0,4},{1,5},{2,6},{3,7},{4,0},{5,1},{6,2},{7,3},{8,12},{9,13},{10,... | collective-permute-start | bytes 1769480 | tf_op jit(solution)/shard_map/ppermute | solution.py:169
  718.9 31.9 %collective-permute-start.72 = (bf16[192,1536]{1,0:T(8,128)(2,1)S(1)}, bf16[192,1536]{1,0:T(8,128)(2,1)S(1)}, u32[]{:S(2)}, u32[]{:S(2)}) collective-permute-start(bf16[192,1536]{1,0:T(8,128)(2,1)S(1)} %pad_maximum_fusion.29), channel_id=1, source_target_pairs={{0,1},{1,0},{2,3},{3,2},{4,5},{5,4},{6,7},{7,6},{8,9},{9,8},{10,11... | collective-permute-start | bytes 1769480 | tf_op jit(solution)/shard_map/ppermute | solution.py:169
  730.5 21.8 %collective-permute-start.70 = (bf16[192,1536]{1,0:T(8,128)(2,1)S(1)}, bf16[192,1536]{1,0:T(8,128)(2,1)S(1)}, u32[]{:S(2)}, u32[]{:S(2)}) collective-permute-start(bf16[192,1536]{1,0:T(8,128)(2,1)S(1)} %pad_maximum_fusion.28), channel_id=1, source_target_pairs={{0,4},{1,5},{2,6},{3,7},{4,0},{5,1},{6,2},{7,3},{8,12},{9,13},{10,... | collective-permute-start | bytes 1769480 | tf_op jit(solution)/shard_map/ppermute | solution.py:169
  731.6 22.8 %collective-permute-start.119 = (bf16[48,1536]{1,0:T(8,128)(2,1)S(1)}, bf16[48,1536]{1,0:T(8,128)(2,1)S(1)}, u32[]{:S(2)}, u32[]{:S(2)}) collective-permute-start(bf16[48,1536]{1,0:T(8,128)(2,1)S(1)} %get-tuple-element.177), channel_id=1, source_target_pairs={{0,8},{1,9},{2,10},{3,11},{4,12},{5,13},{6,14},{7,15},{8,0},{9,1},... | collective-permute-start | bytes 442376 | tf_op jit(solution)/shard_map/ppermute | solution.py:169
  754.6 24.0 %collective-permute-start.81 = (bf16[48,1536]{1,0:T(8,128)(2,1)S(1)}, bf16[48,1536]{1,0:T(8,128)(2,1)S(1)}, u32[]{:S(2)}, u32[]{:S(2)}) collective-permute-start(bf16[48,1536]{1,0:T(8,128)(2,1)S(1)} %get-tuple-element.200), channel_id=1, source_target_pairs={{0,8},{1,9},{2,10},{3,11},{4,12},{5,13},{6,14},{7,15},{8,0},{9,1},... | collective-permute-start | bytes 442376 | tf_op jit(solution)/shard_map/ppermute | solution.py:169
  761.3 25.0 %collective-permute-start.82 = (bf16[48,1536]{1,0:T(8,128)(2,1)S(1)}, bf16[48,1536]{1,0:T(8,128)(2,1)S(1)}, u32[]{:S(2)}, u32[]{:S(2)}) collective-permute-start(bf16[48,1536]{1,0:T(8,128)(2,1)S(1)} %get-tuple-element.202), channel_id=1, source_target_pairs={{0,16},{1,17},{2,18},{3,19},{4,20},{5,21},{6,22},{7,23},{8,24},{9,... | collective-permute-start | bytes 442376 | tf_op jit(solution)/shard_map/ppermute | solution.py:169
  762.2 24.9 %collective-permute-start.73 = (bf16[48,1536]{1,0:T(8,128)(2,1)S(1)}, bf16[48,1536]{1,0:T(8,128)(2,1)S(1)}, u32[]{:S(2)}, u32[]{:S(2)}) collective-permute-start(bf16[48,1536]{1,0:T(8,128)(2,1)S(1)} %get-tuple-element.203), channel_id=1, source_target_pairs={{0,8},{1,9},{2,10},{3,11},{4,12},{5,13},{6,14},{7,15},{8,0},{9,1},... | collective-permute-start | bytes 442376 | tf_op jit(solution)/shard_map/ppermute | solution.py:169
  (273 other events, 2998.3 us)

commit v2 on v1

v2 whole, which is shorter than its diff:
```python
import functools

import jax
import jax.numpy as jnp
from jax import lax
from jax.experimental import pallas as pl
from jax.experimental.pallas import tpu as pltpu
from jax.sharding import PartitionSpec as P

HD = 64
GRID = 16
RELS = 2 * GRID - 1
LANES = 128
STRIP = 128

highest = lax.Precision.HIGHEST
epsilon = 1e-06
masked_score = -30000.0
mask_columns = (-29952.0, -48.0)
bf16 = jnp.bfloat16
f32 = jnp.float32
vmem = pltpu.CompilerParams(vmem_limit_bytes=16 * 2**20)


def cast_low(values):
    return values.astype(bf16)


def matmul(left_side, right_side):
    return jnp.dot(left_side, right_side, preferred_element_type=f32)


def matmul_tn(left_side, right_side):
    return lax.dot_general(
        left_side, right_side, (((0,), (0,)), ((), ())), preferred_element_type=f32
    )


def matmul_nt(left_side, right_side):
    return lax.dot_general(
        left_side, right_side, (((1,), (1,)), ((), ())), preferred_element_type=f32
    )


def gelu_pair(hidden):
    cdf = 0.5 + 0.5 * lax.erf(hidden * (0.5**0.5))
    slope = cdf + hidden * jnp.exp(-0.5 * hidden * hidden) * (0.3989422804014327)
    return cast_low(hidden * cdf), cast_low(slope)


def spread_tables(tables):
    n = tables.shape[0]
    lane = jnp.arange(LANES)
    dimension, offset = jnp.divmod(jnp.arange(2 * RELS), RELS)
    own = jnp.arange(GRID)[None, :, None]
    picks = (offset[:, None, None] == own - lane % GRID + GRID - 1) & (
        dimension[:, None, None] == lane // GRID
    )
    parts = matmul(tables, cast_low(picks).reshape(2 * RELS, GRID * LANES))
    parts = jnp.transpose(cast_low(parts).reshape(n, GRID, LANES), (1, 0, 2)).reshape(GRID, -1)
    lane = jnp.tile(lane, n)
    row = jnp.arange(LANES)[:, None]
    ones = cast_low((row == lane) & (row // 2 == GRID))
    parts = [jnp.where(lane // GRID == c, parts, jnp.zeros_like(parts)) for c in range(2)]
    return jnp.pad(jnp.concatenate(parts, axis=0), ((0, LANES - 2 * GRID), (0, 0))) + ones


def table_grad(pairs):
    pairs = pairs[:, : 2 * GRID, : 2 * GRID].reshape(-1, 2, GRID, 2, GRID)
    pairs = jnp.stack([pairs[:, 0, :, 0], pairs[:, 1, :, 1]], axis=1)
    offset = jnp.arange(GRID)[:, None] - jnp.arange(GRID)[None, :] + GRID - 1
    hot = (offset[:, :, None] == jnp.arange(RELS)).astype(f32)
    return jnp.einsum("hcab,abr->hcr", pairs, hot, precision=highest)


class Projection:
    def __init__(self, views, tile, start, tiles):
        self.views, self.tile, self.start, self.tiles = views, tile, start, tiles

    def arrays(self):
        return [array for share in self.views for array, _, _ in share]

    def specs(self):
        return [
            pl.BlockSpec((rows, self.tile), lambda t, at=at: (at, self.start + t))
            for share in self.views
            for _, at, rows in share
        ]

    def group(self, refs):
        refs, out = list(refs), []
        for share in self.views:
            out.append([refs.pop(0) for _ in share])
        return out, refs


def whole(array):
    return pl.BlockSpec(array.shape, lambda t: (0,) * array.ndim)


def tile_of(array):
    return pl.BlockSpec((None,) + array.shape[1:], lambda t: (t, 0, 0))


def joined(parts, axis):
    return parts[0] if len(parts) == 1 else jnp.concatenate(parts, axis=axis)


def strips(rows):
    return [pl.ds(start, STRIP) for start in range(0, rows, STRIP)]


def project(x, weight, how, slope=None):
    rows, width = x.shape
    count = len(weight.arrays())

    def kernel(x_ref, *refs):
        shares, refs = weight.group(refs)
        x = x_ref[...]
        out = joined([matmul(x, joined([r[...] for r in share], 0)) for share in shares], 1)
        if how == "gelu":
            refs[0][...], refs[1][...] = gelu_pair(out)
        elif how == "slope":
            refs[1][...] = cast_low(out * refs[0][...].astype(f32))
        else:
            refs[0][...] = cast_low(out)

    result = jax.ShapeDtypeStruct((weight.tiles, rows, width), bf16)
    extra = [] if slope is None else [slope]
    outs = [result] * (2 if how == "gelu" else 1)
    got = pl.pallas_call(
        kernel,
        grid=(weight.tiles,),
        in_specs=[whole(x)] + weight.specs() + [tile_of(e) for e in extra],
        out_specs=[tile_of(out) for out in outs],
        out_shape=outs,
        compiler_params=vmem,
        cost_estimate=pl.CostEstimate(
            flops=2 * rows * width * width * weight.tiles,
            bytes_accessed=2 * width * weight.tiles * (width + 2 * rows),
            transcendentals=0,
        ),
    )(x, *weight.arrays(), *extra)
    return got if how == "gelu" else got[0]


def project_back(h, weight, how, extra=(), params=None, at=()):
    tiles, rows, width = h.shape
    n_extra = len(extra) + (params is not None)

    def kernel(h_ref, *refs):
        shares, refs = weight.group(refs)
        extra, outs, sums = refs[:n_extra], refs[n_extra:-1], refs[-1]
        t = pl.program_id(0)
        h = h_ref[...]
        parts = []

        def param(i):
            return extra[-1][at[i] : at[i] + 1, :]

        def forward(cut):
            residual = extra[0][cut, :].astype(f32)
            if len(at) > 2:
                residual = residual * param(2) + param(3)
            values = sums[cut, :] + residual
            center = values - jnp.mean(values, axis=-1, keepdims=True)
            scale = lax.rsqrt(jnp.mean(center * center, axis=-1, keepdims=True) + epsilon)
            normed = center * scale
            return normed, scale, cast_low(normed * param(0) + param(1))

        def backward(grad, normed, scale):
            product = grad * normed
            grads = [jnp.sum(product, axis=0, keepdims=True), jnp.sum(grad, axis=0, keepdims=True)]
            scaled = grad * param(0)
            inner = scaled - jnp.mean(scaled, axis=-1, keepdims=True)
            inner = (inner - normed * jnp.mean(scaled * normed, axis=-1, keepdims=True)) * scale
            return inner, cast_low(inner), jnp.concatenate(grads, axis=0)

        for pieces in zip(*shares):
            parts.append(matmul_nt(h, joined([piece[...] for piece in pieces], 1)))
        total = joined(parts, 1)

        @pl.when(t == 0)
        def _():
            sums[...] = total

        @pl.when(t > 0)
        def _():
            sums[...] += total

        @pl.when(t == tiles - 1)
        def _():
            if how == "low":
                for cut in strips(rows):
                    outs[0][cut, :] = cast_low(sums[cut, :])
            elif how == "add":
                for cut in strips(rows):
                    outs[0][cut, :] = cast_low(sums[cut, :] + extra[0][cut, :])
            elif how == "norm":
                for cut in strips(rows):
                    normed, scale, result = forward(cut)
                    outs[0][cut, :] = normed
                    outs[1][cut, :] = scale
                    outs[2][cut, :] = result
                    outs[3][cut, :] = result[:, width // 2 :]
            else:
                param_grads = jnp.zeros((2, width), f32)
                for cut in strips(rows):
                    if how == "final":
                        normed, scale, result = forward(cut)
                        outs[0][cut, :] = result
                        grad = extra[1][cut, :].astype(f32)
                    else:
                        normed, scale = extra[1][cut, :], extra[2][cut, :]
                        grad = sums[cut, :] + extra[0][cut, :]
                    pre, low, strip_grads = backward(grad, normed, scale)
                    param_grads = param_grads + strip_grads
                    outs[-4][cut, :] = pre
                    outs[-3][cut, :] = low
                    outs[-2][cut, :] = low[:, width // 2 :]
                outs[-1][...] = param_grads

    low = jax.ShapeDtypeStruct((rows, width), bf16)
    wide = jax.ShapeDtypeStruct((rows, width), f32)
    part = jax.ShapeDtypeStruct((rows, width // 2), bf16)
    back = [wide, low, part, jax.ShapeDtypeStruct((2, width), f32)]
    outs = {
        "low": [low],
        "add": [low],
        "norm": [wide, jax.ShapeDtypeStruct((rows, 1), f32), low, part],
        "back": back,
        "final": [low] + back,
    }[how]
    extra = list(extra) + ([] if params is None else [params])
    got = pl.pallas_call(
        kernel,
        grid=(tiles,),
        in_specs=[tile_of(h)] + weight.specs() + [whole(e) for e in extra],
        out_specs=[whole(out) for out in outs],
        out_shape=outs,
        scratch_shapes=[pltpu.VMEM((rows, width), f32)],
        compiler_params=vmem,
        cost_estimate=pl.CostEstimate(
            flops=2 * rows * width * width * tiles,
            bytes_accessed=2 * width * tiles * (width + rows) + 12 * rows * width,
            transcendentals=0,
        ),
    )(h, *weight.arrays(), *extra)
    return got if len(outs) > 1 else got[0]


def weight_grad(products, factor, cut=None):
    width = products[0][0].shape[1]
    high = width // 2
    counts = [product[2].shape[0] for product in products]
    ends = [sum(counts[: i + 1]) for i in range(len(counts))]
    starts = [end - count for end, count in zip(ends, counts)]
    tiles = ends[-1]

    def kernel(*refs):
        sides = [refs[4 * i : 4 * i + 4] for i in range(len(products))]
        outs = refs[4 * len(products) : -len(products)]
        turned = refs[-len(products) :]
        t = pl.program_id(0)
        for (left, left_other, right, right_other), held, start, end in zip(sides, turned, starts, ends):

            @pl.when(t == start)
            def _():
                held[...] = jnp.concatenate([left[...].T, left_other[...].T], axis=1)

            @pl.when((t >= start) & (t < end))
            def _():
                total = matmul(held[...], jnp.concatenate([right[...], right_other[...]], axis=0))
                if factor != 1.0:
                    total = total * factor
                total = cast_low(total)
                if cut is None:
                    outs[0][...] = total
                    return
                rows, columns, strip = cut
                if strip:
                    outs[0][...] = total[rows : rows + strip, columns:]
                    outs[1][...] = total[rows + strip :, columns:]
                else:
                    outs[0][...] = total[rows:, columns:]
                outs[-3][...] = total[rows:, :columns]
                outs[-2][...] = total[:rows, columns:]
                outs[-1][...] = total[:rows, :columns]

    def column(rows, columns):
        return pl.BlockSpec((rows, columns), lambda t: (0, t))

    in_specs, args = [], []
    for product, start, count in zip(products, starts, counts):
        rows = product[0].shape[0]
        tile = pl.BlockSpec(
            (None, rows, width),
            lambda t, start=start, count=count: (jnp.clip(t - start, 0, count - 1), 0, 0),
        )
        in_specs += [pl.BlockSpec((rows, high), lambda t: (0, 0))] * 2 + [tile] * 2
        args += product
    if cut is None:
        parts = [(high, width)]
    else:
        rows, columns, strip = cut
        parts = [(strip, columns), (rows - strip, columns)] if strip else [(rows, columns)]
        parts = parts + [(rows, columns)] * 3
    outs = pl.pallas_call(
        kernel,
        grid=(tiles,),
        in_specs=in_specs,
        out_specs=[column(*part) for part in parts],
        out_shape=[jax.ShapeDtypeStruct((rows, tiles * columns), bf16) for rows, columns in parts],
        scratch_shapes=[pltpu.VMEM((high, 2 * product[0].shape[0]), bf16) for product in products],
        compiler_params=vmem,
        cost_estimate=pl.CostEstimate(
            flops=sum(4 * high * product[2].size for product in products),
            bytes_accessed=sum(4 * product[2].size + 2 * product[0].size for product in products)
            + 2 * tiles * high * width,
            transcendentals=0,
        ),
    )(*args)
    return outs[0] if cut is None else outs


def pair_of(array, role):
    return pl.BlockSpec((None, array.shape[1], LANES), lambda i: (role, 0, i))


def attend_forward(q, k, v, hot, spread, other, keep):
    (q, q_role), (k, k_role), (v, v_role) = q, k, v
    spread, first_pair = spread
    rows, n, width = q.shape[1], k.shape[1], q.shape[2]
    heads = width // HD

    def kernel(q_ref, k_ref, v_ref, hot_ref, spread_ref, other_ref, keep_ref, context_ref, probs_ref):
        keys = jnp.concatenate([k_ref[...] * keep_ref[...], other_ref[...]], axis=1)
        values = v_ref[...]
        first = lax.broadcasted_iota(jnp.int32, (rows, LANES), 1) < HD
        queries = q_ref[...] * jnp.asarray(HD**-0.5, bf16)
        parts = []
        for h in range(2):
            mine = jnp.where(first if h == 0 else ~first, queries, jnp.zeros_like(queries))
            bias = cast_low(matmul(hot_ref[...], spread_ref[:, h * LANES : (h + 1) * LANES]))
            scores = matmul_nt(jnp.concatenate([mine, bias], axis=1), keys)
            weights = jnp.exp(scores - jnp.max(scores, axis=1, keepdims=True))
            probs = cast_low(weights * (1.0 / jnp.sum(weights, axis=1, keepdims=True)))
            probs_ref[h] = probs
            parts.append(matmul(probs, values))
        context_ref[...] = cast_low(jnp.where(first, parts[0], parts[1]))

    probs = jax.ShapeDtypeStruct((heads, rows, n), bf16)
    return pl.pallas_call(
        kernel,
        grid=(heads // 2,),
        in_specs=[
            pair_of(q, q_role),
            pair_of(k, k_role),
            pair_of(v, v_role),
            whole(hot),
            pl.BlockSpec((LANES, 2 * LANES), lambda i: (0, first_pair + i)),
            whole(other),
            whole(keep),
        ],
        out_specs=[
            pl.BlockSpec((rows, LANES), lambda i: (0, i)),
            pl.BlockSpec((2, rows, n), lambda i: (i, 0, 0)),
        ],
        out_shape=[jax.ShapeDtypeStruct((rows, width), bf16), probs],
        compiler_params=vmem,
        cost_estimate=pl.CostEstimate(
            flops=8 * heads * rows * n * LANES,
            bytes_accessed=2 * heads * rows * n,
            transcendentals=heads * rows * n,
        ),
    )(q, k, v, hot, spread, other, keep)


def attend_backward(q, k, v, grad, probs, hot, other, keep):
    (q, q_role), (k, k_role), (v, v_role) = q, k, v
    rows, n, width = q.shape[1], k.shape[1], q.shape[2]
    heads = width // HD
    together = q is k

    def kernel(q_ref, k_ref, v_ref, grad_ref, probs_ref, hot_ref, other_ref, keep_ref, *refs):
        if together:
            grads_ref, pairs_ref, held_ref = refs
            dq_ref, dk_ref, dv_ref = (grads_ref.at[i] for i in range(3))
        else:
            dq_ref, dkv_ref, pairs_ref, held_ref = refs
            dk_ref, dv_ref = dkv_ref.at[0], dkv_ref.at[1]
        keep = keep_ref[...]
        keys = jnp.concatenate([k_ref[...] * keep, other_ref[...]], axis=1)
        values = v_ref[...]
        first = lax.broadcasted_iota(jnp.int32, (rows, LANES), 1) < HD
        grad = grad_ref[...]
        turned_queries = q_ref[...].T
        turned_grad = grad.T
        hot = hot_ref[...]
        query_parts, key_parts, value_parts = [], [], []
        for h in range(2):
            mine = jnp.where(first if h == 0 else ~first, grad, jnp.zeros_like(grad))
            prob_grad = matmul_nt(mine, values)
            probs = probs_ref[h].astype(f32)
            mean = jnp.sum(probs * prob_grad, axis=1, keepdims=True)
            held_ref[...] = cast_low(probs * (prob_grad - mean))
            both = matmul(held_ref[...], keys)
            query_parts.append(both[:, :LANES])
            right = both[:, LANES:]
            high = cast_low(right)
            rest = cast_low(right - high.astype(f32))
            pairs_ref[h] = matmul(hot, high) + matmul(hot, rest)
            mine = slice(h * HD, (h + 1) * HD)
            key_parts.append(matmul(turned_queries[mine], held_ref[...]))
            value_parts.append(matmul(turned_grad[mine], probs_ref[h]))
        dq_ref[...] = cast_low(jnp.where(first, query_parts[0], query_parts[1]) * HD**-0.5)
        turned = jnp.concatenate(key_parts, axis=0).T
        dk_ref[...] = cast_low(turned * HD**-0.5 * keep.astype(f32))
        dv_ref[...] = cast_low(jnp.concatenate(value_parts, axis=0).T)

    def grads_of(array):
        return pl.BlockSpec((array.shape[0], array.shape[1], LANES), lambda i: (0, 0, i))

    if together:
        outs = [jax.ShapeDtypeStruct((3, rows, width), bf16)]
    else:
        outs = [jax.ShapeDtypeStruct((1, rows, width), bf16), jax.ShapeDtypeStruct((2, n, width), bf16)]
    out_specs = [grads_of(out) for out in outs]
    if not together:
        out_specs[0] = pl.BlockSpec((None, rows, LANES), lambda i: (0, 0, i))
    outs.append(jax.ShapeDtypeStruct((heads, LANES, LANES), f32))
    out_specs.append(pl.BlockSpec((2, LANES, LANES), lambda i: (i, 0, 0)))
    return pl.pallas_call(
        kernel,
        grid=(heads // 2,),
        in_specs=[
            pair_of(q, q_role),
            pair_of(k, k_role),
            pair_of(v, v_role),
            pl.BlockSpec((rows, LANES), lambda i: (0, i)),
            pl.BlockSpec((2, rows, n), lambda i: (i, 0, 0)),
            whole(hot),
            whole(other),
            whole(keep),
        ],
        out_specs=out_specs,
        out_shape=outs,
        scratch_shapes=[pltpu.VMEM((rows, n), bf16)],
        compiler_params=vmem,
        cost_estimate=pl.CostEstimate(
            flops=20 * heads * rows * n * LANES, bytes_accessed=2 * heads * rows * n, transcendentals=0
        ),
    )(q, k, v, grad, probs, hot, other, keep)


ORDER = (
    "w1", "page", "w1", "page", "w2", "w1", "page", "w2", "w3", "w1", "page", "w3", "w4", "w1", "w2", "page", "w1", "layers", "w4", "w5", "w3", "layers", "w2", "w5", "w3", "+g6", "w4",
    "w2", "w5", "w6", "w3", "g6", "w2", "layers", "w3", "w6", "w4", "layers", "w4", "w5", "+g4", "w4", "w6", "layers", "g4", "w5", "w6", "+g3", "w5", "+g5", "w6", "layers", "w6",
    "layers", "+g1", "layers", "+g2", "g1", "layers", "layers", "+g1", "g2", "g3", "+g2", "layers", "layers", "+g4", "+g3", "g1", "g2", "g5", "g3", "g4", "g1", "layers",
    "g3", "g2", "out", "g1", "layers", "+g5", "g3", "g4", "g2", "g3", "+g6", "g5", "small", "vision", "g2", "small", "g4", "g5", "g6", "g4", "small", "small", "g1", "g6", "g3", "g5",
    "small", "g2", "small", "g6", "g5", "g6", "g4", "g1", "text", "g5", "g6",
)
WAYS = ("both", "both", "both", "both", "both", "both", "both", "both", "both", "both", "both", "both")


class Flows:
    def __init__(self, token):
        self.token = token
        self.flows, self.pending, self.results = {}, {}, {}

    def add(self, name, flow):
        self.flows[name] = flow
        self.pending[name] = next(flow)

    def step(self, *names):
        held = [self.pending[name] for name in names]
        held, self.token = lax.optimization_barrier((held, self.token))
        for name, arrays in zip(names, held):
            self.send(name, arrays)

    def send(self, name, arrays):
        try:
            self.pending[name] = self.flows[name].send(arrays)
        except StopIteration as end:
            self.results[name] = end.value


def shards(
    text_rows,
    vision_rows,
    segment_ids,
    text_keep,
    segment_box,
    patch_keep,
    attn_qkv_a,
    attn_out_a,
    mlp_in_a,
    mlp_out_a,
    norm_gain_a,
    norm_shift_a,
    box_table_a,
    attn_query_b,
    attn_kv_b,
    attn_out_b,
    mlp_in_b,
    mlp_out_b,
    norm_gain_b,
    norm_shift_b,
    box_table_b,
    out_grad,
):
    pages, length, width = text_rows.shape
    patches = vision_rows.shape[1]
    ndp, nt = lax.axis_size("dp"), lax.axis_size("tensor")
    own, mine = lax.axis_index("dp"), lax.axis_index("tensor")
    block = width // ndp
    share = attn_out_a.shape[0]
    tiles = mlp_in_a.shape[1] // share
    nz = ndp // 4
    z_bits = [range(3, ndp.bit_length() - 1), range(2, 3)]
    copies = nt // pages
    direct = nt == 2 and share % LANES == 0

    def swap(values, dp_mask, tensor_mask):
        pairs = [
            (d * nt + t, (d ^ dp_mask) * nt + (t ^ tensor_mask))
            for d in range(ndp)
            for t in range(nt)
        ]
        return lax.ppermute(values, ("dp", "tensor"), pairs)

    def in_order(relative):
        return [
            lax.select_n(mine, *[relative[a ^ m] for m in range(nt)])
            for a in range(nt)
        ]

    def gather_rows(piece, way="both"):
        (piece,) = yield [piece]
        for bits in z_bits:
            for bit in reversed(bits):
                others = [swap(piece, 1 << bit, 0)]
                if bit == bits[0]:
                    others = yield others
                piece = jnp.concatenate([piece, *others], axis=0)
        half = piece.shape[0] // 2
        if not direct or way == "xy":
            (along_x,) = yield [swap(piece, 2, 0)]
            near = jnp.concatenate([piece, along_x], axis=0)
            others = yield [swap(near, 0, j) for j in range(1, nt)]
            plane = jnp.concatenate([near, *others], axis=0)
        elif way == "yx":
            (along_y,) = yield [swap(piece, 0, 1)]
            near = jnp.concatenate([piece, along_y], axis=0)
            (far,) = yield [swap(near, 2, 0)]
            plane = jnp.concatenate([piece, far[: 2 * half], along_y, far[2 * half :]], axis=0)
        else:
            along_x, along_y = yield swap(piece, 2, 0), swap(piece, 0, 1)
            far = yield swap(along_y[:half], 2, 0), swap(along_x[half:], 0, 1)
            plane = jnp.concatenate([piece, along_x, along_y, *far], axis=0)
        plane, core = yield [plane, swap(plane, 1, 0)]
        return plane, core

    def projection(gathered, start, tiles):
        plane, core = gathered
        rows = width // 2
        if direct:
            views = [[(plane, j, rows), (core, j, rows)] for j in range(nt)]
            return Projection(views, share, start, tiles)
        plane, core = (
            array[:, start * share : (start + tiles) * share].reshape(nt, rows, tiles, share)
            for array in gathered
        )
        both = jnp.concatenate([plane, core], axis=1)
        both = jnp.transpose(both, (1, 2, 0, 3)).reshape(width, tiles * width)
        return Projection([[(both, 0, width)]], width, 0, tiles)

    def scatter_rows(count, way="both"):
        sides, others = {}, {}
        for _ in range(2):
            given = yield
            names = list(given)
            sides.update({name: given[name][0] for name in names})
            got = yield [swap(given[name][1], 1, 0) for name in names]
            others.update(zip(names, got))
        products = [
            (sides[p, "left"], others[p, "left"], sides[p, "right"], others[p, "right"])
            for p in range(count)
        ]
        high = width // 2
        rows = high // 2
        half = rows // 2
        if direct:
            cut = (rows, share, half if way == "both" else 0)
            parts = weight_grad(products, 1.0 / copies, cut)
            *far, near_x, near_y, here = parts
            if way == "both":
                from_x, from_y = yield swap(far[0], 2, 0), swap(far[1], 0, 1)
                near_y = jnp.concatenate([near_y[:half] + from_x, near_y[half:]], axis=0)
                near_x = jnp.concatenate([near_x[:half], near_x[half:] + from_y], axis=0)
                from_x, from_y = yield swap(near_x, 2, 0), swap(near_y, 0, 1)
                here = here.astype(f32) + from_x + from_y
            elif way == "xy":
                far, from_x = yield swap(far[0], 2, 0), swap(near_x, 2, 0)
                (from_y,) = yield [swap(near_y + far, 0, 1)]
                here = here.astype(f32) + from_x + from_y
            else:
                far, from_y = yield swap(far[0], 0, 1), swap(near_y, 0, 1)
                (from_x,) = yield [swap(near_x + far, 2, 0)]
                here = here.astype(f32) + from_x + from_y
        else:
            total = weight_grad(products, 1.0 / copies)
            total = total.reshape(2, rows, -1, nt, share)

            def part(x, j):
                return total[x, :, :, j].reshape(rows, -1)

            from_x = yield [swap(part(1, j), 2, 0) for j in range(nt)]
            here = [part(0, j) + from_x[j] for j in range(nt)]
            from_y = yield [swap(here[j], 0, j) for j in range(1, nt)]
            here = sum([got.astype(f32) for got in from_y], here[0].astype(f32))
        for bits in reversed(z_bits):
            for bit in bits:
                here = cast_low(here)
                half = here.shape[0] // 2
                got = [swap(here[half:], 1 << bit, 0)]
                if bit == bits[-1]:
                    got = yield got
                here = here[:half].astype(f32) + got[0]
        return here

    def to_owners(rows):
        cut = rows.shape[0] // nt
        parts = [rows[a * cut : (a + 1) * cut] for a in range(nt)]
        relative = in_order(parts)
        arrived = yield [relative[0]] + [swap(relative[k], 0, k) for k in range(1, nt)]
        return jnp.stack(in_order(arrived)[::copies])

    def page_parts():
        (rows_text, rows_vision, shares, ids, box, kept_text, kept_patch) = yield [
            text_rows, vision_rows, out_grad, segment_ids, segment_box, text_keep, patch_keep
        ]
        place = jnp.arange(width)
        relative = place // (2 * nz * block) + 2 * (place // (nz * block) % 2)
        for bit in range(2, ndp.bit_length() - 1):
            relative = relative + (1 << bit) * (place // (nz * block >> (bit - 1)) % 2)
        feature = (own ^ relative) * block + place % block
        order = cast_low(jnp.arange(width)[:, None] == feature[None, :])
        shares = in_order([shares[a // copies] for a in range(nt)])
        tables = jnp.stack([box_table_a, box_table_b])
        got = yield [
            order,
            [swap(tables, 0, j) for j in range(1, nt)],
            [swap(shares[j], 0, j) for j in range(1, nt)],
        ]
        order, other_tables, other_shares = got
        page = mine // copies

        def of_page(values):
            return lax.dynamic_index_in_dim(values, page, 0, keepdims=False)

        text = cast_low(matmul(of_page(rows_text), order))
        vision = cast_low(matmul(of_page(rows_vision), order))
        text, vision = yield text, vision

        lane = jnp.arange(LANES)
        target = jnp.where(lane < 2 * GRID, lane % GRID, 1)
        select = jnp.stack([lane // GRID == 0, lane // GRID == 1]).astype(f32)
        fill = (lane // 2 == GRID).astype(f32)
        segment_hot = (of_page(ids)[:, None] == jnp.arange(box.shape[1])).astype(f32)
        token_box = matmul(segment_hot, matmul(of_page(box).astype(f32), select) + fill)
        hot = cast_low(token_box == target)
        patch = jnp.arange(patches)[:, None]
        patch_box = jnp.where(lane // GRID == 0, patch % GRID, patch // GRID)
        patch_box = jnp.where(lane < 2 * GRID, patch_box, fill.astype(jnp.int32))
        patch_hot = cast_low(patch_box == target)

        def other_columns(hot, keep):
            kept = (keep > 0).astype(bf16)[:, None]
            score = jnp.where(lane == 2 * GRID, *[jnp.asarray(m, bf16) for m in mask_columns])
            other = hot * jnp.where(lane < 2 * GRID, kept, score * (1 - kept))
            return other, jnp.broadcast_to(kept, other.shape)

        other_a = other_columns(hot, of_page(kept_text))
        other_b = other_columns(patch_hot, of_page(kept_patch))
        tables = jnp.concatenate([tables] + other_tables, axis=1)
        spread = spread_tables(tables.reshape(-1, 2 * RELS))
        hot, turned, other_a, other_b, spread = yield hot, hot.T, other_a, other_b, spread
        grad_in = jnp.concatenate(in_order([shares[0]] + other_shares), axis=0)
        (grad_in,) = yield [cast_low(matmul(grad_in, order))]
        return order, text, vision, grad_in, hot, turned, other_a, other_b, spread

    flows = Flows(text_keep[0, 0])

    norms = jnp.concatenate([norm_gain_a, norm_shift_a, norm_gain_b, norm_shift_b], axis=0)
    norm_columns = jnp.pad(norms.T, ((0, 0), (0, LANES - norms.shape[0])))
    def weights(*pieces):
        return gather_rows(jnp.concatenate(pieces, axis=1))

    for name, way, pieces in (
        ("w1", WAYS[0], (attn_qkv_a.reshape(block, -1), norm_columns)),
        ("w2", WAYS[1], (attn_out_a.T, mlp_in_a)),
        ("w3", WAYS[2], (mlp_out_a.T,)),
        ("w4", WAYS[3], (attn_query_b, attn_kv_b.reshape(block, -1))),
        ("w5", WAYS[4], (attn_out_b.T, mlp_in_b)),
        ("w6", WAYS[5], (mlp_out_b.T,)),
    ):
        flows.add(name, gather_rows(jnp.concatenate(pieces, axis=1), way))
    flows.add("page", page_parts())
    for i, count in enumerate((1, 2, 2, 1, 2, 1)):
        flows.add(f"g{i + 1}", scatter_rows(count, WAYS[6 + i]))
    results = flows.results
    sides = {}
    tables_grads, norm_grads = {}, {}
    high = width // 2

    def chain():
        yield []
        order, text, vision, grad_in, hot, turned, other_a, other_b, spread = results["page"]
        pairs = spread.shape[1] // (4 * LANES)
        sides["g3"] = {(1, "left"): (vision, vision[:, high:])}
        sides["g6"] = {(0, "left"): (text, text[:, high:])}

        at = 3 * share
        gathered = results["w1"]
        norms = jnp.concatenate([part[:high, at : at + 8] for part in gathered], axis=0)
        (norms,) = yield [norms.T.astype(f32)]
        qkv_a = projection(gathered, 0, 3)
        qkv = project(text, qkv_a, "low")
        triple_a = ((qkv, 0), (qkv, 1), (qkv, 2))
        context_a, probs_a = yield attend_forward(*triple_a, hot, (spread, 0), *other_a)
        out_a, in_a = projection(results["w2"], 0, 1), projection(results["w2"], 1, tiles)
        normed_a0, scale_a0, mixed_a, part = project_back(
            context_a[None], out_a, "norm", [text], norms, (0, 2)
        )
        gelu_a, slope_a = yield project(mixed_a, in_a, "gelu")
        sides["g5"] = {
            (0, "right"): (context_a[None], context_a[None]),
            (1, "left"): (mixed_a, part),
        }
        sides["g4"] = {(0, "right"): (gelu_a, gelu_a)}
        back_a = projection(results["w3"], 0, tiles)
        normed_a1, scale_a1, middle, part = yield project_back(
            gelu_a, back_a, "norm", [normed_a0], norms, (1, 3, 0, 2)
        )
        sides["g3"][0, "left"] = (middle, part)

        query_b, kv_b = projection(results["w4"], 0, 1), projection(results["w4"], 1, 2)
        queries_b = project(middle, query_b, "low")
        kv = project(vision, kv_b, "low")
        triple_b = ((queries_b, 0), (kv, 0), (kv, 1))
        context_b, probs_b = yield attend_forward(*triple_b, hot, (spread, pairs), *other_b)
        out_b, in_b = projection(results["w5"], 0, 1), projection(results["w5"], 1, tiles)
        normed_b0, scale_b0, mixed_b, part = project_back(
            context_b[None], out_b, "norm", [normed_a1], norms, (4, 6, 1, 3)
        )
        gelu_b, slope_b = yield project(mixed_b, in_b, "gelu")
        sides["g2"] = {
            (0, "right"): (context_b[None], context_b[None]),
            (1, "left"): (mixed_b, part),
        }
        sides["g1"] = {(0, "right"): (gelu_b, gelu_b)}
        back_b = projection(results["w6"], 0, tiles)
        final, pre, branch, part, norm_grads["b1"] = yield project_back(
            gelu_b, back_b, "final", [normed_b0, grad_in], norms, (5, 7, 4, 6)
        )

        sides["g1"] = {(0, "left"): (branch, part)}
        flows.add("out", to_owners(cast_low(matmul_nt(final, order))))
        (hidden,) = yield [project(branch, back_b, "slope", slope_b)]
        pre, attn_grad, part, norm_grads["b0"] = project_back(
            hidden, in_b, "back", [pre, normed_b0, scale_b0], norms, (4,)
        )
        (context_grad,) = project(attn_grad, out_b, "low")
        pre, attn_grad, part, context_grad = yield pre, attn_grad, part, context_grad
        sides["g2"] = {(0, "left"): (attn_grad, part), (1, "right"): (hidden, hidden)}
        query_grad, kv_grad, sums = yield attend_backward(
            *triple_b, context_grad, probs_b, turned, *other_b
        )
        tables_grads["b"] = sums
        sides["g3"] = {
            (0, "right"): (query_grad, query_grad),
            (1, "right"): (kv_grad, kv_grad),
        }
        pre, branch, part, norm_grads["a1"] = project_back(
            query_grad, query_b, "back", [pre, normed_a1, scale_a1], norms, (1,)
        )
        hidden = project(branch, back_a, "slope", slope_a)
        pre, branch, part, hidden = yield pre, branch, part, hidden
        sides["g4"] = {(0, "left"): (branch, part)}
        vision_grad = project_back(kv_grad, kv_b, "low")
        flows.add("vision", to_owners(cast_low(matmul_nt(vision_grad, order))))
        pre, attn_grad, part, norm_grads["a0"] = project_back(
            hidden, in_a, "back", [pre, normed_a0, scale_a0], norms, (0,)
        )
        (context_grad,) = project(attn_grad, out_a, "low")
        pre, attn_grad, part, context_grad = yield pre, attn_grad, part, context_grad
        sides["g5"] = {(0, "left"): (attn_grad, part), (1, "right"): (hidden, hidden)}
        qkv_grad, sums = yield attend_backward(
            *triple_a, context_grad, probs_a, turned, *other_a
        )
        tables_grads["a"] = sums
        sides["g6"] = {(0, "right"): (qkv_grad, qkv_grad)}
        text_grad = project_back(qkv_grad, qkv_a, "add", [pre])
        flows.add("text", to_owners(cast_low(matmul_nt(text_grad, order))))
        flows.add("small", small_sums(tables_grads["a"], tables_grads["b"]))

    def small_sums(pairs_a, pairs_b):
        norms = jnp.concatenate([norm_grads[i] for i in ("a0", "a1", "b0", "b1")], axis=0)
        norms = jnp.transpose(norms.reshape(8, ndp, block), (1, 0, 2)).reshape(ndp, 8 * block)
        tables = jnp.stack([table_grad(pairs_a), table_grad(pairs_b)])
        heads = pairs_a.shape[0]
        tables = jnp.transpose(tables.reshape(2, nt, heads // nt, 2, RELS), (1, 0, 2, 3, 4))
        tables = tables.reshape(nt, -1)
        size = tables.shape[1]
        tables = jnp.pad(tables, ((0, 0), (0, -size % (8 * block)))).reshape(nt, -1, 8 * block)
        depth = tables.shape[1]
        tables = tables.reshape(nt * depth, 8 * block)
        norms, tables = yield norms * (1.0 / copies), tables * (1.0 / copies)
        for bits in (range(1), range(1, 2), *reversed(z_bits)):
            for bit in bits:
                half = norms.shape[0] // 2
                got = [swap(jnp.concatenate([norms[half:], tables], axis=0), 1 << bit, 0)]
                if bit == bits[-1]:
                    got = yield got
                norms, tables = norms[:half] + got[0][:half], tables + got[0][half:]
        others = yield [
            swap(jnp.concatenate([norms, tables[j * depth : (j + 1) * depth]], axis=0), 0, j)
            for j in range(1, nt)
        ]
        total = sum(others, jnp.concatenate([norms, tables[:depth]], axis=0))
        tables = total[1:].reshape(-1)[:size].reshape(2, heads // nt, 2, RELS)
        return total[0].reshape(8, block), tables

    flows.add("layers", chain())
    for name in ORDER:
        if name.startswith("+"):
            flows.send(name[1:], sides[name[1:]])
        else:
            flows.step(name)
    norm_sums, tables = results["small"]
    tables = tables + (flows.token - text_keep[0, 0]).astype(f32)
    grad_in_a, grad_in_b = results["g5"], results["g2"]
    grad_second = results["g3"]

    return (
        results["out"],
        results["text"].astype(f32),
        results["vision"].astype(f32),
        results["g6"].reshape(block, 3, share),
        grad_in_a[:, :share].T,
        grad_in_a[:, share:],
        results["g4"].T,
        norm_sums[0:4:2],
        norm_sums[1:4:2],
        tables[0],
        grad_second[:, :share],
        grad_second[:, share:].reshape(block, 2, share),
        grad_in_b[:, :share].T,
        grad_in_b[:, share:],
        results["g1"].T,
        norm_sums[4:8:2],
        norm_sums[5:8:2],
        tables[1],
    )


def solution(mesh):
    return jax.shard_map(
        shards,
        mesh=mesh,
        in_specs=(
            P("dp", None, None),
            P("dp", None, None),
            P("dp", None),
            P("dp", None),
            P("dp", None, None),
            P("dp", None),
            P("dp", None, "tensor"),
            P("tensor", "dp"),
            P("dp", "tensor"),
            P("tensor", "dp"),
            P(None, "dp"),
            P(None, "dp"),
            P("tensor", None, None),
            P("dp", "tensor"),
            P("dp", None, "tensor"),
            P("tensor", "dp"),
            P("dp", "tensor"),
            P("tensor", "dp"),
            P(None, "dp"),
            P(None, "dp"),
            P("tensor", None, None),
            P("dp", "tensor", None),
        ),
        out_specs=(
            P("dp", "tensor", None),
            P("dp", "tensor", None),
            P("dp", "tensor", None),
            P("dp", None, "tensor"),
            P("tensor", "dp"),
            P("dp", "tensor"),
            P("tensor", "dp"),
            P(None, "dp"),
            P(None, "dp"),
            P("tensor", None, None),
            P("dp", "tensor"),
            P("dp", None, "tensor"),
            P("tensor", "dp"),
            P("dp", "tensor"),
            P("tensor", "dp"),
            P(None, "dp"),
            P(None, "dp"),
            P("tensor", None, None),
        ),
        check_vma=False,
    )
```

time: 803 us -> 565 us (0.70)
  matrix products: 309 us -> 10.2 us
  Pallas kernels: 0 us -> 153 us
  starting transfers between devices: 150 us -> 96 us
  waiting for transfers between devices: 206 us -> 159 us
    dot_general x38 -> x0, matrix products: 185 us -> none  [the longest x18 41.2 us: matmul_tn(): lax.dot_general(left_side, right_side, (((0,), (0,)), ((), ())), preferre...]
    pallas_call x0 -> x28, Pallas kernels: none -> 153 us  [the longest x9 45 us: project_back(): pl.pallas_call(kernel, grid=(tiles,), in_specs=[tile_of(h)] + weight.spec...]
    dot_general x15 -> x5, matrix products: 80.7 us -> 5.06 us  [matmul(): return jnp.dot(left_side, right_side, preferred_element_type=f32)]
    ppermute x122 -> x106, starting transfers between devices: 150 us -> 96 us  [swap(): return lax.ppermute(values, ('dp', 'tensor'), pairs)]
    ppermute x122 -> x106, waiting for transfers between devices: 206 us -> 159 us  [swap(): return lax.ppermute(values, ('dp', 'tensor'), pairs)]
    dot_general x10 -> x3, matrix products: 40.5 us -> 3.78 us  [matmul_nt(): lax.dot_general(left_side, right_side, (((1,), (1,)), ((), ())), preferre...]
    unnamed x435 -> x377, local copies, waits for them, and re-layouts: 43.5 us -> 51 us
    slice x44 -> x50, local copies, waits for them, and re-layouts: 15.7 us -> 21.1 us  [the longest x12 6.05 us: gather_rows(): far = (yield (swap(along_y[:half], 2, 0), swap(along_x[half:], 0, 1)))]
  transfers between devices with their start and end apart: 122 -> 106, of which waited for: 51 -> 37; matrix products, arithmetic and copies ran while one was open for 27% -> 18% of each run, Pallas kernels for 0% -> 28%
where the time goes in v2:
time: 565 us; the launch traced here: 557 us
  waiting for transfers between devices  159 us (28%)
  Pallas kernels  153 us (27%)
  starting transfers between devices  96 us (17%)
  local copies, waits for them, and re-layouts  93.5 us (17%)
  other arithmetic  39.9 us (7%)
  matrix products  10.2 us (2%)
    ppermute x106, waiting for transfers between devices, swap(): return lax.ppermute(values, ('dp', 'tensor'), pairs)  159 us
    ppermute x106, starting transfers between devices, swap(): return lax.ppermute(values, ('dp', 'tensor'), pairs)  96 us
    unnamed x377, local copies, waits for them, and re-layouts  51 us
    pallas_call x9, Pallas kernels, project_back(): pl.pallas_call(kernel, grid=(tiles,), in_specs=[tile_of(h)] + weight.spec...  45 us
    pallas_call x6, Pallas kernels, weight_grad(): pl.pallas_call(kernel, grid=(tiles,), in_specs=in_specs, out_specs=[colum...  33.5 us
    pallas_call x9, Pallas kernels, project(): pl.pallas_call(kernel, grid=(weight.tiles,), in_specs=[whole(x)] + weight...  33.1 us
    pallas_call x2, Pallas kernels, attend_backward(): pl.pallas_call(kernel, grid=(heads // 2,), in_specs=[pair_of(q, q_role),...  23.7 us
    pallas_call x2, Pallas kernels, attend_forward(): pl.pallas_call(kernel, grid=(heads // 2,), in_specs=[pair_of(q, q_role),...  18 us
  transfers between devices with their start and end apart: 106, of which 37 were waited for; matrix products, arithmetic and copies ran while one was open for 18% of the time, Pallas kernels for 28%

profile of v2, /device:TPU:0, one launch (start us, length us, event | category | flops | bytes accessed | tf_op | source)
XLA Modules:
  0.0 556.6 jit_solution(14666889597336149042)
XLA Ops:
  2.2 3.0 collective-permute-start
  10.1 3.1 collective-permute-start.2
  28.9 4.5 collective-permute-done.3
  42.7 3.4 collective-permute-done.6
  63.5 8.6 %collective-permute-done.11 = bf16[96,1920]{1,0:T(8,128)(2,1)S(1)} collective-permute-done((bf16[96,1920]{1,0:T(8,128)(2,1)S(1)}, bf16[96,1920]{1,0:T(8,128)(2,1)S(1)}, u32[]{:S(2)}, u32[]{:S(2)}) %collective-permute-start.11) | collective-permute-done | bytes 368672 | tf_op jit(solution)/shard_map/ppermute | solution.py:530
  78.5 5.2 collective-permute-done.15
  101.9 6.3 %collective-permute-done.21 = bf16[48,1920]{1,0:T(8,128)(2,1)S(1)} collective-permute-done((bf16[48,1920]{1,0:T(8,128)(2,1)S(1)}, bf16[48,1920]{1,0:T(8,128)(2,1)S(1)}, u32[]{:S(2)}, u32[]{:S(2)}) %collective-permute-start.21) | collective-permute-done | bytes 184352 | tf_op jit(solution)/shard_map/ppermute | solution.py:530
  110.9 5.0 collective-permute-done.18
  131.0 4.5 shard_map.349.q_ref.k_ref.v_ref
  138.3 9.8 %shard_map.350 = (bf16[512,768]{1,0:T(8,128)(2,1)}, bf16[12,512,512]{2,1,0:T(8,128)(2,1)S(1)}) custom-call(bf16[3,512,768]{2,1,0:T(8,128)(2,1)S(1)} %shard_map.349.q_ref.k_ref.v_ref, bf16[3,512,768]{2,1,0:T(8,128)(2,1)S(1)} %shard_map.349.q_ref.k_ref.v_ref, bf16[3,512,768]{2,1,0:T(8,128)(2,1)S(1)} %shard_map.349.q_ref.k_ref.v_ref, ...), custom_call_target="tpu_custom_call" | custom-call | flops 3221225472 | bytes 6291456 | tf_op jit(solution)/shard_map/pallas_call | solution.py:353
  148.2 2.7 copy-done.121
  150.9 3.9 shard_map.351
  154.8 5.9 %shard_map.352 = (bf16[4,512,768]{2,1,0:T(8,128)(2,1)S(1)}, bf16[4,512,768]{2,1,0:T(8,128)(2,1)S(1)}) custom-call(bf16[512,768]{1,0:T(8,128)(2,1)S(1)} %get-tuple-element.443.x_ref.refs_4_, bf16[768,1920]{1,0:T(8,128)(2,1)S(1)} %constant_dynamic-update-slice_fusion.16.refs_0_.refs_2_, bf16[768,1920]{1,0:T(8,128)(2,1)S(1)} %collective-permute-done.22.refs_1_.refs_3_, ...), custom_call_target="tpu_custom_call" | custom-call | flops 2415919104 | bytes 11010048 | tf_op jit(solution)/shard_map/pallas_call | solution.py:131
  165.4 5.0 collective-permute-done.32
  174.8 6.5 %shard_map.353 = (f32[512,768]{1,0:T(8,128)S(1)}, f32[512,1]{1,0:T(8,128)S(1)}, bf16[512,768]{1,0:T(8,128)(2,1)S(1)}, bf16[512,384]{1,0:T(8,128)(2,1)S(1)}) custom-call(bf16[4,512,768]{2,1,0:T(8,128)(2,1)S(1)} %get-tuple-element.454.h_ref.refs_2_, bf16[768,1536]{1,0:T(8,128)(2,1)} %constant_dynamic-update-slice_fusion.26.refs_0_.refs_2_, ...), custom_call_target="tpu_custom_call" | custom-call | flops 2415919104 | bytes 12582912 | tf_op jit(solution)/shard_map/pallas_call | solution.py:235
  181.3 9.6 %collective-permute-done.35 = bf16[192,1920]{1,0:T(8,128)(2,1)S(1)} collective-permute-done((bf16[192,1920]{1,0:T(8,128)(2,1)S(1)}, bf16[192,1920]{1,0:T(8,128)(2,1)S(1)}, u32[]{:S(2)}, u32[]{:S(2)}) %collective-permute-start.35) | collective-permute-done | bytes 737312 | tf_op jit(solution)/shard_map/ppermute | solution.py:530
  195.9 5.3 collective-permute-done.39
  204.5 14.0 %collective-permute-done.37 = bf16[192,1536]{1,0:T(8,128)(2,1)S(1)} collective-permute-done((bf16[192,1536]{1,0:T(8,128)(2,1)S(1)}, bf16[192,1536]{1,0:T(8,128)(2,1)S(1)}, u32[]{:S(2)}, u32[]{:S(2)}) %collective-permute-start.37) | collective-permute-done | bytes 589856 | tf_op jit(solution)/shard_map/ppermute | solution.py:530
  221.7 5.5 collective-permute-done.42
  231.2 8.2 %shard_map.356 = (bf16[512,768]{1,0:T(8,128)(2,1)S(1)}, bf16[12,512,256]{2,1,0:T(8,128)(2,1)S(1)}) custom-call(bf16[1,512,768]{2,1,0:T(8,128)(2,1)S(1)} %shard_map.354.q_ref, bf16[2,256,768]{2,1,0:T(8,128)(2,1)S(1)} %shard_map.355.k_ref.v_ref, bf16[2,256,768]{2,1,0:T(8,128)(2,1)S(1)} %shard_map.355.k_ref.v_ref, bf16[512,128]{1,0:T(8,128)(2,1)S(1)} %copy-done.89, ...), custom_call_target="tpu_custom_call" | custom-call | flops 1610612736 | bytes 3145728 | tf_op jit(solution)/shard_map/pallas_call | solution.py:353
  242.8 5.9 %shard_map.358 = (bf16[4,512,768]{2,1,0:T(8,128)(2,1)S(1)}, bf16[4,512,768]{2,1,0:T(8,128)(2,1)S(1)}) custom-call(bf16[512,768]{1,0:T(8,128)(2,1)S(1)} %get-tuple-element.498.x_ref.refs_4_, bf16[768,1920]{1,0:T(8,128)(2,1)S(1)} %constant_dynamic-update-slice_fusion.46.refs_0_.refs_2_, bf16[768,1920]{1,0:T(8,128)(2,1)S(1)} %collective-permute-done.44.refs_1_.refs_3_, ...), custom_call_target="tpu_custom_call" | custom-call | flops 2415919104 | bytes 11010048 | tf_op jit(solution)/shard_map/pallas_call | solution.py:131
  249.2 6.5 %shard_map.359 = (bf16[512,768]{1,0:T(8,128)(2,1)S(1)}, f32[512,768]{1,0:T(8,128)S(1)}, bf16[512,768]{1,0:T(8,128)(2,1)S(1)}, bf16[512,384]{1,0:T(8,128)(2,1)S(1)}, f32[2,768]{1,0:T(2,128)S(1)}) custom-call(bf16[4,512,768]{2,1,0:T(8,128)(2,1)S(1)} %get-tuple-element.505.h_ref.refs_2_, ...), custom_call_target="tpu_custom_call" | custom-call | flops 2415919104 | bytes 12582912 | tf_op jit(solution)/shard_map/pallas_call | solution.py:235
  256.9 5.4 shard_map.360.h_ref.refs_6_
  274.1 7.7 %shard_map.361 = (f32[512,768]{1,0:T(8,128)S(1)}, bf16[512,768]{1,0:T(8,128)(2,1)S(1)}, bf16[512,384]{1,0:T(8,128)(2,1)}, f32[2,768]{1,0:T(2,128)S(1)}) custom-call(bf16[4,512,768]{2,1,0:T(8,128)(2,1)} %shard_map.360.h_ref.refs_6_, bf16[768,1920]{1,0:T(8,128)(2,1)S(1)} %copy-done.3, bf16[768,1920]{1,0:T(8,128)(2,1)S(1)} %copy-done.8, ...), custom_call_target="tpu_custom_call" | custom-call | flops 2415919104 | bytes 12582912 | tf_op jit(solution)/shard_map/pallas_call | solution.py:235
  284.9 9.5 %shard_map.363 = (bf16[1,512,768]{2,1,0:T(8,128)(2,1)}, bf16[2,256,768]{2,1,0:T(8,128)(2,1)}, f32[12,128,128]{2,1,0:T(8,128)S(1)}) custom-call(bf16[1,512,768]{2,1,0:T(8,128)(2,1)S(1)} %copy-done.59, bf16[2,256,768]{2,1,0:T(8,128)(2,1)S(1)} %copy-done.64, bf16[2,256,768]{2,1,0:T(8,128)(2,1)S(1)} %copy-done.64, bf16[512,768]{1,0:T(8,128)(2,1)S(1)} %bitcast.142, ...), custom_call_target="tpu_custom_call" | custom-call | flops 4026531840 | bytes 3145728 | tf_op jit(solution)/shard_map/pallas_call | solution.py:433
  297.0 3.6 shard_map.364
  300.6 6.8 %shard_map.365.h_ref.refs_6_ = bf16[4,512,768]{2,1,0:T(8,128)(2,1)} custom-call(bf16[512,768]{1,0:T(8,128)(2,1)S(1)} %get-tuple-element.621.x_ref.refs_0_, bf16[768,1536]{1,0:T(8,128)(2,1)} %constant_dynamic-update-slice_fusion.26.refs_0_.refs_2_, bf16[768,1536]{1,0:T(8,128)(2,1)S(1)} %copy-done.16, ...), custom_call_target="tpu_custom_call" | custom-call | flops 2415919104 | bytes 11010048 | tf_op jit(solution)/shard_map/pallas_call | solution.py:131
  317.8 3.8 shard_map.370
  324.3 7.6 %shard_map.368 = (f32[512,768]{1,0:T(8,128)S(1)}, bf16[512,768]{1,0:T(8,128)(2,1)S(1)}, bf16[512,384]{1,0:T(8,128)(2,1)}, f32[2,768]{1,0:T(2,128)S(1)}) custom-call(bf16[4,512,768]{2,1,0:T(8,128)(2,1)} %shard_map.365.h_ref.refs_6_, bf16[768,1920]{1,0:T(8,128)(2,1)S(1)} %constant_dynamic-update-slice_fusion.16.refs_0_.refs_2_, ...), custom_call_target="tpu_custom_call" | custom-call | flops 2415919104 | bytes 12582912 | tf_op jit(solution)/shard_map/pallas_call | solution.py:235
  344.9 7.2 %shard_map.366 = (bf16[96,1920]{1,0:T(8,128)(2,1)S(1)}, bf16[96,1920]{1,0:T(8,128)(2,1)S(1)}, bf16[192,1920]{1,0:T(8,128)(2,1)S(1)}, bf16[192,1920]{1,0:T(8,128)(2,1)S(1)}, bf16[192,1920]{1,0:T(8,128)(2,1)S(1)}) custom-call(bf16[512,768]{1,0:T(8,128)(2,1)S(1)} %copy-done.57, bf16[512,384]{1,0:T(8,128)(2,1)} %collective-permute-done.48.refs_1_, ...), custom_call_target="tpu_custom_call" | custom-call | flops 3019898880 | bytes 12386304 | tf_op jit(solution)/shard_map/pallas_call | solution.py:308
  354.5 4.7 shard_map.367
  361.2 14.2 %shard_map.371 = (bf16[3,512,768]{2,1,0:T(8,128)(2,1)}, f32[12,128,128]{2,1,0:T(8,128)S(1)}) custom-call(bf16[3,512,768]{2,1,0:T(8,128)(2,1)S(1)} %copy-done.37, bf16[3,512,768]{2,1,0:T(8,128)(2,1)S(1)} %copy-done.37, bf16[3,512,768]{2,1,0:T(8,128)(2,1)S(1)} %copy-done.37, bf16[512,768]{1,0:T(8,128)(2,1)S(1)} %bitcast.141, ...), custom_call_target="tpu_custom_call" | custom-call | flops 8053063680 | bytes 6291456 | tf_op jit(solution)/shard_map/pallas_call | solution.py:433
  377.7 5.3 shard_map.373
  388.4 6.2 %collective-permute-done.56 = bf16[96,1920]{1,0:T(8,128)(2,1)S(1)} collective-permute-done((bf16[96,1920]{1,0:T(8,128)(2,1)S(1)}, bf16[96,1920]{1,0:T(8,128)(2,1)S(1)}, u32[]{:S(2)}, u32[]{:S(2)}) %collective-permute-start.56) | collective-permute-done | bytes 368672 | tf_op jit(solution)/shard_map/ppermute | solution.py:530
  399.7 5.7 %collective-permute-done.67 = bf16[192,1536]{1,0:T(8,128)(2,1)S(1)} collective-permute-done((bf16[192,1536]{1,0:T(8,128)(2,1)S(1)}, bf16[192,1536]{1,0:T(8,128)(2,1)S(1)}, u32[]{:S(2)}, u32[]{:S(2)}) %collective-permute-start.67) | collective-permute-done | bytes 589856 | tf_op jit(solution)/shard_map/ppermute | solution.py:530
  414.6 5.1 shard_map.372
  426.2 5.2 collective-permute-done.78
  433.6 5.3 collective-permute-done.75
  439.7 6.7 %collective-permute-done.76 = bf16[192,1920]{1,0:T(8,128)(2,1)S(1)} collective-permute-done((bf16[192,1920]{1,0:T(8,128)(2,1)S(1)}, bf16[192,1920]{1,0:T(8,128)(2,1)S(1)}, u32[]{:S(2)}, u32[]{:S(2)}) %collective-permute-start.76) | collective-permute-done | bytes 737312 | tf_op jit(solution)/shard_map/ppermute | solution.py:530
  449.9 8.1 %shard_map.375 = (bf16[96,1920]{1,0:T(8,128)(2,1)S(1)}, bf16[96,1920]{1,0:T(8,128)(2,1)S(1)}, bf16[192,1920]{1,0:T(8,128)(2,1)S(1)}, bf16[192,1920]{1,0:T(8,128)(2,1)S(1)}, bf16[192,1920]{1,0:T(8,128)(2,1)S(1)}) custom-call(bf16[512,768]{1,0:T(8,128)(2,1)S(1)} %copy-done.53, bf16[512,384]{1,0:T(8,128)(2,1)} %collective-permute-done.70.refs_1_, ...), custom_call_target="tpu_custom_call" | custom-call | flops 3019898880 | bytes 12386304 | tf_op jit(solution)/shard_map/pallas_call | solution.py:308
  465.3 5.4 collective-permute-done.87
  474.8 5.3 collective-permute-done.85
  482.5 4.3 shard_map.376
  489.4 5.8 %collective-permute-done.92 = bf16[96,1152]{1,0:T(8,128)(2,1)S(1)} collective-permute-done((bf16[96,1152]{1,0:T(8,128)(2,1)S(1)}, bf16[96,1152]{1,0:T(8,128)(2,1)S(1)}, u32[]{:S(2)}, u32[]{:S(2)}) %collective-permute-start.92) | collective-permute-done | bytes 221216 | tf_op jit(solution)/shard_map/ppermute | solution.py:530
  497.7 3.6 collective-permute-done.93
  509.1 5.4 collective-permute-done.101
  522.6 11.7 %collective-permute-done.103 = bf16[96,1920]{1,0:T(8,128)(2,1)S(1)} collective-permute-done((bf16[96,1920]{1,0:T(8,128)(2,1)}, bf16[96,1920]{1,0:T(8,128)(2,1)S(1)}, u32[]{:S(2)}, u32[]{:S(2)}) %collective-permute-start.103) | collective-permute-done | bytes 368672 | tf_op jit(solution)/shard_map/ppermute | solution.py:530
  538.2 7.0 %collective-permute-done.105 = bf16[48,1920]{1,0:T(8,128)(2,1)S(1)} collective-permute-done((bf16[48,1920]{1,0:T(8,128)(2,1)S(1)}, bf16[48,1920]{1,0:T(8,128)(2,1)S(1)}, u32[]{:S(2)}, u32[]{:S(2)}) %collective-permute-start.105) | collective-permute-done | bytes 184352 | tf_op jit(solution)/shard_map/ppermute | solution.py:530
  (776 shorter events, 252.5 us)
Async XLA Ops:
  2.2 26.8 %collective-permute-start = (bf16[2,6,2,31]{3,2,1,0:T(2,128)(2,1)}, bf16[2,6,2,31]{3,2,1,0:T(2,128)(2,1)}, u32[]{:S(2)}, u32[]{:S(2)}) collective-permute-start(bf16[2,6,2,31]{3,2,1,0:T(2,128)(2,1)} %pad_maximum_fusion.30), channel_id=1, source_target_pairs={{0,1},{1,0},{2,3},{3,2},{4,5},{5,4},{6,7},{7,6},{8,9},{9,8},{10,11... | collective-permute-start | bytes 4472 | tf_op jit(solution)/shard_map/ppermute | solution.py:530
  10.1 18.8 %collective-permute-start.1 = (bf16[256,768]{1,0:T(8,128)(2,1)}, bf16[256,768]{1,0:T(8,128)(2,1)}, u32[]{:S(2)}, u32[]{:S(2)}) collective-permute-start(bf16[256,768]{1,0:T(8,128)(2,1)} %select_bitcast_fusion.4), channel_id=1, source_target_pairs={{0,1},{1,0},{2,3},{3,2},{4,5},{5,4},{6,7},{7,6},{8,9},{9,8},{10,11... | collective-permute-start | bytes 1179656 | tf_op jit(solution)/shard_map/ppermute | solution.py:530
  57.1 21.4 %collective-permute-start.10 = (bf16[768,1280]{1,0:T(8,128)(2,1)}, bf16[768,1280]{1,0:T(8,128)(2,1)S(1)}, u32[]{:S(2)}, u32[]{:S(2)}) collective-permute-start(bf16[768,1280]{1,0:T(8,128)(2,1)} %constant_dynamic-update-slice_fusion.3.refs_0_.refs_2_), channel_id=1, source_target_pairs={{0,2},{1,3},{2,0},{3,1},{4,6},{5,7},{6,4},{7,5},{8,10},{9,11},{10,... | collective-permute-start | bytes 5898248 | tf_op jit(solution)/shard_map/ppermute | solution.py:530
  63.0 21.3 %collective-permute-start.14 = (bf16[96,1536]{1,0:T(8,128)(2,1)S(1)}, bf16[96,1536]{1,0:T(8,128)(2,1)S(1)}, u32[]{:S(2)}, u32[]{:S(2)}) collective-permute-start(bf16[96,1536]{1,0:T(8,128)(2,1)S(1)} %pad_maximum_fusion.15), channel_id=1, source_target_pairs={{0,8},{1,9},{2,10},{3,11},{4,12},{5,13},{6,14},{7,15},{8,0},{9,1},... | collective-permute-start | bytes 884744 | tf_op jit(solution)/shard_map/ppermute | solution.py:530
  72.9 19.7 %collective-permute-start.12 = (bf16[192,1920]{1,0:T(8,128)(2,1)}, bf16[192,1920]{1,0:T(8,128)(2,1)}, u32[]{:S(2)}, u32[]{:S(2)}) collective-permute-start(bf16[192,1920]{1,0:T(8,128)(2,1)} %get-tuple-element.812), channel_id=1, source_target_pairs={{0,4},{1,5},{2,6},{3,7},{4,0},{5,1},{6,2},{7,3},{8,12},{9,13},{10,... | collective-permute-start | bytes 2211848 | tf_op jit(solution)/shard_map/ppermute | solution.py:530
  74.4 19.7 %collective-permute-start.13 = (bf16[192,1920]{1,0:T(8,128)(2,1)}, bf16[192,1920]{1,0:T(8,128)(2,1)}, u32[]{:S(2)}, u32[]{:S(2)}) collective-permute-start(bf16[192,1920]{1,0:T(8,128)(2,1)} %get-tuple-element.812), channel_id=1, source_target_pairs={{0,1},{1,0},{2,3},{3,2},{4,5},{5,4},{6,7},{7,6},{8,9},{9,8},{10,11... | collective-permute-start | bytes 2211848 | tf_op jit(solution)/shard_map/ppermute | solution.py:530
  85.2 25.6 %collective-permute-start.19 = (bf16[192,1536]{1,0:T(8,128)(2,1)}, bf16[192,1536]{1,0:T(8,128)(2,1)}, u32[]{:S(2)}, u32[]{:S(2)}) collective-permute-start(bf16[192,1536]{1,0:T(8,128)(2,1)} %get-tuple-element.817), channel_id=1, source_target_pairs={{0,4},{1,5},{2,6},{3,7},{4,0},{5,1},{6,2},{7,3},{8,12},{9,13},{10,... | collective-permute-start | bytes 1769480 | tf_op jit(solution)/shard_map/ppermute | solution.py:530
  86.2 24.7 %collective-permute-start.20 = (bf16[192,1536]{1,0:T(8,128)(2,1)}, bf16[192,1536]{1,0:T(8,128)(2,1)}, u32[]{:S(2)}, u32[]{:S(2)}) collective-permute-start(bf16[192,1536]{1,0:T(8,128)(2,1)} %get-tuple-element.817), channel_id=1, source_target_pairs={{0,1},{1,0},{2,3},{3,2},{4,5},{5,4},{6,7},{7,6},{8,9},{9,8},{10,11... | collective-permute-start | bytes 1769480 | tf_op jit(solution)/shard_map/ppermute | solution.py:530
  116.0 34.8 %collective-permute-start.22 = (bf16[768,1920]{1,0:T(8,128)(2,1)S(1)}, bf16[768,1920]{1,0:T(8,128)(2,1)S(1)}, u32[]{:S(2)}, u32[]{:S(2)}) collective-permute-start(bf16[768,1920]{1,0:T(8,128)(2,1)S(1)} %constant_dynamic-update-slice_fusion.16.refs_0_.refs_2_), channel_id=1, source_target_pairs={{0,2},{1,3},{2,0},{3,1},{4,6},{5,7},{6,4},{7,5},{8,10},{9,11},{10,... | collective-permute-start | bytes 8847368 | tf_op jit(solution)/shard_map/ppermute | solution.py:530
  130.2 20.6 %collective-permute-start.30 = (bf16[768,1536]{1,0:T(8,128)(2,1)}, bf16[768,1536]{1,0:T(8,128)(2,1)S(1)}, u32[]{:S(2)}, u32[]{:S(2)}) collective-permute-start(bf16[768,1536]{1,0:T(8,128)(2,1)} %constant_dynamic-update-slice_fusion.26.refs_0_.refs_2_), channel_id=1, source_target_pairs={{0,2},{1,3},{2,0},{3,1},{4,6},{5,7},{6,4},{7,5},{8,10},{9,11},{10,... | collective-permute-start | bytes 7077896 | tf_op jit(solution)/shard_map/ppermute | solution.py:530
  135.6 26.8 %collective-permute-start.27 = (bf16[192,1152]{1,0:T(8,128)(2,1)S(1)}, bf16[192,1152]{1,0:T(8,128)(2,1)S(1)}, u32[]{:S(2)}, u32[]{:S(2)}) collective-permute-start(bf16[192,1152]{1,0:T(8,128)(2,1)S(1)} %get-tuple-element.821), channel_id=1, source_target_pairs={{0,4},{1,5},{2,6},{3,7},{4,0},{5,1},{6,2},{7,3},{8,12},{9,13},{10,... | collective-permute-start | bytes 1327112 | tf_op jit(solution)/shard_map/ppermute | solution.py:530
  136.2 26.1 %collective-permute-start.28 = (bf16[192,1152]{1,0:T(8,128)(2,1)S(1)}, bf16[192,1152]{1,0:T(8,128)(2,1)S(1)}, u32[]{:S(2)}, u32[]{:S(2)}) collective-permute-start(bf16[192,1152]{1,0:T(8,128)(2,1)S(1)} %get-tuple-element.821), channel_id=1, source_target_pairs={{0,1},{1,0},{2,3},{3,2},{4,5},{5,4},{6,7},{7,6},{8,9},{9,8},{10,11... | collective-permute-start | bytes 1327112 | tf_op jit(solution)/shard_map/ppermute | solution.py:530
  162.4 31.9 %collective-permute-start.41 = (bf16[4,512,768]{2,1,0:T(8,128)(2,1)S(1)}, bf16[4,512,768]{2,1,0:T(8,128)(2,1)S(1)}, u32[]{:S(2)}, u32[]{:S(2)}) collective-permute-start(bf16[4,512,768]{2,1,0:T(8,128)(2,1)S(1)} %get-tuple-element.454.h_ref.refs_2_), channel_id=1, source_target_pairs={{0,2},{1,3},{2,0},{3,1},{4,6},{5,7},{6,4},{7,5},{8,10},{9,11},{10,... | collective-permute-start | bytes 9437192 | tf_op jit(solution)/shard_map/ppermute | solution.py:530
  171.7 22.5 %collective-permute-start.34 = (bf16[768,1152]{1,0:T(8,128)(2,1)S(1)}, bf16[768,1152]{1,0:T(8,128)(2,1)S(1)}, u32[]{:S(2)}, u32[]{:S(2)}) collective-permute-start(bf16[768,1152]{1,0:T(8,128)(2,1)S(1)} %constant_dynamic-update-slice_fusion.33.refs_0_.refs_2_), channel_id=1, source_target_pairs={{0,2},{1,3},{2,0},{3,1},{4,6},{5,7},{6,4},{7,5},{8,10},{9,11},{10,... | collective-permute-start | bytes 5308424 | tf_op jit(solution)/shard_map/ppermute | solution.py:530
  172.0 18.9 %collective-permute-start.35 = (bf16[192,1920]{1,0:T(8,128)(2,1)S(1)}, bf16[192,1920]{1,0:T(8,128)(2,1)S(1)}, u32[]{:S(2)}, u32[]{:S(2)}) collective-permute-start(bf16[192,1920]{1,0:T(8,128)(2,1)S(1)} %get-tuple-element.811), channel_id=1, source_target_pairs={{0,4},{1,5},{2,6},{3,7},{4,0},{5,1},{6,2},{7,3},{8,12},{9,13},{10,... | collective-permute-start | bytes 2211848 | tf_op jit(solution)/shard_map/ppermute | solution.py:530
  172.6 18.6 %collective-permute-start.36 = (bf16[192,1920]{1,0:T(8,128)(2,1)S(1)}, bf16[192,1920]{1,0:T(8,128)(2,1)S(1)}, u32[]{:S(2)}, u32[]{:S(2)}) collective-permute-start(bf16[192,1920]{1,0:T(8,128)(2,1)S(1)} %get-tuple-element.811), channel_id=1, source_target_pairs={{0,1},{1,0},{2,3},{3,2},{4,5},{5,4},{6,7},{7,6},{8,9},{9,8},{10,11... | collective-permute-start | bytes 2211848 | tf_op jit(solution)/shard_map/ppermute | solution.py:530
  173.8 20.4 %collective-permute-start.31 = (bf16[96,1536]{1,0:T(8,128)(2,1)S(1)}, bf16[96,1536]{1,0:T(8,128)(2,1)S(1)}, u32[]{:S(2)}, u32[]{:S(2)}) collective-permute-start(bf16[96,1536]{1,0:T(8,128)(2,1)S(1)} %pad_maximum_fusion.16), channel_id=1, source_target_pairs={{0,8},{1,9},{2,10},{3,11},{4,12},{5,13},{6,14},{7,15},{8,0},{9,1},... | collective-permute-start | bytes 884744 | tf_op jit(solution)/shard_map/ppermute | solution.py:530
  202.5 19.1 %collective-permute-start.44 = (bf16[768,1920]{1,0:T(8,128)(2,1)S(1)}, bf16[768,1920]{1,0:T(8,128)(2,1)S(1)}, u32[]{:S(2)}, u32[]{:S(2)}) collective-permute-start(bf16[768,1920]{1,0:T(8,128)(2,1)S(1)} %constant_dynamic-update-slice_fusion.46.refs_0_.refs_2_), channel_id=1, source_target_pairs={{0,2},{1,3},{2,0},{3,1},{4,6},{5,7},{6,4},{7,5},{8,10},{9,11},{10,... | collective-permute-start | bytes 8847368 | tf_op jit(solution)/shard_map/ppermute | solution.py:530
  228.5 20.1 %collective-permute-start.45 = (bf16[768,1536]{1,0:T(8,128)(2,1)S(1)}, bf16[768,1536]{1,0:T(8,128)(2,1)S(1)}, u32[]{:S(2)}, u32[]{:S(2)}) collective-permute-start(bf16[768,1536]{1,0:T(8,128)(2,1)S(1)} %constant_dynamic-update-slice_fusion.53.refs_0_.refs_2_), channel_id=1, source_target_pairs={{0,2},{1,3},{2,0},{3,1},{4,6},{5,7},{6,4},{7,5},{8,10},{9,11},{10,... | collective-permute-start | bytes 7077896 | tf_op jit(solution)/shard_map/ppermute | solution.py:530
  264.0 70.0 %collective-permute-start.49 = (bf16[4,512,768]{2,1,0:T(8,128)(2,1)}, bf16[4,512,768]{2,1,0:T(8,128)(2,1)}, u32[]{:S(2)}, u32[]{:S(2)}) collective-permute-start(bf16[4,512,768]{2,1,0:T(8,128)(2,1)} %shard_map.360.h_ref.refs_6_), channel_id=1, source_target_pairs={{0,2},{1,3},{2,0},{3,1},{4,6},{5,7},{6,4},{7,5},{8,10},{9,11},{10,... | collective-permute-start | bytes 9437192 | tf_op jit(solution)/shard_map/ppermute | solution.py:530
  264.7 31.0 %collective-permute-start.51 = (bf16[256,384]{1,0:T(8,128)(2,1)}, bf16[256,384]{1,0:T(8,128)(2,1)}, u32[]{:S(2)}, u32[]{:S(2)}) collective-permute-start(bf16[256,384]{1,0:T(8,128)(2,1)} %slice.359), channel_id=1, source_target_pairs={{0,2},{1,3},{2,0},{3,1},{4,6},{5,7},{6,4},{7,5},{8,10},{9,11},{10,... | collective-permute-start | bytes 589832 | tf_op jit(solution)/shard_map/ppermute | solution.py:530
  266.9 28.9 %collective-permute-start.52 = (bf16[512,384]{1,0:T(8,128)(2,1)}, bf16[512,384]{1,0:T(8,128)(2,1)S(1)}, u32[]{:S(2)}, u32[]{:S(2)}) collective-permute-start(bf16[512,384]{1,0:T(8,128)(2,1)} %copy-done.105), channel_id=1, source_target_pairs={{0,2},{1,3},{2,0},{3,1},{4,6},{5,7},{6,4},{7,5},{8,10},{9,11},{10,... | collective-permute-start | bytes 1179656 | tf_op jit(solution)/shard_map/ppermute | solution.py:530
  266.9 27.4 %collective-permute-start.53 = (bf16[1,512,768]{2,1,0:T(8,128)(2,1)}, bf16[1,512,768]{2,1,0:T(8,128)(2,1)S(1)}, u32[]{:S(2)}, u32[]{:S(2)}) collective-permute-start(bf16[1,512,768]{2,1,0:T(8,128)(2,1)} %bitcast.144), channel_id=1, source_target_pairs={{0,2},{1,3},{2,0},{3,1},{4,6},{5,7},{6,4},{7,5},{8,10},{9,11},{10,... | collective-permute-start | bytes 2359304 | tf_op jit(solution)/shard_map/ppermute | solution.py:530
  283.1 24.3 %collective-permute-start.50 = (bf16[512,384]{1,0:T(8,128)(2,1)S(1)}, bf16[512,384]{1,0:T(8,128)(2,1)S(1)}, u32[]{:S(2)}, u32[]{:S(2)}) collective-permute-start(bf16[512,384]{1,0:T(8,128)(2,1)S(1)} %copy-done.109), channel_id=1, source_target_pairs={{0,2},{1,3},{2,0},{3,1},{4,6},{5,7},{6,4},{7,5},{8,10},{9,11},{10,... | collective-permute-start | bytes 1179656 | tf_op jit(solution)/shard_map/ppermute | solution.py:530
  295.2 47.9 %collective-permute-start.59 = (bf16[1,512,768]{2,1,0:T(8,128)(2,1)}, bf16[1,512,768]{2,1,0:T(8,128)(2,1)}, u32[]{:S(2)}, u32[]{:S(2)}) collective-permute-start(bf16[1,512,768]{2,1,0:T(8,128)(2,1)} %bitcast.18.h_ref.refs_2_), channel_id=1, source_target_pairs={{0,2},{1,3},{2,0},{3,1},{4,6},{5,7},{6,4},{7,5},{8,10},{9,11},{10,... | collective-permute-start | bytes 2359304 | tf_op jit(solution)/shard_map/ppermute | solution.py:530
  295.8 28.0 %collective-permute-start.48 = (bf16[512,384]{1,0:T(8,128)(2,1)}, bf16[512,384]{1,0:T(8,128)(2,1)}, u32[]{:S(2)}, u32[]{:S(2)}) collective-permute-start(bf16[512,384]{1,0:T(8,128)(2,1)} %get-tuple-element.529), channel_id=1, source_target_pairs={{0,2},{1,3},{2,0},{3,1},{4,6},{5,7},{6,4},{7,5},{8,10},{9,11},{10,... | collective-permute-start | bytes 1179656 | tf_op jit(solution)/shard_map/ppermute | solution.py:530
  296.5 46.8 %collective-permute-start.57 = (bf16[1,512,768]{2,1,0:T(8,128)(2,1)}, bf16[1,512,768]{2,1,0:T(8,128)(2,1)}, u32[]{:S(2)}, u32[]{:S(2)}) collective-permute-start(bf16[1,512,768]{2,1,0:T(8,128)(2,1)} %get-tuple-element.542.h_ref.refs_2_), channel_id=1, source_target_pairs={{0,2},{1,3},{2,0},{3,1},{4,6},{5,7},{6,4},{7,5},{8,10},{9,11},{10,... | collective-permute-start | bytes 2359304 | tf_op jit(solution)/shard_map/ppermute | solution.py:530
  308.2 35.7 %collective-permute-start.58 = (bf16[2,256,768]{2,1,0:T(8,128)(2,1)}, bf16[2,256,768]{2,1,0:T(8,128)(2,1)}, u32[]{:S(2)}, u32[]{:S(2)}) collective-permute-start(bf16[2,256,768]{2,1,0:T(8,128)(2,1)} %get-tuple-element.559.refs_6_.h_ref), channel_id=1, source_target_pairs={{0,2},{1,3},{2,0},{3,1},{4,6},{5,7},{6,4},{7,5},{8,10},{9,11},{10,... | collective-permute-start | bytes 2359304 | tf_op jit(solution)/shard_map/ppermute | solution.py:530
  323.8 18.1 %collective-permute-start.60 = (bf16[512,384]{1,0:T(8,128)(2,1)}, bf16[512,384]{1,0:T(8,128)(2,1)}, u32[]{:S(2)}, u32[]{:S(2)}) collective-permute-start(bf16[512,384]{1,0:T(8,128)(2,1)} %get-tuple-element.560), channel_id=1, source_target_pairs={{0,2},{1,3},{2,0},{3,1},{4,6},{5,7},{6,4},{7,5},{8,10},{9,11},{10,... | collective-permute-start | bytes 1179656 | tf_op jit(solution)/shard_map/ppermute | solution.py:530
  334.0 19.0 %collective-permute-start.65 = (bf16[512,384]{1,0:T(8,128)(2,1)}, bf16[512,384]{1,0:T(8,128)(2,1)}, u32[]{:S(2)}, u32[]{:S(2)}) collective-permute-start(bf16[512,384]{1,0:T(8,128)(2,1)} %get-tuple-element.578), channel_id=1, source_target_pairs={{0,2},{1,3},{2,0},{3,1},{4,6},{5,7},{6,4},{7,5},{8,10},{9,11},{10,... | collective-permute-start | bytes 1179656 | tf_op jit(solution)/shard_map/ppermute | solution.py:530
  341.9 52.8 %collective-permute-start.46 = (bf16[256,768]{1,0:T(8,128)(2,1)S(1)}, bf16[256,768]{1,0:T(8,128)(2,1)S(1)}, u32[]{:S(2)}, u32[]{:S(2)}) collective-permute-start(bf16[256,768]{1,0:T(8,128)(2,1)S(1)} %copy-done.147), channel_id=1, source_target_pairs={{0,1},{1,0},{2,3},{3,2},{4,5},{5,4},{6,7},{7,6},{8,9},{9,8},{10,11... | collective-permute-start | bytes 1179656 | tf_op jit(solution)/shard_map/ppermute | solution.py:530
  343.1 104.4 %collective-permute-start.71 = (bf16[4,512,768]{2,1,0:T(8,128)(2,1)}, bf16[4,512,768]{2,1,0:T(8,128)(2,1)}, u32[]{:S(2)}, u32[]{:S(2)}) collective-permute-start(bf16[4,512,768]{2,1,0:T(8,128)(2,1)} %shard_map.365.h_ref.refs_6_), channel_id=1, source_target_pairs={{0,2},{1,3},{2,0},{3,1},{4,6},{5,7},{6,4},{7,5},{8,10},{9,11},{10,... | collective-permute-start | bytes 9437192 | tf_op jit(solution)/shard_map/ppermute | solution.py:530
  353.0 34.1 %collective-permute-start.55 = (bf16[96,1920]{1,0:T(8,128)(2,1)S(1)}, bf16[96,1920]{1,0:T(8,128)(2,1)S(1)}, u32[]{:S(2)}, u32[]{:S(2)}) collective-permute-start(bf16[96,1920]{1,0:T(8,128)(2,1)S(1)} %get-tuple-element.556), channel_id=1, source_target_pairs={{0,4},{1,5},{2,6},{3,7},{4,0},{5,1},{6,2},{7,3},{8,12},{9,13},{10,... | collective-permute-start | bytes 1105928 | tf_op jit(solution)/shard_map/ppermute | solution.py:530
  359.3 23.7 %collective-permute-start.61 = (bf16[96,1152]{1,0:T(8,128)(2,1)S(1)}, bf16[96,1152]{1,0:T(8,128)(2,1)S(1)}, u32[]{:S(2)}, u32[]{:S(2)}) collective-permute-start(bf16[96,1152]{1,0:T(8,128)(2,1)S(1)} %get-tuple-element.566), channel_id=1, source_target_pairs={{0,4},{1,5},{2,6},{3,7},{4,0},{5,1},{6,2},{7,3},{8,12},{9,13},{10,... | collective-permute-start | bytes 663560 | tf_op jit(solution)/shard_map/ppermute | solution.py:530
  360.0 24.1 %collective-permute-start.62 = (bf16[96,1152]{1,0:T(8,128)(2,1)S(1)}, bf16[96,1152]{1,0:T(8,128)(2,1)S(1)}, u32[]{:S(2)}, u32[]{:S(2)}) collective-permute-start(bf16[96,1152]{1,0:T(8,128)(2,1)S(1)} %get-tuple-element.567), channel_id=1, source_target_pairs={{0,1},{1,0},{2,3},{3,2},{4,5},{5,4},{6,7},{7,6},{8,9},{9,8},{10,11... | collective-permute-start | bytes 663560 | tf_op jit(solution)/shard_map/ppermute | solution.py:530
  387.2 18.3 %collective-permute-start.67 = (bf16[192,1536]{1,0:T(8,128)(2,1)S(1)}, bf16[192,1536]{1,0:T(8,128)(2,1)S(1)}, u32[]{:S(2)}, u32[]{:S(2)}) collective-permute-start(bf16[192,1536]{1,0:T(8,128)(2,1)S(1)} %pad_maximum_fusion.6), channel_id=1, source_target_pairs={{0,1},{1,0},{2,3},{3,2},{4,5},{5,4},{6,7},{7,6},{8,9},{9,8},{10,11... | collective-permute-start | bytes 1769480 | tf_op jit(solution)/shard_map/ppermute | solution.py:530
  394.6 53.7 %collective-permute-start.70 = (bf16[512,384]{1,0:T(8,128)(2,1)}, bf16[512,384]{1,0:T(8,128)(2,1)}, u32[]{:S(2)}, u32[]{:S(2)}) collective-permute-start(bf16[512,384]{1,0:T(8,128)(2,1)} %get-tuple-element.608), channel_id=1, source_target_pairs={{0,2},{1,3},{2,0},{3,1},{4,6},{5,7},{6,4},{7,5},{8,10},{9,11},{10,... | collective-permute-start | bytes 1179656 | tf_op jit(solution)/shard_map/ppermute | solution.py:530
  394.7 30.4 %collective-permute-start.77 = (bf16[96,1536]{1,0:T(8,128)(2,1)}, bf16[96,1536]{1,0:T(8,128)(2,1)}, u32[]{:S(2)}, u32[]{:S(2)}) collective-permute-start(bf16[96,1536]{1,0:T(8,128)(2,1)} %get-tuple-element.624), channel_id=1, source_target_pairs={{0,4},{1,5},{2,6},{3,7},{4,0},{5,1},{6,2},{7,3},{8,12},{9,13},{10,... | collective-permute-start | bytes 884744 | tf_op jit(solution)/shard_map/ppermute | solution.py:530
  399.2 22.2 %collective-permute-start.72 = (bf16[192,1152]{1,0:T(8,128)(2,1)}, bf16[192,1152]{1,0:T(8,128)(2,1)}, u32[]{:S(2)}, u32[]{:S(2)}) collective-permute-start(bf16[192,1152]{1,0:T(8,128)(2,1)} %pad_maximum_fusion.9), channel_id=1, source_target_pairs={{0,4},{1,5},{2,6},{3,7},{4,0},{5,1},{6,2},{7,3},{8,12},{9,13},{10,... | collective-permute-start | bytes 1327112 | tf_op jit(solution)/shard_map/ppermute | solution.py:530
  425.1 21.3 %collective-permute-start.76 = (bf16[192,1920]{1,0:T(8,128)(2,1)S(1)}, bf16[192,1920]{1,0:T(8,128)(2,1)S(1)}, u32[]{:S(2)}, u32[]{:S(2)}) collective-permute-start(bf16[192,1920]{1,0:T(8,128)(2,1)S(1)} %copy-done.139), channel_id=1, source_target_pairs={{0,1},{1,0},{2,3},{3,2},{4,5},{5,4},{6,7},{7,6},{8,9},{9,8},{10,11... | collective-permute-start | bytes 2211848 | tf_op jit(solution)/shard_map/ppermute | solution.py:530
  446.4 27.3 %collective-permute-start.86 = (bf16[3,512,768]{2,1,0:T(8,128)(2,1)}, bf16[3,512,768]{2,1,0:T(8,128)(2,1)S(1)}, u32[]{:S(2)}, u32[]{:S(2)}) collective-permute-start(bf16[3,512,768]{2,1,0:T(8,128)(2,1)} %get-tuple-element.597.h_ref.refs_2_), channel_id=1, source_target_pairs={{0,2},{1,3},{2,0},{3,1},{4,6},{5,7},{6,4},{7,5},{8,10},{9,11},{10,... | collective-permute-start | bytes 7077896 | tf_op jit(solution)/shard_map/ppermute | solution.py:530
  459.8 28.5 %collective-permute-start.69 = (bf16[96,1536]{1,0:T(8,128)(2,1)S(1)}, bf16[96,1536]{1,0:T(8,128)(2,1)S(1)}, u32[]{:S(2)}, u32[]{:S(2)}) collective-permute-start(bf16[96,1536]{1,0:T(8,128)(2,1)S(1)} %copy-done.148), channel_id=1, source_target_pairs={{0,8},{1,9},{2,10},{3,11},{4,12},{5,13},{6,14},{7,15},{8,0},{9,1},... | collective-permute-start | bytes 884744 | tf_op jit(solution)/shard_map/ppermute | solution.py:530
  463.3 39.2 %collective-permute-start.99 = (bf16[48,1152]{1,0:T(8,128)(2,1)S(1)}, bf16[48,1152]{1,0:T(8,128)(2,1)S(1)}, u32[]{:S(2)}, u32[]{:S(2)}) collective-permute-start(bf16[48,1152]{1,0:T(8,128)(2,1)S(1)} %slice.476), channel_id=1, source_target_pairs={{0,16},{1,17},{2,18},{3,19},{4,20},{5,21},{6,22},{7,23},{8,24},{9,... | collective-permute-start | bytes 331784 | tf_op jit(solution)/shard_map/ppermute | solution.py:530
  473.6 30.5 %collective-permute-start.97 = (bf16[192,1920]{1,0:T(8,128)(2,1)S(1)}, bf16[192,1920]{1,0:T(8,128)(2,1)S(1)}, u32[]{:S(2)}, u32[]{:S(2)}) collective-permute-start(bf16[192,1920]{1,0:T(8,128)(2,1)S(1)} %pad_maximum_fusion.3), channel_id=1, source_target_pairs={{0,4},{1,5},{2,6},{3,7},{4,0},{5,1},{6,2},{7,3},{8,12},{9,13},{10,... | collective-permute-start | bytes 2211848 | tf_op jit(solution)/shard_map/ppermute | solution.py:530
  480.1 25.3 %collective-permute-start.98 = (bf16[192,1920]{1,0:T(8,128)(2,1)S(1)}, bf16[192,1920]{1,0:T(8,128)(2,1)S(1)}, u32[]{:S(2)}, u32[]{:S(2)}) collective-permute-start(bf16[192,1920]{1,0:T(8,128)(2,1)S(1)} %pad_maximum_fusion.4), channel_id=1, source_target_pairs={{0,1},{1,0},{2,3},{3,2},{4,5},{5,4},{6,7},{7,6},{8,9},{9,8},{10,11... | collective-permute-start | bytes 2211848 | tf_op jit(solution)/shard_map/ppermute | solution.py:530
  501.3 36.9 %collective-permute-start.68 = (bf16[256,768]{1,0:T(8,128)(2,1)}, bf16[256,768]{1,0:T(8,128)(2,1)}, u32[]{:S(2)}, u32[]{:S(2)}) collective-permute-start(bf16[256,768]{1,0:T(8,128)(2,1)} %get-tuple-element.772), channel_id=1, source_target_pairs={{0,1},{1,0},{2,3},{3,2},{4,5},{5,4},{6,7},{7,6},{8,9},{9,8},{10,11... | collective-permute-start | bytes 1179656 | tf_op jit(solution)/shard_map/ppermute | solution.py:530
  504.2 34.0 %collective-permute-start.91 = (bf16[48,1536]{1,0:T(8,128)(2,1)}, bf16[48,1536]{1,0:T(8,128)(2,1)}, u32[]{:S(2)}, u32[]{:S(2)}) collective-permute-start(bf16[48,1536]{1,0:T(8,128)(2,1)} %slice.471), channel_id=1, source_target_pairs={{0,16},{1,17},{2,18},{3,19},{4,20},{5,21},{6,22},{7,23},{8,24},{9,... | collective-permute-start | bytes 442376 | tf_op jit(solution)/shard_map/ppermute | solution.py:530
  519.2 19.0 %collective-permute-start.90 = (bf16[48,1536]{1,0:T(8,128)(2,1)}, bf16[48,1536]{1,0:T(8,128)(2,1)}, u32[]{:S(2)}, u32[]{:S(2)}) collective-permute-start(bf16[48,1536]{1,0:T(8,128)(2,1)} %slice.469), channel_id=1, source_target_pairs={{0,16},{1,17},{2,18},{3,19},{4,20},{5,21},{6,22},{7,23},{8,24},{9,... | collective-permute-start | bytes 442376 | tf_op jit(solution)/shard_map/ppermute | solution.py:530
  (227 other events, 2135.0 us)

commit v3 on v2

--- a/solution.py
+++ b/solution.py
@@ -73,12 +73,16 @@
     return jnp.einsum("hcab,abr->hcr", pairs, hot, precision=highest)
 
 
+def in_hbm(array):
+    return pltpu.with_memory_space_constraint(array, pltpu.HBM)
+
+
 class Projection:
     def __init__(self, views, tile, start, tiles):
         self.views, self.tile, self.start, self.tiles = views, tile, start, tiles
 
     def arrays(self):
-        return [array for share in self.views for array, _, _ in share]
+        return [in_hbm(array) for share in self.views for array, _, _ in share]
 
     def specs(self):
         return [
@@ -87,11 +91,33 @@
             for _, at, rows in share
         ]
 
-    def group(self, refs):
-        refs, out = list(refs), []
+    def read(self, refs):
+        refs, shares = list(refs), []
         for share in self.views:
-            out.append([refs.pop(0) for _ in share])
-        return out, refs
+            shares.append(joined([refs.pop(0)[...] for _ in share], 0))
+        return joined(shares, 1), refs
+
+
+class BlocksProjection:
+    def __init__(self, array, places, tile, start, tiles):
+        self.array, self.places, self.tile, self.start, self.tiles = array, places, tile, start, tiles
+
+    def arrays(self):
+        return [self.places, in_hbm(self.array)]
+
+    def specs(self):
+        return [
+            pl.BlockSpec(memory_space=pltpu.SMEM),
+            pl.BlockSpec(
+                self.array.shape[:2] + (self.tile,), lambda t: (0, 0, self.start + t)
+            ),
+        ]
+
+    def read(self, refs):
+        places, blocks, *refs = refs
+        shares, count = self.places.shape
+        parts = [[blocks[places[j, r]] for r in range(count)] for j in range(shares)]
+        return joined([joined(part, 0) for part in parts], 1), refs
 
 
 def whole(array):
@@ -112,12 +138,10 @@
 
 def project(x, weight, how, slope=None):
     rows, width = x.shape
-    count = len(weight.arrays())
 
     def kernel(x_ref, *refs):
-        shares, refs = weight.group(refs)
-        x = x_ref[...]
-        out = joined([matmul(x, joined([r[...] for r in share], 0)) for share in shares], 1)
+        tile, refs = weight.read(refs)
+        out = matmul(x_ref[...], tile)
         if how == "gelu":
             refs[0][...], refs[1][...] = gelu_pair(out)
         elif how == "slope":
@@ -149,11 +173,9 @@
     n_extra = len(extra) + (params is not None)
 
     def kernel(h_ref, *refs):
-        shares, refs = weight.group(refs)
+        tile, refs = weight.read(refs)
         extra, outs, sums = refs[:n_extra], refs[n_extra:-1], refs[-1]
         t = pl.program_id(0)
-        h = h_ref[...]
-        parts = []
 
         def param(i):
             return extra[-1][at[i] : at[i] + 1, :]
@@ -176,9 +198,7 @@
             inner = (inner - normed * jnp.mean(scaled * normed, axis=-1, keepdims=True)) * scale
             return inner, cast_low(inner), jnp.concatenate(grads, axis=0)
 
-        for pieces in zip(*shares):
-            parts.append(matmul_nt(h, joined([piece[...] for piece in pieces], 1)))
-        total = joined(parts, 1)
+        total = matmul_nt(h_ref[...], tile)
 
         @pl.when(t == 0)
         def _():
@@ -249,9 +269,10 @@
     return got if len(outs) > 1 else got[0]
 
 
-def weight_grad(products, factor, cut=None):
+def weight_grad(products, factor, way=None):
     width = products[0][0].shape[1]
     high = width // 2
+    rows, columns = high // 2, width // 2
     counts = [product[2].shape[0] for product in products]
     ends = [sum(counts[: i + 1]) for i in range(len(counts))]
     starts = [end - count for end, count in zip(ends, counts)]
@@ -274,37 +295,44 @@
                 if factor != 1.0:
                     total = total * factor
                 total = cast_low(total)
-                if cut is None:
+                if way is None:
                     outs[0][...] = total
                     return
-                rows, columns, strip = cut
-                if strip:
-                    outs[0][...] = total[rows : rows + strip, columns:]
-                    outs[1][...] = total[rows + strip :, columns:]
+                parts = {
+                    (x, y): total[x * rows : (x + 1) * rows, y * columns : (y + 1) * columns]
+                    for x in range(2)
+                    for y in range(2)
+                }
+                if way == "both":
+                    outs[0][...] = parts[1, 1][: rows // 2]
+                    outs[1][...] = parts[1, 1][rows // 2 :]
+                    outs[2][...] = parts[1, 0]
+                    outs[3][...] = parts[0, 1]
                 else:
-                    outs[0][...] = total[rows:, columns:]
-                outs[-3][...] = total[rows:, :columns]
-                outs[-2][...] = total[:rows, columns:]
-                outs[-1][...] = total[:rows, :columns]
+                    other = (1, 0) if way == "xy" else (0, 1)
+                    outs[0][:rows, :] = parts[1, 1]
+                    outs[0][rows:, :] = parts[other]
+                    outs[1][...] = parts[other[::-1]]
+                outs[-1][...] = parts[0, 0]
 
     def column(rows, columns):
         return pl.BlockSpec((rows, columns), lambda t: (0, t))
 
     in_specs, args = [], []
     for product, start, count in zip(products, starts, counts):
-        rows = product[0].shape[0]
+        depth = product[0].shape[0]
         tile = pl.BlockSpec(
-            (None, rows, width),
+            (None, depth, width),
             lambda t, start=start, count=count: (jnp.clip(t - start, 0, count - 1), 0, 0),
         )
-        in_specs += [pl.BlockSpec((rows, high), lambda t: (0, 0))] * 2 + [tile] * 2
+        in_specs += [pl.BlockSpec((depth, high), lambda t: (0, 0))] * 2 + [tile] * 2
         args += product
-    if cut is None:
+    if way is None:
         parts = [(high, width)]
+    elif way == "both":
+        parts = [(rows // 2, columns)] * 2 + [(rows, columns)] * 3
     else:
-        rows, columns, strip = cut
-        parts = [(strip, columns), (rows - strip, columns)] if strip else [(rows, columns)]
-        parts = parts + [(rows, columns)] * 3
+        parts = [(high, columns), (rows, columns), (rows, columns)]
     outs = pl.pallas_call(
         kernel,
         grid=(tiles,),
@@ -320,7 +348,57 @@
             transcendentals=0,
         ),
     )(*args)
-    return outs[0] if cut is None else outs
+    return outs[0] if way is None else outs
+
+
+def weight_grad_blocks(products, places):
+    rows, width = products[0][0].shape
+    shares, count = places.shape
+    block, share = width // count, width // shares
+    counts = [right.shape[0] for _, right in products]
+    ends = [sum(counts[: i + 1]) for i in range(len(counts))]
+    starts = [end - count for end, count in zip(ends, counts)]
+    tiles = ends[-1]
+
+    def kernel(places, *refs):
+        out, turned = refs[2 * len(products)], refs[2 * len(products) + 1 :]
+        t = pl.program_id(0)
+        for i, (held, start, end) in enumerate(zip(turned, starts, ends)):
+
+            @pl.when(t == start)
+            def _():
+                held[...] = refs[2 * i][...].T
+
+            @pl.when((t >= start) & (t < end))
+            def _():
+                total = cast_low(matmul(held[...], refs[2 * i + 1][...]))
+                for j in range(shares):
+                    for r in range(count):
+                        part = total[r * block : (r + 1) * block, j * share : (j + 1) * share]
+                        out[places[j, r]] = part
+
+    in_specs, args = [pl.BlockSpec(memory_space=pltpu.SMEM)], [places]
+    for (left, right), start, depth in zip(products, starts, counts):
+        tile = pl.BlockSpec(
+            (None, rows, width),
+            lambda t, start=start, depth=depth: (jnp.clip(t - start, 0, depth - 1), 0, 0),
+        )
+        in_specs += [whole(left), tile]
+        args += [left, right]
+    return pl.pallas_call(
+        kernel,
+        grid=(tiles,),
+        in_specs=in_specs,
+        out_specs=pl.BlockSpec((places.size, block, share), lambda t: (0, 0, t)),
+        out_shape=jax.ShapeDtypeStruct((places.size, block, tiles * share), bf16),
+        scratch_shapes=[pltpu.VMEM((width, rows), bf16) for _ in products],
+        compiler_params=vmem,
+        cost_estimate=pl.CostEstimate(
+            flops=sum(2 * width * right.size for _, right in products),
+            bytes_accessed=sum(2 * right.size for _, right in products) + 2 * tiles * width * width,
+            transcendentals=0,
+        ),
+    )(*args)
 
 
 def pair_of(array, role):
@@ -453,14 +531,29 @@
     )(q, k, v, grad, probs, hot, other, keep)
 
 
+GATHERS = (
+    (("qkv",), "both"),
+    (("outa", "ina",), "both"),
+    (("mlpa",), "both"),
+    (("q", "kv", "outb", "inb", "mlpb",), "blocks"),
+)
+SCATTERS = (
+    (("mlpb", "inb",), "blocks"),
+    (("q", "kv", "outb", "mlpa",), "both"),
+    (("ina", "outa",), "both"),
+    (("qkv",), "both"),
+)
+
+PAGE, LAYERS, OUT, VISION, TEXT, SMALL, W1, W2, W3, W4, G1, G2, G3, G4 = range(1, 15)
+GATHER, SCATTER = W1, G1
+
 ORDER = (
-    "w1", "page", "w1", "page", "w2", "w1", "page", "w2", "w3", "w1", "page", "w3", "w4", "w1", "w2", "page", "w1", "layers", "w4", "w5", "w3", "layers", "w2", "w5", "w3", "+g6", "w4",
-    "w2", "w5", "w6", "w3", "g6", "w2", "layers", "w3", "w6", "w4", "layers", "w4", "w5", "+g4", "w4", "w6", "layers", "g4", "w5", "w6", "+g3", "w5", "+g5", "w6", "layers", "w6",
-    "layers", "+g1", "layers", "+g2", "g1", "layers", "layers", "+g1", "g2", "g3", "+g2", "layers", "layers", "+g4", "+g3", "g1", "g2", "g5", "g3", "g4", "g1", "layers",
-    "g3", "g2", "out", "g1", "layers", "+g5", "g3", "g4", "g2", "g3", "+g6", "g5", "small", "vision", "g2", "small", "g4", "g5", "g6", "g4", "small", "small", "g1", "g6", "g3", "g5",
-    "small", "g2", "small", "g6", "g5", "g6", "g4", "g1", "text", "g5", "g6",
+    W1, PAGE, W1, W1, PAGE, W2, W2, W1, PAGE, W3, W1, W2, PAGE, W1, PAGE, W3, LAYERS, LAYERS,
+    LAYERS, W2, W3, W2, W2, LAYERS, LAYERS, W3, W3, W3, LAYERS, W4, LAYERS, LAYERS, LAYERS,
+    LAYERS, LAYERS, LAYERS, LAYERS, -G1, OUT, -G2, LAYERS, G2, LAYERS, LAYERS, VISION, -G2, G2,
+    LAYERS, -G3, G3, -G4, G4, G2, LAYERS, -G3, G3, G2, LAYERS, -G4, G3, G2, TEXT, G4, G3, SMALL,
+    SMALL, G2, G4, SMALL, G3, SMALL, G4, SMALL, G3, G4, SMALL, G4, G1,
 )
-WAYS = ("both", "both", "both", "both", "both", "both", "both", "both", "both", "both", "both", "both")
 
 
 class Flows:
@@ -478,9 +571,14 @@
         for name, arrays in zip(names, held):
             self.send(name, arrays)
 
+    def mark(self, values):
+        values, self.token = lax.optimization_barrier((values, self.token))
+        return values
+
     def send(self, name, arrays):
         try:
-            self.pending[name] = self.flows[name].send(arrays)
+            arrays = self.flows[name].send(arrays)
+            self.pending[name] = self.mark(arrays) if name == LAYERS else arrays
         except StopIteration as end:
             self.results[name] = end.value
 
@@ -527,7 +625,7 @@
             for d in range(ndp)
             for t in range(nt)
         ]
-        return lax.ppermute(values, ("dp", "tensor"), pairs)
+        return lax.ppermute(flows.mark(values), ("dp", "tensor"), pairs)
 
     def in_order(relative):
         return [
@@ -535,7 +633,7 @@
             for a in range(nt)
         ]
 
-    def gather_rows(piece, way="both"):
+    def gather_rows(piece, way):
         (piece,) = yield [piece]
         for bits in z_bits:
             for bit in reversed(bits):
@@ -543,91 +641,131 @@
                 if bit == bits[0]:
                     others = yield others
                 piece = jnp.concatenate([piece, *others], axis=0)
-        half = piece.shape[0] // 2
-        if not direct or way == "xy":
-            (along_x,) = yield [swap(piece, 2, 0)]
-            near = jnp.concatenate([piece, along_x], axis=0)
-            others = yield [swap(near, 0, j) for j in range(1, nt)]
-            plane = jnp.concatenate([near, *others], axis=0)
-        elif way == "yx":
+        rows = piece.shape[0]
+        half = rows // 2
+
+        if direct and way == "both":
+            along_x, along_y = yield swap(piece, 2, 0), swap(piece, 0, 1)
+            first = (piece, along_x, along_y)
+            *far, piece_c, along_x_c, along_y_c = yield (
+                swap(along_y[:half], 2, 0),
+                swap(along_x[half:], 0, 1),
+                *[swap(array, 1, 0) for array in first],
+            )
+            far_c = yield [swap(array, 1, 0) for array in far]
+            return [
+                [(array, 0, rows) for array in (piece, along_x, piece_c, along_x_c)],
+                [(along_y, 0, rows)]
+                + [(array, 0, half) for array in far]
+                + [(along_y_c, 0, rows)]
+                + [(array, 0, half) for array in far_c],
+            ]
+        if direct and way == "yx":
             (along_y,) = yield [swap(piece, 0, 1)]
             near = jnp.concatenate([piece, along_y], axis=0)
-            (far,) = yield [swap(near, 2, 0)]
-            plane = jnp.concatenate([piece, far[: 2 * half], along_y, far[2 * half :]], axis=0)
-        else:
-            along_x, along_y = yield swap(piece, 2, 0), swap(piece, 0, 1)
-            far = yield swap(along_y[:half], 2, 0), swap(along_x[half:], 0, 1)
-            plane = jnp.concatenate([piece, along_x, along_y, *far], axis=0)
-        plane, core = yield [plane, swap(plane, 1, 0)]
-        return plane, core
-
-    def projection(gathered, start, tiles):
-        plane, core = gathered
-        rows = width // 2
+            far, near_c = yield swap(near, 2, 0), swap(near, 1, 0)
+            (far_c,) = yield [swap(far, 1, 0)]
+            return [[(array, j, rows) for array in (near, far, near_c, far_c)] for j in range(2)]
+        (along_x,) = yield [swap(piece, 2, 0)]
+        near = jnp.concatenate([piece, along_x], axis=0)
+        near_c, *others = yield [swap(near, 1, 0)] + [swap(near, 0, j) for j in range(1, nt)]
+        others_c = yield [swap(array, 1, 0) for array in others]
+        return [
+            [(array, 0, 2 * rows), (array_c, 0, 2 * rows)]
+            for array, array_c in zip([near, *others], [near_c, *others_c])
+        ]
+
+    def projection(*names):
+        group = next(group for group in gathers if names[0] in group)
+        views = results[gathers[group]]
+        counts = [pieces[name].shape[1] // share for name in group]
+        first = group.index(names[0])
+        start, tiles = sum(counts[:first]), sum(counts[first : first + len(names)])
+        if not isinstance(views, list):
+            return BlocksProjection(views, places, share, start, tiles)
         if direct:
-            views = [[(plane, j, rows), (core, j, rows)] for j in range(nt)]
             return Projection(views, share, start, tiles)
-        plane, core = (
-            array[:, start * share : (start + tiles) * share].reshape(nt, rows, tiles, share)
-            for array in gathered
-        )
-        both = jnp.concatenate([plane, core], axis=1)
-        both = jnp.transpose(both, (1, 2, 0, 3)).reshape(width, tiles * width)
-        return Projection([[(both, 0, width)]], width, 0, tiles)
-
-    def scatter_rows(count, way="both"):
-        sides, others = {}, {}
+        shares = [
+            jnp.concatenate([array[:, start * share : (start + tiles) * share] for array, _, _ in part], axis=0)
+            for part in views
+        ]
+        both = jnp.stack([part.reshape(width, tiles, share) for part in shares], axis=2)
+        return Projection([[(both.reshape(width, tiles * width), 0, width)]], width, 0, tiles)
+
+    def at_once(flow, arrays):
+        try:
+            while True:
+                arrays = flow.send(arrays)
+        except StopIteration as end:
+            return end.value
+
+    def gather_blocks(piece):
+        if direct:
+            (blocks,) = yield [lax.all_gather(flows.mark(piece), ("dp", "tensor"))]
+            return blocks
+        (piece,) = yield [piece]
+        flow = gather_rows(piece, "xy")
+        return at_once(flow, next(flow))
+
+    def scatter_blocks(names):
+        sides = yield
+        if direct:
+            held = {key: array for key, (array, _) in sides.items()}
+            products = [(held[name, "left"], held[name, "right"]) for name in names]
+            parts = weight_grad_blocks(products, places)
+            parts = flows.mark(parts.reshape(-1, parts.shape[2]))
+            (out,) = yield [
+                lax.psum_scatter(parts, ("dp", "tensor"), scatter_dimension=0, tiled=True)
+            ]
+            return out.astype(f32)
+        yield []
+        flow = scatter_rows(names, "xy")
+        next(flow)
+        flow.send(flow.send(sides))
+        return at_once(flow, {})
+
+    def scatter_rows(names, way):
+        held, others = {}, {}
         for _ in range(2):
             given = yield
-            names = list(given)
-            sides.update({name: given[name][0] for name in names})
-            got = yield [swap(given[name][1], 1, 0) for name in names]
-            others.update(zip(names, got))
+            held.update({key: array for key, (array, _) in given.items()})
+            got = yield [swap(part, 1, 0) for _, part in given.values()]
+            others.update(zip(given, got))
         products = [
-            (sides[p, "left"], others[p, "left"], sides[p, "right"], others[p, "right"])
-            for p in range(count)
+            tuple(found[name, side] for side in ("left", "right") for found in (held, others))
+            for name in names
         ]
-        high = width // 2
-        rows = high // 2
+        rows = width // 4
         half = rows // 2
         if direct:
-            cut = (rows, share, half if way == "both" else 0)
-            parts = weight_grad(products, 1.0 / copies, cut)
-            *far, near_x, near_y, here = parts
+            away, *near, here = weight_grad(products, 1.0 / copies, way)
             if way == "both":
-                from_x, from_y = yield swap(far[0], 2, 0), swap(far[1], 0, 1)
-                near_y = jnp.concatenate([near_y[:half] + from_x, near_y[half:]], axis=0)
-                near_x = jnp.concatenate([near_x[:half], near_x[half:] + from_y], axis=0)
-                from_x, from_y = yield swap(near_x, 2, 0), swap(near_y, 0, 1)
-                here = here.astype(f32) + from_x + from_y
-            elif way == "xy":
-                far, from_x = yield swap(far[0], 2, 0), swap(near_x, 2, 0)
-                (from_y,) = yield [swap(near_y + far, 0, 1)]
-                here = here.astype(f32) + from_x + from_y
+                far_y, near_x, near_y = near
+                from_x, from_y = yield swap(away, 2, 0), swap(far_y, 0, 1)
+                near_y = lax.dynamic_update_slice(near_y, near_y[:half] + from_x, (0, 0))
+                near_x = lax.dynamic_update_slice(near_x, near_x[half:] + from_y, (half, 0))
+                got = yield swap(near_x, 2, 0), swap(near_y, 0, 1)
             else:
-                far, from_y = yield swap(far[0], 0, 1), swap(near_y, 0, 1)
-                (from_x,) = yield [swap(near_x + far, 2, 0)]
-                here = here.astype(f32) + from_x + from_y
+                masks = ((2, 0), (0, 1)) if way == "xy" else ((0, 1), (2, 0))
+                (came,) = yield [swap(away, *masks[0])]
+                (other,) = yield [swap(near[0] + came[:rows], *masks[1])]
+                got = [came[rows:], other]
         else:
-            total = weight_grad(products, 1.0 / copies)
-            total = total.reshape(2, rows, -1, nt, share)
-
-            def part(x, j):
-                return total[x, :, :, j].reshape(rows, -1)
-
-            from_x = yield [swap(part(1, j), 2, 0) for j in range(nt)]
-            here = [part(0, j) + from_x[j] for j in range(nt)]
-            from_y = yield [swap(here[j], 0, j) for j in range(1, nt)]
-            here = sum([got.astype(f32) for got in from_y], here[0].astype(f32))
+            total = weight_grad(products, 1.0 / copies).reshape(2, rows, -1, nt, share)
+            parts = [[total[x, :, :, j].reshape(rows, -1) for j in range(nt)] for x in range(2)]
+            from_x = yield [swap(part, 2, 0) for part in parts[1]]
+            near = [part + came for part, came in zip(parts[0], from_x)]
+            here = near[0]
+            got = yield [swap(near[j], 0, j) for j in range(1, nt)]
         for bits in reversed(z_bits):
             for bit in bits:
-                here = cast_low(here)
                 half = here.shape[0] // 2
-                got = [swap(here[half:], 1 << bit, 0)]
+                away = sum([part[half:] for part in got], here[half:].astype(f32))
+                here = sum([part[:half] for part in got], here[:half].astype(f32))
+                got = [swap(cast_low(away), 1 << bit, 0)]
                 if bit == bits[-1]:
                     got = yield got
-                here = here[:half].astype(f32) + got[0]
-        return here
+        return here + got[0]
 
     def to_owners(rows):
         cut = rows.shape[0] // nt
@@ -640,11 +778,7 @@
         (rows_text, rows_vision, shares, ids, box, kept_text, kept_patch) = yield [
             text_rows, vision_rows, out_grad, segment_ids, segment_box, text_keep, patch_keep
         ]
-        place = jnp.arange(width)
-        relative = place // (2 * nz * block) + 2 * (place // (nz * block) % 2)
-        for bit in range(2, ndp.bit_length() - 1):
-            relative = relative + (1 << bit) * (place // (nz * block >> (bit - 1)) % 2)
-        feature = (own ^ relative) * block + place % block
+        feature = source * block + jnp.arange(width) % block
         order = cast_low(jnp.arange(width)[:, None] == feature[None, :])
         shares = in_order([shares[a // copies] for a in range(nt)])
         tables = jnp.stack([box_table_a, box_table_b])
@@ -690,6 +824,13 @@
         (grad_in,) = yield [cast_low(matmul(grad_in, order))]
         return order, text, vision, grad_in, hot, turned, other_a, other_b, spread
 
+    at = jnp.arange(width) // block
+    relative = at // (2 * nz) + 2 * (at // nz % 2)
+    for bit in range(2, ndp.bit_length() - 1):
+        relative = relative + (1 << bit) * (at // (nz >> (bit - 1)) % 2)
+    source = own ^ relative
+    places = source[::block] * nt + (mine ^ jnp.arange(nt, dtype=jnp.int32))[:, None]
+
     flows = Flows(text_keep[0, 0])
 
     norms = jnp.concatenate([norm_gain_a, norm_shift_a, norm_gain_b, norm_shift_b], axis=0)
@@ -697,168 +838,184 @@
     def weights(*pieces):
         return gather_rows(jnp.concatenate(pieces, axis=1))
 
-    for name, way, pieces in (
-        ("w1", WAYS[0], (attn_qkv_a.reshape(block, -1), norm_columns)),
-        ("w2", WAYS[1], (attn_out_a.T, mlp_in_a)),
-        ("w3", WAYS[2], (mlp_out_a.T,)),
-        ("w4", WAYS[3], (attn_query_b, attn_kv_b.reshape(block, -1))),
-        ("w5", WAYS[4], (attn_out_b.T, mlp_in_b)),
-        ("w6", WAYS[5], (mlp_out_b.T,)),
-    ):
-        flows.add(name, gather_rows(jnp.concatenate(pieces, axis=1), way))
-    flows.add("page", page_parts())
-    for i, count in enumerate((1, 2, 2, 1, 2, 1)):
-        flows.add(f"g{i + 1}", scatter_rows(count, WAYS[6 + i]))
+    pieces = {
+        "qkv": attn_qkv_a.reshape(block, -1),
+        "outa": attn_out_a.T,
+        "ina": mlp_in_a,
+        "mlpa": mlp_out_a.T,
+        "q": attn_query_b,
+        "kv": attn_kv_b.reshape(block, -1),
+        "outb": attn_out_b.T,
+        "inb": mlp_in_b,
+        "mlpb": mlp_out_b.T,
+    }
+    gathers, scatters = {}, {}
+    for i, (group, way) in enumerate(GATHERS):
+        gathers[group] = GATHER + i
+        own_pieces = [pieces[name] for name in group] + [norm_columns] * ("qkv" in group)
+        piece = jnp.concatenate(own_pieces, axis=1)
+        gather = gather_blocks(piece) if way == "blocks" else gather_rows(piece, way)
+        flows.add(gathers[group], gather)
+    flows.add(PAGE, page_parts())
+    for i, (group, way) in enumerate(SCATTERS):
+        scatters[group] = SCATTER + i
+        scatter = scatter_blocks(group) if way == "blocks" else scatter_rows(group, way)
+        flows.add(scatters[group], scatter)
     results = flows.results
-    sides = {}
+    sides, sent = {}, set()
     tables_grads, norm_grads = {}, {}
     high = width // 2
 
+    def given(flow):
+        group = next(group for group, name in scatters.items() if name == flow)
+        ready = {key: side for key, side in sides.items() if key[0] in group and key not in sent}
+        sent.update(ready)
+        return ready
+
     def chain():
         yield []
-        order, text, vision, grad_in, hot, turned, other_a, other_b, spread = results["page"]
+        order, text, vision, grad_in, hot, turned, other_a, other_b, spread = results[PAGE]
         pairs = spread.shape[1] // (4 * LANES)
-        sides["g3"] = {(1, "left"): (vision, vision[:, high:])}
-        sides["g6"] = {(0, "left"): (text, text[:, high:])}
-
-        at = 3 * share
-        gathered = results["w1"]
-        norms = jnp.concatenate([part[:high, at : at + 8] for part in gathered], axis=0)
-        (norms,) = yield [norms.T.astype(f32)]
-        qkv_a = projection(gathered, 0, 3)
-        qkv = project(text, qkv_a, "low")
+        sides["kv", "left"] = (vision, vision[:, high:])
+        sides["qkv", "left"] = (text, text[:, high:])
+
+        group = next(group for group in gathers if "qkv" in group)
+        at = sum(pieces[name].shape[1] for name in group)
+        norms = [
+            array[i * rows : (i + 1) * rows, at : at + 8]
+            for array, i, rows in results[gathers[group]][0]
+        ]
+        (norms,) = yield [jnp.concatenate(norms, axis=0).T.astype(f32)]
+        qkv_a = projection("qkv")
+        (qkv,) = yield [project(text, qkv_a, "low")]
         triple_a = ((qkv, 0), (qkv, 1), (qkv, 2))
         context_a, probs_a = yield attend_forward(*triple_a, hot, (spread, 0), *other_a)
-        out_a, in_a = projection(results["w2"], 0, 1), projection(results["w2"], 1, tiles)
-        normed_a0, scale_a0, mixed_a, part = project_back(
+        out_a = projection("outa")
+        normed_a0, scale_a0, mixed_a, part = yield project_back(
             context_a[None], out_a, "norm", [text], norms, (0, 2)
         )
+        sides["outa", "right"] = (context_a[None], context_a[None])
+        sides["ina", "left"] = (mixed_a, part)
+        in_a = projection("ina")
         gelu_a, slope_a = yield project(mixed_a, in_a, "gelu")
-        sides["g5"] = {
-            (0, "right"): (context_a[None], context_a[None]),
-            (1, "left"): (mixed_a, part),
-        }
-        sides["g4"] = {(0, "right"): (gelu_a, gelu_a)}
-        back_a = projection(results["w3"], 0, tiles)
+        sides["mlpa", "right"] = (gelu_a, gelu_a)
+        back_a = projection("mlpa")
         normed_a1, scale_a1, middle, part = yield project_back(
             gelu_a, back_a, "norm", [normed_a0], norms, (1, 3, 0, 2)
         )
-        sides["g3"][0, "left"] = (middle, part)
-
-        query_b, kv_b = projection(results["w4"], 0, 1), projection(results["w4"], 1, 2)
-        queries_b = project(middle, query_b, "low")
-        kv = project(vision, kv_b, "low")
+        sides["q", "left"] = (middle, part)
+
+        query_b, kv_b = projection("q"), projection("kv")
+        queries_b, kv = yield project(middle, query_b, "low"), project(vision, kv_b, "low")
         triple_b = ((queries_b, 0), (kv, 0), (kv, 1))
         context_b, probs_b = yield attend_forward(*triple_b, hot, (spread, pairs), *other_b)
-        out_b, in_b = projection(results["w5"], 0, 1), projection(results["w5"], 1, tiles)
-        normed_b0, scale_b0, mixed_b, part = project_back(
+        out_b = projection("outb")
+        normed_b0, scale_b0, mixed_b, part = yield project_back(
             context_b[None], out_b, "norm", [normed_a1], norms, (4, 6, 1, 3)
         )
+        sides["outb", "right"] = (context_b[None], context_b[None])
+        sides["inb", "left"] = (mixed_b, part)
+        in_b = projection("inb")
         gelu_b, slope_b = yield project(mixed_b, in_b, "gelu")
-        sides["g2"] = {
-            (0, "right"): (context_b[None], context_b[None]),
-            (1, "left"): (mixed_b, part),
-        }
-        sides["g1"] = {(0, "right"): (gelu_b, gelu_b)}
-        back_b = projection(results["w6"], 0, tiles)
+        sides["mlpb", "right"] = (gelu_b, gelu_b)
+        back_b = projection("mlpb")
         final, pre, branch, part, norm_grads["b1"] = yield project_back(
             gelu_b, back_b, "final", [normed_b0, grad_in], norms, (5, 7, 4, 6)
         )
 
-        sides["g1"] = {(0, "left"): (branch, part)}
-        flows.add("out", to_owners(cast_low(matmul_nt(final, order))))
+        sides["mlpb", "left"] = (branch, part)
+        flows.add(OUT, to_owners(cast_low(matmul_nt(final, order))))
         (hidden,) = yield [project(branch, back_b, "slope", slope_b)]
+        sides["inb", "right"] = (hidden, hidden)
         pre, attn_grad, part, norm_grads["b0"] = project_back(
             hidden, in_b, "back", [pre, normed_b0, scale_b0], norms, (4,)
         )
         (context_grad,) = project(attn_grad, out_b, "low")
         pre, attn_grad, part, context_grad = yield pre, attn_grad, part, context_grad
-        sides["g2"] = {(0, "left"): (attn_grad, part), (1, "right"): (hidden, hidden)}
-        query_grad, kv_grad, sums = yield attend_backward(
+        sides["outb", "left"] = (attn_grad, part)
+        query_grad, kv_grad, tables_grads["b"] = yield attend_backward(
             *triple_b, context_grad, probs_b, turned, *other_b
         )
-        tables_grads["b"] = sums
-        sides["g3"] = {
-            (0, "right"): (query_grad, query_grad),
-            (1, "right"): (kv_grad, kv_grad),
-        }
-        pre, branch, part, norm_grads["a1"] = project_back(
+        sides["q", "right"] = (query_grad, query_grad)
+        sides["kv", "right"] = (kv_grad, kv_grad)
+        vision_grad = project_back(kv_grad, kv_b, "low")
+        flows.add(VISION, to_owners(cast_low(matmul_nt(vision_grad, order))))
+        pre, branch, part, norm_grads["a1"] = yield project_back(
             query_grad, query_b, "back", [pre, normed_a1, scale_a1], norms, (1,)
         )
-        hidden = project(branch, back_a, "slope", slope_a)
-        pre, branch, part, hidden = yield pre, branch, part, hidden
-        sides["g4"] = {(0, "left"): (branch, part)}
-        vision_grad = project_back(kv_grad, kv_b, "low")
-        flows.add("vision", to_owners(cast_low(matmul_nt(vision_grad, order))))
+        sides["mlpa", "left"] = (branch, part)
+        (hidden,) = yield [project(branch, back_a, "slope", slope_a)]
+        sides["ina", "right"] = (hidden, hidden)
         pre, attn_grad, part, norm_grads["a0"] = project_back(
             hidden, in_a, "back", [pre, normed_a0, scale_a0], norms, (0,)
         )
         (context_grad,) = project(attn_grad, out_a, "low")
         pre, attn_grad, part, context_grad = yield pre, attn_grad, part, context_grad
-        sides["g5"] = {(0, "left"): (attn_grad, part), (1, "right"): (hidden, hidden)}
-        qkv_grad, sums = yield attend_backward(
+        sides["outa", "left"] = (attn_grad, part)
+        qkv_grad, tables_grads["a"] = yield attend_backward(
             *triple_a, context_grad, probs_a, turned, *other_a
         )
-        tables_grads["a"] = sums
-        sides["g6"] = {(0, "right"): (qkv_grad, qkv_grad)}
+        sides["qkv", "right"] = (qkv_grad, qkv_grad)
         text_grad = project_back(qkv_grad, qkv_a, "add", [pre])
-        flows.add("text", to_owners(cast_low(matmul_nt(text_grad, order))))
-        flows.add("small", small_sums(tables_grads["a"], tables_grads["b"]))
-
-    def small_sums(pairs_a, pairs_b):
+        flows.add(TEXT, to_owners(cast_low(matmul_nt(text_grad, order))))
+        flows.add(SMALL, small_sums(order))
+
+    def small_sums(order):
         norms = jnp.concatenate([norm_grads[i] for i in ("a0", "a1", "b0", "b1")], axis=0)
-        norms = jnp.transpose(norms.reshape(8, ndp, block), (1, 0, 2)).reshape(ndp, 8 * block)
-        tables = jnp.stack([table_grad(pairs_a), table_grad(pairs_b)])
-        heads = pairs_a.shape[0]
-        tables = jnp.transpose(tables.reshape(2, nt, heads // nt, 2, RELS), (1, 0, 2, 3, 4))
-        tables = tables.reshape(nt, -1)
-        size = tables.shape[1]
-        tables = jnp.pad(tables, ((0, 0), (0, -size % (8 * block)))).reshape(nt, -1, 8 * block)
-        depth = tables.shape[1]
-        tables = tables.reshape(nt * depth, 8 * block)
-        norms, tables = yield norms * (1.0 / copies), tables * (1.0 / copies)
-        for bits in (range(1), range(1, 2), *reversed(z_bits)):
+        norms = lax.dot_general(
+            norms, order.astype(f32), (((1,), (1,)), ((), ())), precision=highest, preferred_element_type=f32
+        )
+        tables = jnp.stack([table_grad(tables_grads["a"]), table_grad(tables_grads["b"])])
+        kept = (2, tables.shape[1] // nt, 2, RELS)
+        tables = tables.reshape(2, nt, -1)
+        size = 2 * tables.shape[2]
+        tables = jnp.stack(in_order([tables[:, j].reshape(size) for j in range(nt)]))
+        total = jnp.concatenate([norms, jnp.pad(tables, ((0, 0), (0, width - size)))], axis=0)
+        (total,) = yield [total * (1.0 / copies)]
+        for bits in (range(1), range(1, 2), *z_bits):
             for bit in bits:
-                half = norms.shape[0] // 2
-                got = [swap(jnp.concatenate([norms[half:], tables], axis=0), 1 << bit, 0)]
+                got = [swap(total, 1 << bit, 0)]
                 if bit == bits[-1]:
                     got = yield got
-                norms, tables = norms[:half] + got[0][:half], tables + got[0][half:]
-        others = yield [
-            swap(jnp.concatenate([norms, tables[j * depth : (j + 1) * depth]], axis=0), 0, j)
-            for j in range(1, nt)
-        ]
-        total = sum(others, jnp.concatenate([norms, tables[:depth]], axis=0))
-        tables = total[1:].reshape(-1)[:size].reshape(2, heads // nt, 2, RELS)
-        return total[0].reshape(8, block), tables
-
-    flows.add("layers", chain())
+                total = total + got[0]
+        got = yield [swap(total, 0, j) for j in range(1, nt)]
+        total = sum(got, total)
+        norms = lax.dynamic_slice(total, (0, own * block), (8, block))
+        tables = lax.dynamic_slice(total, (8 + mine, 0), (1, size))
+        return norms, tables.reshape(kept)
+
+    flows.add(LAYERS, chain())
     for name in ORDER:
-        if name.startswith("+"):
-            flows.send(name[1:], sides[name[1:]])
+        if name < 0:
+            flows.send(-name, given(-name))
         else:
             flows.step(name)
-    norm_sums, tables = results["small"]
+    norm_sums, tables = results[SMALL]
     tables = tables + (flows.token - text_keep[0, 0]).astype(f32)
-    grad_in_a, grad_in_b = results["g5"], results["g2"]
-    grad_second = results["g3"]
+    grads = {}
+    for group, flow in scatters.items():
+        start = 0
+        for name in group:
+            size = pieces[name].shape[1]
+            grads[name] = results[flow][:, start : start + size]
+            start += size
 
     return (
-        results["out"],
-        results["text"].astype(f32),
-        results["vision"].astype(f32),
-        results["g6"].reshape(block, 3, share),
-        grad_in_a[:, :share].T,
-        grad_in_a[:, share:],
-        results["g4"].T,
+        results[OUT],
+        results[TEXT].astype(f32),
+        results[VISION].astype(f32),
+        grads["qkv"].reshape(block, 3, share),
+        grads["outa"].T,
+        grads["ina"],
+        grads["mlpa"].T,
         norm_sums[0:4:2],
         norm_sums[1:4:2],
         tables[0],
-        grad_second[:, :share],
-        grad_second[:, share:].reshape(block, 2, share),
-        grad_in_b[:, :share].T,
-        grad_in_b[:, share:],
-        results["g1"].T,
+        grads["q"],
+        grads["kv"].reshape(block, 2, share),
+        grads["outb"].T,
+        grads["inb"],
+        grads["mlpb"].T,
         norm_sums[4:8:2],
         norm_sums[5:8:2],
         tables[1],

time: 565 us -> 502 us (0.89)
  starting transfers between devices: 96 us -> 58.3 us
  waiting for transfers between devices: 159 us -> 123 us
  between operations: 5.04 us -> 18 us
    ppermute x106 -> x75, waiting for transfers between devices: 159 us -> 117 us  [swap(): return lax.ppermute(flows.mark(values), ('dp', 'tensor'), pairs)]
    ppermute x106 -> x75, starting transfers between devices: 96 us -> 58.3 us  [swap(): return lax.ppermute(flows.mark(values), ('dp', 'tensor'), pairs)]
    pallas_call x6 -> x3, Pallas kernels: 33.5 us -> 22 us  [weight_grad(): pl.pallas_call(kernel, grid=(tiles,), in_specs=in_specs, out_specs=[colum...]
    pallas_call x0 -> x1, Pallas kernels: none -> 9.74 us  [weight_grad_blocks(): pl.pallas_call(kernel, grid=(tiles,), in_specs=in_specs, out_specs=pl.Blo...]
    concatenate x22 -> x3, other arithmetic: 9.15 us -> 1.36 us  [the longest x2 1.35 us: shards(): piece = jnp.concatenate(own_pieces, axis=1)]
    reduce_scatter x0 -> x1, waiting for transfers between devices: none -> 6.54 us  [scatter_blocks(): lax.psum_scatter(parts, ('dp', 'tensor'), scatter_dimension=0, tiled=True)]
    dynamic_update_slice x0 -> x6, other arithmetic: none -> 6.46 us  [the longest x3 3.71 us: scatter_rows(): near_y = lax.dynamic_update_slice(near_y, near_y[:half] + from_x, (0, 0))]
    pallas_call x9, Pallas kernels: 33.1 us -> 38.9 us  [project(): pl.pallas_call(kernel, grid=(weight.tiles,), in_specs=[whole(x)] + weight...]
  transfers between devices with their start and end apart: 106 -> 77, of which waited for: 37 -> 30; matrix products, arithmetic and copies ran while one was open for 18% -> 17% of each run, Pallas kernels for 28% -> 21%
where the time goes in v3:
time: 502 us; the launch traced here: 494 us
  Pallas kernels  158 us (31%)
  waiting for transfers between devices  123 us (25%)
  local copies, waits for them, and re-layouts  89.9 us (18%)
  starting transfers between devices  58.3 us (12%)
  other arithmetic  37.5 us (7%)
  between operations  18 us (4%)
  matrix products  8.86 us (2%)
    ppermute x75, waiting for transfers between devices, swap(): return lax.ppermute(flows.mark(values), ('dp', 'tensor'), pairs)  117 us
    ppermute x75, starting transfers between devices, swap(): return lax.ppermute(flows.mark(values), ('dp', 'tensor'), pairs)  58.3 us
    unnamed x320, local copies, waits for them, and re-layouts  50.8 us
    pallas_call x9, Pallas kernels, project_back(): pl.pallas_call(kernel, grid=(tiles,), in_specs=[tile_of(h)] + weight.spec...  46.7 us
    pallas_call x9, Pallas kernels, project(): pl.pallas_call(kernel, grid=(weight.tiles,), in_specs=[whole(x)] + weight...  38.9 us
    pallas_call x2, Pallas kernels, attend_backward(): pl.pallas_call(kernel, grid=(heads // 2,), in_specs=[pair_of(q, q_role),...  23 us
    pallas_call x3, Pallas kernels, weight_grad(): pl.pallas_call(kernel, grid=(tiles,), in_specs=in_specs, out_specs=[colum...  22 us
    pallas_call x2, Pallas kernels, attend_forward(): pl.pallas_call(kernel, grid=(heads // 2,), in_specs=[pair_of(q, q_role),...  17.6 us
  transfers between devices with their start and end apart: 77, of which 30 were waited for; matrix products, arithmetic and copies ran while one was open for 17% of the time, Pallas kernels for 21%

profile of v3, /device:TPU:0, one launch (start us, length us, event | category | flops | bytes accessed | tf_op | source)
XLA Modules:
  0.0 493.8 jit_solution(13347492858641405958)
XLA Ops:
  15.5 3.0 collective-permute-start
  19.2 3.1 collective-permute-start.2
  36.7 8.1 %collective-permute-done.3 = bf16[96,1280]{1,0:T(8,128)(2,1)S(1)} collective-permute-done((bf16[96,1280]{1,0:T(8,128)(2,1)S(1)}, bf16[96,1280]{1,0:T(8,128)(2,1)S(1)}, u32[]{:S(2)}, u32[]{:S(2)}) %collective-permute-start.3) | collective-permute-done | bytes 245792 | tf_op jit(solution)/shard_map/ppermute | solution.py:628
  61.2 9.3 %collective-permute-done.6 = bf16[48,1920]{1,0:T(8,128)(2,1)} collective-permute-done((bf16[48,1920]{1,0:T(8,128)(2,1)}, bf16[48,1920]{1,0:T(8,128)(2,1)}, u32[]{:S(2)}, u32[]{:S(2)}) %collective-permute-start.6) | collective-permute-done | bytes 184352 | tf_op jit(solution)/shard_map/ppermute | solution.py:628
  76.2 6.0 %collective-permute-done.7.refs_5_ = bf16[96,1280]{1,0:T(8,128)(2,1)S(1)} collective-permute-done((bf16[96,1280]{1,0:T(8,128)(2,1)S(1)}, bf16[96,1280]{1,0:T(8,128)(2,1)S(1)}, u32[]{:S(2)}, u32[]{:S(2)}) %collective-permute-start.7) | collective-permute-done | bytes 245792 | tf_op jit(solution)/shard_map/ppermute | solution.py:628
  85.2 3.9 collective-permute-done.8.refs_6_
  94.6 11.4 %collective-permute-done.15 = bf16[48,1536]{1,0:T(8,128)(2,1)} collective-permute-done((bf16[48,1536]{1,0:T(8,128)(2,1)}, bf16[48,1536]{1,0:T(8,128)(2,1)}, u32[]{:S(2)}, u32[]{:S(2)}) %collective-permute-start.15) | collective-permute-done | bytes 147488 | tf_op jit(solution)/shard_map/ppermute | solution.py:628
  107.1 4.8 shard_map.349.q_ref.k_ref.v_ref
  112.0 9.8 %shard_map.350 = (bf16[512,768]{1,0:T(8,128)(2,1)}, bf16[12,512,512]{2,1,0:T(8,128)(2,1)S(1)}) custom-call(bf16[3,512,768]{2,1,0:T(8,128)(2,1)S(1)} %shard_map.349.q_ref.k_ref.v_ref, bf16[3,512,768]{2,1,0:T(8,128)(2,1)S(1)} %shard_map.349.q_ref.k_ref.v_ref, bf16[3,512,768]{2,1,0:T(8,128)(2,1)S(1)} %shard_map.349.q_ref.k_ref.v_ref, ...), custom_call_target="tpu_custom_call" | custom-call | flops 3221225472 | bytes 6291456 | tf_op jit(solution)/shard_map/pallas_call | solution.py:431
  121.9 2.6 copy-done.81
  134.3 7.0 %collective-permute-done.18.refs_5_ = bf16[96,1920]{1,0:T(8,128)(2,1)S(1)} collective-permute-done((bf16[96,1920]{1,0:T(8,128)(2,1)S(1)}, bf16[96,1920]{1,0:T(8,128)(2,1)S(1)}, u32[]{:S(2)}, u32[]{:S(2)}) %collective-permute-start.18) | collective-permute-done | bytes 368672 | tf_op jit(solution)/shard_map/ppermute | solution.py:628
  144.9 3.6 shard_map.351
  149.2 7.1 %shard_map.352 = (bf16[4,512,768]{2,1,0:T(8,128)(2,1)S(1)}, bf16[4,512,768]{2,1,0:T(8,128)(2,1)S(1)}) custom-call(bf16[512,768]{1,0:T(8,128)(2,1)S(1)} %get-tuple-element.609.x_ref.refs_0_, bf16[192,1920]{1,0:T(8,128)(2,1)} %copy-done.92, bf16[192,1920]{1,0:T(8,128)(2,1)} %copy-done.90, bf16[192,1920]{1,0:T(8,128)(2,1)} %copy-done.93, ...), custom_call_target="tpu_custom_call" | custom-call | flops 2415919104 | bytes 11010048 | tf_op jit(solution)/shard_map/pallas_call | solution.py:155
  165.2 7.2 %collective-permute-done.28.refs_5_ = bf16[96,1536]{1,0:T(8,128)(2,1)S(1)} collective-permute-done((bf16[96,1536]{1,0:T(8,128)(2,1)}, bf16[96,1536]{1,0:T(8,128)(2,1)S(1)}, u32[]{:S(2)}, u32[]{:S(2)}) %collective-permute-start.28) | collective-permute-done | bytes 294944 | tf_op jit(solution)/shard_map/ppermute | solution.py:628
  179.2 6.3 %shard_map.353 = (f32[512,768]{1,0:T(8,128)S(1)}, f32[512,1]{1,0:T(8,128)S(1)}, bf16[512,768]{1,0:T(8,128)(2,1)S(1)}, bf16[512,384]{1,0:T(8,128)(2,1)S(1)}) custom-call(bf16[4,512,768]{2,1,0:T(8,128)(2,1)S(1)} %copy-done.9, bf16[192,1536]{1,0:T(8,128)(2,1)} %constant_dynamic-update-slice_fusion.9.refs_0_, bf16[192,1536]{1,0:T(8,128)(2,1)} %copy-done.98, ...), custom_call_target="tpu_custom_call" | custom-call | flops 2415919104 | bytes 12582912 | tf_op jit(solution)/shard_map/pallas_call | solution.py:255
  187.9 2.4 shard_map.355.k_ref.v_ref
  190.4 2.4 shard_map.354.q_ref
  192.8 7.8 %shard_map.356 = (bf16[512,768]{1,0:T(8,128)(2,1)S(1)}, bf16[12,512,256]{2,1,0:T(8,128)(2,1)S(1)}) custom-call(bf16[1,512,768]{2,1,0:T(8,128)(2,1)S(1)} %shard_map.354.q_ref, bf16[2,256,768]{2,1,0:T(8,128)(2,1)S(1)} %shard_map.355.k_ref.v_ref, bf16[2,256,768]{2,1,0:T(8,128)(2,1)S(1)} %shard_map.355.k_ref.v_ref, bf16[512,128]{1,0:T(8,128)(2,1)S(1)} %copy-done.58, ...), custom_call_target="tpu_custom_call" | custom-call | flops 1610612736 | bytes 3145728 | tf_op jit(solution)/shard_map/pallas_call | solution.py:431
  202.3 3.6 shard_map.357
  205.9 6.4 %shard_map.358 = (bf16[4,512,768]{2,1,0:T(8,128)(2,1)S(1)}, bf16[4,512,768]{2,1,0:T(8,128)(2,1)S(1)}) custom-call(bf16[512,768]{1,0:T(8,128)(2,1)S(1)} %get-tuple-element.675.x_ref.refs_2_, s32[2,16]{1,0:T(2,128)S(1)} %broadcast_add_fusion.refs_0_.places, bf16[32,48,4608]{2,1,0:T(8,128)(2,1)} %bitcast.148), custom_call_target="tpu_custom_call" | custom-call | flops 2415919104 | bytes 11010048 | tf_op jit(solution)/shard_map/pallas_call | solution.py:155
  212.3 7.8 %shard_map.359 = (bf16[512,768]{1,0:T(8,128)(2,1)S(1)}, f32[512,768]{1,0:T(8,128)S(1)}, bf16[512,768]{1,0:T(8,128)(2,1)S(1)}, bf16[512,384]{1,0:T(8,128)(2,1)}, f32[2,768]{1,0:T(2,128)S(1)}) custom-call(bf16[4,512,768]{2,1,0:T(8,128)(2,1)S(1)} %get-tuple-element.679.h_ref.refs_1_, s32[2,16]{1,0:T(2,128)S(1)} %broadcast_add_fusion.refs_0_.places, ...), custom_call_target="tpu_custom_call" | custom-call | flops 2415919104 | bytes 12582912 | tf_op jit(solution)/shard_map/pallas_call | solution.py:255
  222.9 5.1 %shard_map.360.refs_3_.h_ref = bf16[4,512,768]{2,1,0:T(8,128)(2,1)S(1)} custom-call(bf16[512,768]{1,0:T(8,128)(2,1)S(1)} %get-tuple-element.690.x_ref.refs_0_, s32[2,16]{1,0:T(2,128)S(1)} %broadcast_add_fusion.refs_0_.places, bf16[32,48,4608]{2,1,0:T(8,128)(2,1)} %bitcast.150, bf16[4,512,768]{2,1,0:T(8,128)(2,1)S(1)} %get-tuple-element.691.refs_2_), custom_call_target="tpu_custom_call" | custom-call | flops 2415919104 | bytes 11010048 | tf_op jit(solution)/shard_map/pallas_call | solution.py:155
  228.0 6.6 %shard_map.362 = (f32[512,768]{1,0:T(8,128)S(1)}, bf16[512,768]{1,0:T(8,128)(2,1)S(1)}, bf16[512,384]{1,0:T(8,128)(2,1)S(1)}, f32[2,768]{1,0:T(2,128)S(1)}) custom-call(bf16[4,512,768]{2,1,0:T(8,128)(2,1)S(1)} %shard_map.360.refs_3_.h_ref, s32[2,16]{1,0:T(2,128)S(1)} %broadcast_add_fusion.refs_0_.places, bf16[32,48,4608]{2,1,0:T(8,128)(2,1)} %bitcast.151, ...), custom_call_target="tpu_custom_call" | custom-call | flops 2415919104 | bytes 12582912 | tf_op jit(solution)/shard_map/pallas_call | solution.py:255
  239.2 9.7 %shard_map.361 = bf16[32,48,3072]{2,1,0:T(8,128)(2,1)S(1)} custom-call(s32[2,16]{1,0:T(2,128)S(1)} %broadcast_add_fusion.refs_0_.places, bf16[512,768]{1,0:T(8,128)(2,1)S(1)} %get-tuple-element.690.x_ref.refs_0_, bf16[4,512,768]{2,1,0:T(8,128)(2,1)S(1)} %get-tuple-element.679.h_ref.refs_1_, bf16[512,768]{1,0:T(8,128)(2,1)S(1)} %get-tuple-element.675.x_ref.refs_2_, ...), custom_call_target="tpu_custom_call" | custom-call | flops 4831838208 | bytes 15728640 | tf_op jit(solution)/shard_map/pallas_call | solution.py:388
  249.0 3.7 copy-done.2
  263.2 8.7 %shard_map.364 = (bf16[1,512,768]{2,1,0:T(8,128)(2,1)S(1)}, bf16[2,256,768]{2,1,0:T(8,128)(2,1)S(1)}, f32[12,128,128]{2,1,0:T(8,128)S(1)}) custom-call(bf16[1,512,768]{2,1,0:T(8,128)(2,1)S(1)} %copy-done.31, bf16[2,256,768]{2,1,0:T(8,128)(2,1)S(1)} %copy-done.42, bf16[2,256,768]{2,1,0:T(8,128)(2,1)S(1)} %copy-done.42, bf16[512,768]{1,0:T(8,128)(2,1)S(1)} %bitcast.143, ...), custom_call_target="tpu_custom_call" | custom-call | flops 4026531840 | bytes 3145728 | tf_op jit(solution)/shard_map/pallas_call | solution.py:511
  272.0 2.9 shard_map.366
  276.1 2.8 shard_map.365
  280.1 5.8 %shard_map.367.h_ref.refs_2_ = bf16[4,512,768]{2,1,0:T(8,128)(2,1)S(1)} custom-call(bf16[512,768]{1,0:T(8,128)(2,1)S(1)} %get-tuple-element.740.x_ref.refs_12_, bf16[192,1536]{1,0:T(8,128)(2,1)} %constant_dynamic-update-slice_fusion.9.refs_0_, bf16[192,1536]{1,0:T(8,128)(2,1)} %copy-done.98, bf16[192,1536]{1,0:T(8,128)(2,1)} %copy-done.106, ...), custom_call_target="tpu_custom_call" | custom-call | flops 2415919104 | bytes 11010048 | tf_op jit(solution)/shard_map/pallas_call | solution.py:155
  287.6 2.9 collective-permute-done.41.refs_9_
  291.2 9.7 %shard_map.368 = (bf16[96,3072]{1,0:T(8,128)(2,1)S(1)}, bf16[96,3072]{1,0:T(8,128)(2,1)S(1)}, bf16[192,3072]{1,0:T(8,128)(2,1)S(1)}, bf16[192,3072]{1,0:T(8,128)(2,1)S(1)}, bf16[192,3072]{1,0:T(8,128)(2,1)S(1)}) custom-call(bf16[512,768]{1,0:T(8,128)(2,1)S(1)} %copy-done.25, bf16[512,384]{1,0:T(8,128)(2,1)} %collective-permute-done.38.refs_1_, ...), custom_call_target="tpu_custom_call" | custom-call | flops 4227858432 | bytes 18481152 | tf_op jit(solution)/shard_map/pallas_call | solution.py:336
  300.9 7.7 %shard_map.369 = (f32[512,768]{1,0:T(8,128)S(1)}, bf16[512,768]{1,0:T(8,128)(2,1)S(1)}, bf16[512,384]{1,0:T(8,128)(2,1)S(1)}, f32[2,768]{1,0:T(2,128)S(1)}) custom-call(bf16[4,512,768]{2,1,0:T(8,128)(2,1)S(1)} %shard_map.367.h_ref.refs_2_, bf16[192,1920]{1,0:T(8,128)(2,1)} %copy-done.92, bf16[192,1920]{1,0:T(8,128)(2,1)} %copy-done.90, ...), custom_call_target="tpu_custom_call" | custom-call | flops 2415919104 | bytes 12582912 | tf_op jit(solution)/shard_map/pallas_call | solution.py:255
  309.9 2.6 shard_map.370
  325.9 6.0 %collective-permute-done.45 = bf16[96,3072]{1,0:T(8,128)(2,1)} collective-permute-done((bf16[96,3072]{1,0:T(8,128)(2,1)}, bf16[96,3072]{1,0:T(8,128)(2,1)}, u32[]{:S(2)}, u32[]{:S(2)}) %collective-permute-start.45) | collective-permute-done | bytes 589856 | tf_op jit(solution)/shard_map/ppermute | solution.py:628
  332.9 2.5 add_dynamic-update-slice_fusion
  339.4 3.1 copy-done.82
  342.5 14.3 %shard_map.371 = (bf16[3,512,768]{2,1,0:T(8,128)(2,1)}, f32[12,128,128]{2,1,0:T(8,128)S(1)}) custom-call(bf16[3,512,768]{2,1,0:T(8,128)(2,1)S(1)} %copy-done.14, bf16[3,512,768]{2,1,0:T(8,128)(2,1)S(1)} %copy-done.14, bf16[3,512,768]{2,1,0:T(8,128)(2,1)S(1)} %copy-done.14, bf16[512,768]{1,0:T(8,128)(2,1)S(1)} %bitcast.144, ...), custom_call_target="tpu_custom_call" | custom-call | flops 8053063680 | bytes 6291456 | tf_op jit(solution)/shard_map/pallas_call | solution.py:511
  359.4 7.4 %shard_map.372 = (bf16[96,1920]{1,0:T(8,128)(2,1)S(1)}, bf16[96,1920]{1,0:T(8,128)(2,1)S(1)}, bf16[192,1920]{1,0:T(8,128)(2,1)S(1)}, bf16[192,1920]{1,0:T(8,128)(2,1)S(1)}, bf16[192,1920]{1,0:T(8,128)(2,1)S(1)}) custom-call(bf16[512,768]{1,0:T(8,128)(2,1)S(1)} %copy-done.71, bf16[512,384]{1,0:T(8,128)(2,1)} %collective-permute-done.48.refs_1_, ...), custom_call_target="tpu_custom_call" | custom-call | flops 3019898880 | bytes 12386304 | tf_op jit(solution)/shard_map/pallas_call | solution.py:336
  370.8 5.4 %shard_map.373 = bf16[512,768]{1,0:T(8,128)(2,1)S(1)} custom-call(bf16[3,512,768]{2,1,0:T(8,128)(2,1)} %get-tuple-element.855.h_ref.refs_2_, bf16[192,1280]{1,0:T(8,128)(2,1)} %constant_dynamic-update-slice_fusion.3.refs_0_, bf16[192,1280]{1,0:T(8,128)(2,1)} %collective-permute-done.4.refs_1_, bf16[192,1280]{1,0:T(8,128)(2,1)} %copy-done.107, ...), custom_call_target="tpu_custom_call" | custom-call | flops 1811939328 | bytes 10616832 | tf_op jit(solution)/shard_map/pallas_call | solution.py:255
  380.7 4.8 collective-permute-done.56
  393.6 14.9 %collective-permute-done.55 = bf16[96,3072]{1,0:T(8,128)(2,1)} collective-permute-done((bf16[96,3072]{1,0:T(8,128)(2,1)}, bf16[96,3072]{1,0:T(8,128)(2,1)}, u32[]{:S(2)}, u32[]{:S(2)}) %collective-permute-start.55) | collective-permute-done | bytes 589856 | tf_op jit(solution)/shard_map/ppermute | solution.py:628
  411.2 4.9 %shard_map.374 = (bf16[96,1152]{1,0:T(8,128)(2,1)S(1)}, bf16[96,1152]{1,0:T(8,128)(2,1)S(1)}, bf16[192,1152]{1,0:T(8,128)(2,1)S(1)}, bf16[192,1152]{1,0:T(8,128)(2,1)S(1)}, bf16[192,1152]{1,0:T(8,128)(2,1)S(1)}) custom-call(bf16[512,768]{1,0:T(8,128)(2,1)S(1)} %copy-done.7, bf16[512,384]{1,0:T(8,128)(2,1)} %collective-permute-done.50.refs_1_, ...), custom_call_target="tpu_custom_call" | custom-call | flops 1811939328 | bytes 7274496 | tf_op jit(solution)/shard_map/pallas_call | solution.py:336
  436.0 3.9 collective-permute-done.69
  442.3 2.8 collective-permute-start.72
  445.5 4.2 collective-permute-done.66
  451.4 4.6 collective-permute-done.71
  464.6 8.2 %collective-permute-done.73 = bf16[48,1152]{1,0:T(8,128)(2,1)S(1)} collective-permute-done((bf16[48,1152]{1,0:T(8,128)(2,1)S(1)}, bf16[48,1152]{1,0:T(8,128)(2,1)S(1)}, u32[]{:S(2)}, u32[]{:S(2)}) %collective-permute-start.73) | collective-permute-done | bytes 110624 | tf_op jit(solution)/shard_map/ppermute | solution.py:628
  472.8 6.5 %reduce-scatter.2.cloned.1.call-done = bf16[48,3072]{1,0:T(8,128)(2,1)} async-done(((bf16[1536,3072]{1,0:T(8,128)(2,1)}), bf16[48,3072]{1,0:T(8,128)(2,1)}) %reduce-scatter.2.cloned.1.call-update) | async-done | bytes 294928 | tf_op jit(solution)/shard_map/reduce_scatter | solution.py:718
  (599 shorter events, 190.7 us)
Async XLA Ops:
  7.3 180.6 %all-gather.3.cloned.1.call-start = ((), (), s32[]{:S(2)}) async-start(), calls=%async_computation.2 | async-start | bytes 14598144 | tf_op jit(solution)/shard_map/all_gather | solution.py:704
  14.0 465.4 %reduce-scatter.2.cloned.1.call-start = ((), (), s32[]{:S(2)}) async-start(), calls=%async_computation.1 | async-start | bytes 9732096 | tf_op jit(solution)/shard_map/reduce_scatter | solution.py:718
  15.5 35.0 %collective-permute-start = (bf16[2,6,2,31]{3,2,1,0:T(2,128)(2,1)}, bf16[2,6,2,31]{3,2,1,0:T(2,128)(2,1)}, u32[]{:S(2)}, u32[]{:S(2)}) collective-permute-start(bf16[2,6,2,31]{3,2,1,0:T(2,128)(2,1)} %pad_maximum_fusion.7), channel_id=1, source_target_pairs={{0,1},{1,0},{2,3},{3,2},{4,5},{5,4},{6,7},{7,6},{8,9},{9,8},{10,11... | collective-permute-start | bytes 4472 | tf_op jit(solution)/shard_map/ppermute | solution.py:628
  19.2 31.3 %collective-permute-start.1 = (bf16[256,768]{1,0:T(8,128)(2,1)}, bf16[256,768]{1,0:T(8,128)(2,1)}, u32[]{:S(2)}, u32[]{:S(2)}) collective-permute-start(bf16[256,768]{1,0:T(8,128)(2,1)} %select_bitcast_fusion.4), channel_id=1, source_target_pairs={{0,1},{1,0},{2,3},{3,2},{4,5},{5,4},{6,7},{7,6},{8,9},{9,8},{10,11... | collective-permute-start | bytes 1179656 | tf_op jit(solution)/shard_map/ppermute | solution.py:628
  19.2 11.9 %collective-permute-start.2 = (bf16[48,1280]{1,0:T(8,128)(2,1)}, bf16[48,1280]{1,0:T(8,128)(2,1)}, u32[]{:S(2)}, u32[]{:S(2)}) collective-permute-start(bf16[48,1280]{1,0:T(8,128)(2,1)} %fusion.33), channel_id=1, source_target_pairs={{0,16},{1,17},{2,18},{3,19},{4,20},{5,21},{6,22},{7,23},{8,24},{9,... | collective-permute-start | bytes 368648 | tf_op jit(solution)/shard_map/ppermute | solution.py:628
  32.1 12.6 %collective-permute-start.3 = (bf16[96,1280]{1,0:T(8,128)(2,1)S(1)}, bf16[96,1280]{1,0:T(8,128)(2,1)S(1)}, u32[]{:S(2)}, u32[]{:S(2)}) collective-permute-start(bf16[96,1280]{1,0:T(8,128)(2,1)S(1)} %pad_maximum_fusion.3), channel_id=1, source_target_pairs={{0,8},{1,9},{2,10},{3,11},{4,12},{5,13},{6,14},{7,15},{8,0},{9,1},... | collective-permute-start | bytes 737288 | tf_op jit(solution)/shard_map/ppermute | solution.py:628
  46.8 25.4 %collective-permute-start.4 = (bf16[192,1280]{1,0:T(8,128)(2,1)}, bf16[192,1280]{1,0:T(8,128)(2,1)}, u32[]{:S(2)}, u32[]{:S(2)}) collective-permute-start(bf16[192,1280]{1,0:T(8,128)(2,1)} %constant_dynamic-update-slice_fusion.3.refs_0_), channel_id=1, source_target_pairs={{0,4},{1,5},{2,6},{3,7},{4,0},{5,1},{6,2},{7,3},{8,12},{9,13},{10,... | collective-permute-start | bytes 1474568 | tf_op jit(solution)/shard_map/ppermute | solution.py:628
  48.3 23.9 %collective-permute-start.5 = (bf16[192,1280]{1,0:T(8,128)(2,1)}, bf16[192,1280]{1,0:T(8,128)(2,1)}, u32[]{:S(2)}, u32[]{:S(2)}) collective-permute-start(bf16[192,1280]{1,0:T(8,128)(2,1)} %constant_dynamic-update-slice_fusion.3.refs_0_), channel_id=1, source_target_pairs={{0,1},{1,0},{2,3},{3,2},{4,5},{5,4},{6,7},{7,6},{8,9},{9,8},{10,11... | collective-permute-start | bytes 1474568 | tf_op jit(solution)/shard_map/ppermute | solution.py:628
  50.5 20.0 %collective-permute-start.6 = (bf16[48,1920]{1,0:T(8,128)(2,1)}, bf16[48,1920]{1,0:T(8,128)(2,1)}, u32[]{:S(2)}, u32[]{:S(2)}) collective-permute-start(bf16[48,1920]{1,0:T(8,128)(2,1)} %pad_maximum_fusion.4), channel_id=1, source_target_pairs={{0,16},{1,17},{2,18},{3,19},{4,20},{5,21},{6,22},{7,23},{8,24},{9,... | collective-permute-start | bytes 552968 | tf_op jit(solution)/shard_map/ppermute | solution.py:628
  75.1 14.0 %collective-permute-start.9 = (bf16[192,1280]{1,0:T(8,128)(2,1)}, bf16[192,1280]{1,0:T(8,128)(2,1)S(1)}, u32[]{:S(2)}, u32[]{:S(2)}) collective-permute-start(bf16[192,1280]{1,0:T(8,128)(2,1)} %constant_dynamic-update-slice_fusion.3.refs_0_), channel_id=1, source_target_pairs={{0,2},{1,3},{2,0},{3,1},{4,6},{5,7},{6,4},{7,5},{8,10},{9,11},{10,... | collective-permute-start | bytes 1474568 | tf_op jit(solution)/shard_map/ppermute | solution.py:628
  75.1 14.0 %collective-permute-start.10 = (bf16[192,1280]{1,0:T(8,128)(2,1)}, bf16[192,1280]{1,0:T(8,128)(2,1)}, u32[]{:S(2)}, u32[]{:S(2)}) collective-permute-start(bf16[192,1280]{1,0:T(8,128)(2,1)} %collective-permute-done.4.refs_1_), channel_id=1, source_target_pairs={{0,2},{1,3},{2,0},{3,1},{4,6},{5,7},{6,4},{7,5},{8,10},{9,11},{10,... | collective-permute-start | bytes 1474568 | tf_op jit(solution)/shard_map/ppermute | solution.py:628
  75.6 13.5 %collective-permute-start.11 = (bf16[192,1280]{1,0:T(8,128)(2,1)}, bf16[192,1280]{1,0:T(8,128)(2,1)}, u32[]{:S(2)}, u32[]{:S(2)}) collective-permute-start(bf16[192,1280]{1,0:T(8,128)(2,1)} %collective-permute-done.5.refs_4_), channel_id=1, source_target_pairs={{0,2},{1,3},{2,0},{3,1},{4,6},{5,7},{6,4},{7,5},{8,10},{9,11},{10,... | collective-permute-start | bytes 1474568 | tf_op jit(solution)/shard_map/ppermute | solution.py:628
  76.1 13.6 %collective-permute-start.14 = (bf16[96,1920]{1,0:T(8,128)(2,1)}, bf16[96,1920]{1,0:T(8,128)(2,1)}, u32[]{:S(2)}, u32[]{:S(2)}) collective-permute-start(bf16[96,1920]{1,0:T(8,128)(2,1)} %pad_maximum_fusion.1), channel_id=1, source_target_pairs={{0,8},{1,9},{2,10},{3,11},{4,12},{5,13},{6,14},{7,15},{8,0},{9,1},... | collective-permute-start | bytes 1105928 | tf_op jit(solution)/shard_map/ppermute | solution.py:628
  89.1 16.9 %collective-permute-start.15 = (bf16[48,1536]{1,0:T(8,128)(2,1)}, bf16[48,1536]{1,0:T(8,128)(2,1)}, u32[]{:S(2)}, u32[]{:S(2)}) collective-permute-start(bf16[48,1536]{1,0:T(8,128)(2,1)} %bitcast.10), channel_id=1, source_target_pairs={{0,16},{1,17},{2,18},{3,19},{4,20},{5,21},{6,22},{7,23},{8,24},{9,... | collective-permute-start | bytes 442376 | tf_op jit(solution)/shard_map/ppermute | solution.py:628
  91.8 34.9 %collective-permute-start.16 = (bf16[192,1920]{1,0:T(8,128)(2,1)S(1)}, bf16[192,1920]{1,0:T(8,128)(2,1)S(1)}, u32[]{:S(2)}, u32[]{:S(2)}) collective-permute-start(bf16[192,1920]{1,0:T(8,128)(2,1)S(1)} %constant_dynamic-update-slice_fusion.6.refs_0_), channel_id=1, source_target_pairs={{0,4},{1,5},{2,6},{3,7},{4,0},{5,1},{6,2},{7,3},{8,12},{9,13},{10,... | collective-permute-start | bytes 2211848 | tf_op jit(solution)/shard_map/ppermute | solution.py:628
  93.3 34.7 %collective-permute-start.17 = (bf16[192,1920]{1,0:T(8,128)(2,1)S(1)}, bf16[192,1920]{1,0:T(8,128)(2,1)S(1)}, u32[]{:S(2)}, u32[]{:S(2)}) collective-permute-start(bf16[192,1920]{1,0:T(8,128)(2,1)S(1)} %constant_dynamic-update-slice_fusion.6.refs_0_), channel_id=1, source_target_pairs={{0,1},{1,0},{2,3},{3,2},{4,5},{5,4},{6,7},{7,6},{8,9},{9,8},{10,11... | collective-permute-start | bytes 2211848 | tf_op jit(solution)/shard_map/ppermute | solution.py:628
  111.9 19.0 %collective-permute-start.23 = (bf16[96,1536]{1,0:T(8,128)(2,1)S(1)}, bf16[96,1536]{1,0:T(8,128)(2,1)S(1)}, u32[]{:S(2)}, u32[]{:S(2)}) collective-permute-start(bf16[96,1536]{1,0:T(8,128)(2,1)S(1)} %pad_maximum_fusion.2), channel_id=1, source_target_pairs={{0,8},{1,9},{2,10},{3,11},{4,12},{5,13},{6,14},{7,15},{8,0},{9,1},... | collective-permute-start | bytes 884744 | tf_op jit(solution)/shard_map/ppermute | solution.py:628
  128.1 13.5 %collective-permute-start.20 = (bf16[192,1920]{1,0:T(8,128)(2,1)S(1)}, bf16[192,1920]{1,0:T(8,128)(2,1)S(1)}, u32[]{:S(2)}, u32[]{:S(2)}) collective-permute-start(bf16[192,1920]{1,0:T(8,128)(2,1)S(1)} %constant_dynamic-update-slice_fusion.6.refs_0_), channel_id=1, source_target_pairs={{0,2},{1,3},{2,0},{3,1},{4,6},{5,7},{6,4},{7,5},{8,10},{9,11},{10,... | collective-permute-start | bytes 2211848 | tf_op jit(solution)/shard_map/ppermute | solution.py:628
  128.2 13.4 %collective-permute-start.21 = (bf16[192,1920]{1,0:T(8,128)(2,1)S(1)}, bf16[192,1920]{1,0:T(8,128)(2,1)S(1)}, u32[]{:S(2)}, u32[]{:S(2)}) collective-permute-start(bf16[192,1920]{1,0:T(8,128)(2,1)S(1)} %collective-permute-done.16.refs_1_), channel_id=1, source_target_pairs={{0,2},{1,3},{2,0},{3,1},{4,6},{5,7},{6,4},{7,5},{8,10},{9,11},{10,... | collective-permute-start | bytes 2211848 | tf_op jit(solution)/shard_map/ppermute | solution.py:628
  128.7 12.9 %collective-permute-start.22 = (bf16[192,1920]{1,0:T(8,128)(2,1)S(1)}, bf16[192,1920]{1,0:T(8,128)(2,1)S(1)}, u32[]{:S(2)}, u32[]{:S(2)}) collective-permute-start(bf16[192,1920]{1,0:T(8,128)(2,1)S(1)} %collective-permute-done.17.refs_4_), channel_id=1, source_target_pairs={{0,2},{1,3},{2,0},{3,1},{4,6},{5,7},{6,4},{7,5},{8,10},{9,11},{10,... | collective-permute-start | bytes 2211848 | tf_op jit(solution)/shard_map/ppermute | solution.py:628
  130.3 10.9 %collective-permute-start.18 = (bf16[96,1920]{1,0:T(8,128)(2,1)S(1)}, bf16[96,1920]{1,0:T(8,128)(2,1)S(1)}, u32[]{:S(2)}, u32[]{:S(2)}) collective-permute-start(bf16[96,1920]{1,0:T(8,128)(2,1)S(1)} %slice.252), channel_id=1, source_target_pairs={{0,4},{1,5},{2,6},{3,7},{4,0},{5,1},{6,2},{7,3},{8,12},{9,13},{10,... | collective-permute-start | bytes 1105928 | tf_op jit(solution)/shard_map/ppermute | solution.py:628
  142.2 17.4 %collective-permute-start.26 = (bf16[192,1536]{1,0:T(8,128)(2,1)}, bf16[192,1536]{1,0:T(8,128)(2,1)S(1)}, u32[]{:S(2)}, u32[]{:S(2)}) collective-permute-start(bf16[192,1536]{1,0:T(8,128)(2,1)} %constant_dynamic-update-slice_fusion.9.refs_0_), channel_id=1, source_target_pairs={{0,4},{1,5},{2,6},{3,7},{4,0},{5,1},{6,2},{7,3},{8,12},{9,13},{10,... | collective-permute-start | bytes 1769480 | tf_op jit(solution)/shard_map/ppermute | solution.py:628
  143.7 15.9 %collective-permute-start.27 = (bf16[192,1536]{1,0:T(8,128)(2,1)}, bf16[192,1536]{1,0:T(8,128)(2,1)}, u32[]{:S(2)}, u32[]{:S(2)}) collective-permute-start(bf16[192,1536]{1,0:T(8,128)(2,1)} %constant_dynamic-update-slice_fusion.9.refs_0_), channel_id=1, source_target_pairs={{0,1},{1,0},{2,3},{3,2},{4,5},{5,4},{6,7},{7,6},{8,9},{9,8},{10,11... | collective-permute-start | bytes 1769480 | tf_op jit(solution)/shard_map/ppermute | solution.py:628
  162.2 11.2 %collective-permute-start.30 = (bf16[192,1536]{1,0:T(8,128)(2,1)}, bf16[192,1536]{1,0:T(8,128)(2,1)S(1)}, u32[]{:S(2)}, u32[]{:S(2)}) collective-permute-start(bf16[192,1536]{1,0:T(8,128)(2,1)} %constant_dynamic-update-slice_fusion.9.refs_0_), channel_id=1, source_target_pairs={{0,2},{1,3},{2,0},{3,1},{4,6},{5,7},{6,4},{7,5},{8,10},{9,11},{10,... | collective-permute-start | bytes 1769480 | tf_op jit(solution)/shard_map/ppermute | solution.py:628
  162.2 11.2 %collective-permute-start.31 = (bf16[192,1536]{1,0:T(8,128)(2,1)S(1)}, bf16[192,1536]{1,0:T(8,128)(2,1)}, u32[]{:S(2)}, u32[]{:S(2)}) collective-permute-start(bf16[192,1536]{1,0:T(8,128)(2,1)S(1)} %collective-permute-done.26.refs_1_), channel_id=1, source_target_pairs={{0,2},{1,3},{2,0},{3,1},{4,6},{5,7},{6,4},{7,5},{8,10},{9,11},{10,... | collective-permute-start | bytes 1769480 | tf_op jit(solution)/shard_map/ppermute | solution.py:628
  221.9 30.7 %collective-permute-start.35 = (bf16[256,768]{1,0:T(8,128)(2,1)}, bf16[256,768]{1,0:T(8,128)(2,1)}, u32[]{:S(2)}, u32[]{:S(2)}) collective-permute-start(bf16[256,768]{1,0:T(8,128)(2,1)} %get-tuple-element.689), channel_id=1, source_target_pairs={{0,1},{1,0},{2,3},{3,2},{4,5},{5,4},{6,7},{7,6},{8,9},{9,8},{10,11... | collective-permute-start | bytes 1179656 | tf_op jit(solution)/shard_map/ppermute | solution.py:628
  252.6 19.3 %collective-permute-start.37 = (bf16[4,512,768]{2,1,0:T(8,128)(2,1)}, bf16[4,512,768]{2,1,0:T(8,128)(2,1)}, u32[]{:S(2)}, u32[]{:S(2)}) collective-permute-start(bf16[4,512,768]{2,1,0:T(8,128)(2,1)} %copy-done.8), channel_id=1, source_target_pairs={{0,2},{1,3},{2,0},{3,1},{4,6},{5,7},{6,4},{7,5},{8,10},{9,11},{10,... | collective-permute-start | bytes 9437192 | tf_op jit(solution)/shard_map/ppermute | solution.py:628
  252.6 19.3 %collective-permute-start.39 = (bf16[1,512,768]{2,1,0:T(8,128)(2,1)}, bf16[1,512,768]{2,1,0:T(8,128)(2,1)}, u32[]{:S(2)}, u32[]{:S(2)}) collective-permute-start(bf16[1,512,768]{2,1,0:T(8,128)(2,1)} %bitcast.141), channel_id=1, source_target_pairs={{0,2},{1,3},{2,0},{3,1},{4,6},{5,7},{6,4},{7,5},{8,10},{9,11},{10,... | collective-permute-start | bytes 2359304 | tf_op jit(solution)/shard_map/ppermute | solution.py:628
  253.1 18.8 %collective-permute-start.38 = (bf16[512,384]{1,0:T(8,128)(2,1)}, bf16[512,384]{1,0:T(8,128)(2,1)}, u32[]{:S(2)}, u32[]{:S(2)}) collective-permute-start(bf16[512,384]{1,0:T(8,128)(2,1)} %copy-done.78), channel_id=1, source_target_pairs={{0,2},{1,3},{2,0},{3,1},{4,6},{5,7},{6,4},{7,5},{8,10},{9,11},{10,... | collective-permute-start | bytes 1179656 | tf_op jit(solution)/shard_map/ppermute | solution.py:628
  254.8 17.1 %collective-permute-start.36 = (bf16[256,384]{1,0:T(8,128)(2,1)}, bf16[256,384]{1,0:T(8,128)(2,1)S(1)}, u32[]{:S(2)}, u32[]{:S(2)}) collective-permute-start(bf16[256,384]{1,0:T(8,128)(2,1)} %slice.259), channel_id=1, source_target_pairs={{0,2},{1,3},{2,0},{3,1},{4,6},{5,7},{6,4},{7,5},{8,10},{9,11},{10,... | collective-permute-start | bytes 589832 | tf_op jit(solution)/shard_map/ppermute | solution.py:628
  315.8 16.0 %collective-permute-start.45 = (bf16[96,3072]{1,0:T(8,128)(2,1)}, bf16[96,3072]{1,0:T(8,128)(2,1)}, u32[]{:S(2)}, u32[]{:S(2)}) collective-permute-start(bf16[96,3072]{1,0:T(8,128)(2,1)} %copy-done.73), channel_id=1, source_target_pairs={{0,4},{1,5},{2,6},{3,7},{4,0},{5,1},{6,2},{7,3},{8,12},{9,13},{10,... | collective-permute-start | bytes 1769480 | tf_op jit(solution)/shard_map/ppermute | solution.py:628
  317.3 15.6 %collective-permute-start.46 = (bf16[96,3072]{1,0:T(8,128)(2,1)}, bf16[96,3072]{1,0:T(8,128)(2,1)}, u32[]{:S(2)}, u32[]{:S(2)}) collective-permute-start(bf16[96,3072]{1,0:T(8,128)(2,1)} %copy-done.72), channel_id=1, source_target_pairs={{0,1},{1,0},{2,3},{3,2},{4,5},{5,4},{6,7},{7,6},{8,9},{9,8},{10,11... | collective-permute-start | bytes 1769480 | tf_op jit(solution)/shard_map/ppermute | solution.py:628
  337.8 31.6 %collective-permute-start.51 = (bf16[192,3072]{1,0:T(8,128)(2,1)}, bf16[192,3072]{1,0:T(8,128)(2,1)S(1)}, u32[]{:S(2)}, u32[]{:S(2)}) collective-permute-start(bf16[192,3072]{1,0:T(8,128)(2,1)} %add_dynamic-update-slice_fusion), channel_id=1, source_target_pairs={{0,4},{1,5},{2,6},{3,7},{4,0},{5,1},{6,2},{7,3},{8,12},{9,13},{10,... | collective-permute-start | bytes 3538952 | tf_op jit(solution)/shard_map/ppermute | solution.py:628
  338.4 31.0 %collective-permute-start.52 = (bf16[192,3072]{1,0:T(8,128)(2,1)}, bf16[192,3072]{1,0:T(8,128)(2,1)S(1)}, u32[]{:S(2)}, u32[]{:S(2)}) collective-permute-start(bf16[192,3072]{1,0:T(8,128)(2,1)} %add_dynamic-update-slice_fusion.1), channel_id=1, source_target_pairs={{0,1},{1,0},{2,3},{3,2},{4,5},{5,4},{6,7},{7,6},{8,9},{9,8},{10,11... | collective-permute-start | bytes 3538952 | tf_op jit(solution)/shard_map/ppermute | solution.py:628
  366.8 18.7 %collective-permute-start.56 = (bf16[96,1920]{1,0:T(8,128)(2,1)S(1)}, bf16[96,1920]{1,0:T(8,128)(2,1)S(1)}, u32[]{:S(2)}, u32[]{:S(2)}) collective-permute-start(bf16[96,1920]{1,0:T(8,128)(2,1)S(1)} %get-tuple-element.837), channel_id=1, source_target_pairs={{0,4},{1,5},{2,6},{3,7},{4,0},{5,1},{6,2},{7,3},{8,12},{9,13},{10,... | collective-permute-start | bytes 1105928 | tf_op jit(solution)/shard_map/ppermute | solution.py:628
  368.0 18.5 %collective-permute-start.57 = (bf16[96,1920]{1,0:T(8,128)(2,1)S(1)}, bf16[96,1920]{1,0:T(8,128)(2,1)S(1)}, u32[]{:S(2)}, u32[]{:S(2)}) collective-permute-start(bf16[96,1920]{1,0:T(8,128)(2,1)S(1)} %get-tuple-element.838), channel_id=1, source_target_pairs={{0,1},{1,0},{2,3},{3,2},{4,5},{5,4},{6,7},{7,6},{8,9},{9,8},{10,11... | collective-permute-start | bytes 1105928 | tf_op jit(solution)/shard_map/ppermute | solution.py:628
  377.8 31.7 %collective-permute-start.54 = (bf16[256,768]{1,0:T(8,128)(2,1)}, bf16[256,768]{1,0:T(8,128)(2,1)}, u32[]{:S(2)}, u32[]{:S(2)}) collective-permute-start(bf16[256,768]{1,0:T(8,128)(2,1)} %get-tuple-element.834), channel_id=1, source_target_pairs={{0,1},{1,0},{2,3},{3,2},{4,5},{5,4},{6,7},{7,6},{8,9},{9,8},{10,11... | collective-permute-start | bytes 1179656 | tf_op jit(solution)/shard_map/ppermute | solution.py:628
  378.4 30.0 %collective-permute-start.55 = (bf16[96,3072]{1,0:T(8,128)(2,1)}, bf16[96,3072]{1,0:T(8,128)(2,1)}, u32[]{:S(2)}, u32[]{:S(2)}) collective-permute-start(bf16[96,3072]{1,0:T(8,128)(2,1)} %get-tuple-element.835), channel_id=1, source_target_pairs={{0,8},{1,9},{2,10},{3,11},{4,12},{5,13},{6,14},{7,15},{8,0},{9,1},... | collective-permute-start | bytes 1769480 | tf_op jit(solution)/shard_map/ppermute | solution.py:628
  386.5 24.7 %collective-permute-start.58 = (bf16[3,512,768]{2,1,0:T(8,128)(2,1)}, bf16[3,512,768]{2,1,0:T(8,128)(2,1)}, u32[]{:S(2)}, u32[]{:S(2)}) collective-permute-start(bf16[3,512,768]{2,1,0:T(8,128)(2,1)} %get-tuple-element.855.h_ref.refs_2_), channel_id=1, source_target_pairs={{0,2},{1,3},{2,0},{3,1},{4,6},{5,7},{6,4},{7,5},{8,10},{9,11},{10,... | collective-permute-start | bytes 7077896 | tf_op jit(solution)/shard_map/ppermute | solution.py:628
  391.5 26.6 %collective-permute-start.62 = (bf16[192,1920]{1,0:T(8,128)(2,1)S(1)}, bf16[192,1920]{1,0:T(8,128)(2,1)S(1)}, u32[]{:S(2)}, u32[]{:S(2)}) collective-permute-start(bf16[192,1920]{1,0:T(8,128)(2,1)S(1)} %add_dynamic-update-slice_fusion.2), channel_id=1, source_target_pairs={{0,4},{1,5},{2,6},{3,7},{4,0},{5,1},{6,2},{7,3},{8,12},{9,13},{10,... | collective-permute-start | bytes 2211848 | tf_op jit(solution)/shard_map/ppermute | solution.py:628
  392.9 26.3 %collective-permute-start.63 = (bf16[192,1920]{1,0:T(8,128)(2,1)S(1)}, bf16[192,1920]{1,0:T(8,128)(2,1)S(1)}, u32[]{:S(2)}, u32[]{:S(2)}) collective-permute-start(bf16[192,1920]{1,0:T(8,128)(2,1)S(1)} %add_dynamic-update-slice_fusion.3), channel_id=1, source_target_pairs={{0,1},{1,0},{2,3},{3,2},{4,5},{5,4},{6,7},{7,6},{8,9},{9,8},{10,11... | collective-permute-start | bytes 2211848 | tf_op jit(solution)/shard_map/ppermute | solution.py:628
  409.6 15.0 %collective-permute-start.61 = (bf16[48,3072]{1,0:T(8,128)(2,1)S(1)}, bf16[48,3072]{1,0:T(8,128)(2,1)S(1)}, u32[]{:S(2)}, u32[]{:S(2)}) collective-permute-start(bf16[48,3072]{1,0:T(8,128)(2,1)S(1)} %fusion.14), channel_id=1, source_target_pairs={{0,16},{1,17},{2,18},{3,19},{4,20},{5,21},{6,22},{7,23},{8,24},{9,... | collective-permute-start | bytes 884744 | tf_op jit(solution)/shard_map/ppermute | solution.py:628
  423.1 16.8 %collective-permute-start.69 = (bf16[96,1920]{1,0:T(8,128)(2,1)}, bf16[96,1920]{1,0:T(8,128)(2,1)}, u32[]{:S(2)}, u32[]{:S(2)}) collective-permute-start(bf16[96,1920]{1,0:T(8,128)(2,1)} %get-tuple-element.900), channel_id=1, source_target_pairs={{0,8},{1,9},{2,10},{3,11},{4,12},{5,13},{6,14},{7,15},{8,0},{9,1},... | collective-permute-start | bytes 1105928 | tf_op jit(solution)/shard_map/ppermute | solution.py:628
  432.1 13.4 %collective-permute-start.65 = (bf16[192,1152]{1,0:T(8,128)(2,1)S(1)}, bf16[192,1152]{1,0:T(8,128)(2,1)S(1)}, u32[]{:S(2)}, u32[]{:S(2)}) collective-permute-start(bf16[192,1152]{1,0:T(8,128)(2,1)S(1)} %add_dynamic-update-slice_fusion.5), channel_id=1, source_target_pairs={{0,4},{1,5},{2,6},{3,7},{4,0},{5,1},{6,2},{7,3},{8,12},{9,13},{10,... | collective-permute-start | bytes 1327112 | tf_op jit(solution)/shard_map/ppermute | solution.py:628
  433.1 16.6 %collective-permute-start.66 = (bf16[192,1152]{1,0:T(8,128)(2,1)S(1)}, bf16[192,1152]{1,0:T(8,128)(2,1)S(1)}, u32[]{:S(2)}, u32[]{:S(2)}) collective-permute-start(bf16[192,1152]{1,0:T(8,128)(2,1)S(1)} %add_dynamic-update-slice_fusion.4), channel_id=1, source_target_pairs={{0,1},{1,0},{2,3},{3,2},{4,5},{5,4},{6,7},{7,6},{8,9},{9,8},{10,11... | collective-permute-start | bytes 1327112 | tf_op jit(solution)/shard_map/ppermute | solution.py:628
  440.9 15.1 %collective-permute-start.71 = (bf16[48,1920]{1,0:T(8,128)(2,1)S(1)}, bf16[48,1920]{1,0:T(8,128)(2,1)S(1)}, u32[]{:S(2)}, u32[]{:S(2)}) collective-permute-start(bf16[48,1920]{1,0:T(8,128)(2,1)S(1)} %fusion.18), channel_id=1, source_target_pairs={{0,16},{1,17},{2,18},{3,19},{4,20},{5,21},{6,22},{7,23},{8,24},{9,... | collective-permute-start | bytes 552968 | tf_op jit(solution)/shard_map/ppermute | solution.py:628
  449.8 11.1 %collective-permute-start.70 = (bf16[96,1152]{1,0:T(8,128)(2,1)S(1)}, bf16[96,1152]{1,0:T(8,128)(2,1)S(1)}, u32[]{:S(2)}, u32[]{:S(2)}) collective-permute-start(bf16[96,1152]{1,0:T(8,128)(2,1)S(1)} %get-tuple-element.911), channel_id=1, source_target_pairs={{0,8},{1,9},{2,10},{3,11},{4,12},{5,13},{6,14},{7,15},{8,0},{9,1},... | collective-permute-start | bytes 663560 | tf_op jit(solution)/shard_map/ppermute | solution.py:628
  461.0 11.8 %collective-permute-start.73 = (bf16[48,1152]{1,0:T(8,128)(2,1)S(1)}, bf16[48,1152]{1,0:T(8,128)(2,1)S(1)}, u32[]{:S(2)}, u32[]{:S(2)}) collective-permute-start(bf16[48,1152]{1,0:T(8,128)(2,1)S(1)} %fusion.26), channel_id=1, source_target_pairs={{0,16},{1,17},{2,18},{3,19},{4,20},{5,21},{6,22},{7,23},{8,24},{9,... | collective-permute-start | bytes 331784 | tf_op jit(solution)/shard_map/ppermute | solution.py:628
  (180 other events, 1288.3 us)
Sparse Core Ops, SparseCore 0:
  14.1 135.8 all-gather.2
  315.9 163.3 reduce-scatter.1

commit v4 on v3

--- a/solution.py
+++ b/solution.py
@@ -19,7 +19,7 @@
 mask_columns = (-29952.0, -48.0)
 bf16 = jnp.bfloat16
 f32 = jnp.float32
-vmem = pltpu.CompilerParams(vmem_limit_bytes=16 * 2**20)
+vmem = pltpu.CompilerParams(vmem_limit_bytes=24 * 2**20)
 
 
 def cast_low(values):
@@ -548,7 +548,7 @@
 GATHER, SCATTER = W1, G1
 
 ORDER = (
-    W1, PAGE, W1, W1, PAGE, W2, W2, W1, PAGE, W3, W1, W2, PAGE, W1, PAGE, W3, LAYERS, LAYERS,
+    W1, PAGE, W1, W1, PAGE, W2, W2, W1, PAGE, W3, W1, W2, PAGE, W1, PAGE, LAYERS, LAYERS, W3,
     LAYERS, W2, W3, W2, W2, LAYERS, LAYERS, W3, W3, W3, LAYERS, W4, LAYERS, LAYERS, LAYERS,
     LAYERS, LAYERS, LAYERS, LAYERS, -G1, OUT, -G2, LAYERS, G2, LAYERS, LAYERS, VISION, -G2, G2,
     LAYERS, -G3, G3, -G4, G4, G2, LAYERS, -G3, G3, G2, LAYERS, -G4, G3, G2, TEXT, G4, G3, SMALL,
@@ -717,7 +717,7 @@
             (out,) = yield [
                 lax.psum_scatter(parts, ("dp", "tensor"), scatter_dimension=0, tiled=True)
             ]
-            return out.astype(f32)
+            return out
         yield []
         flow = scatter_rows(names, "xy")
         next(flow)
@@ -997,7 +997,7 @@
         start = 0
         for name in group:
             size = pieces[name].shape[1]
-            grads[name] = results[flow][:, start : start + size]
+            grads[name] = results[flow][:, start : start + size].astype(f32)
             start += size
 
     return (

time: 502 us -> 498 us (level)
  transfers between devices with their start and end apart: 77 -> 77, of which waited for: 30 -> 31; matrix products, arithmetic and copies ran while one was open for 17% -> 17% of each run, Pallas kernels for 21% -> 21%
where the time goes in v4:
time: 498 us; the launch traced here: 491 us
  Pallas kernels  158 us (32%)
  waiting for transfers between devices  122 us (24%)
  local copies, waits for them, and re-layouts  87.3 us (18%)
  starting transfers between devices  58.1 us (12%)
  other arithmetic  38.3 us (8%)
  between operations  17.8 us (4%)
  matrix products  8.88 us (2%)
    ppermute x75, waiting for transfers between devices, swap(): return lax.ppermute(flows.mark(values), ('dp', 'tensor'), pairs)  116 us
    ppermute x75, starting transfers between devices, swap(): return lax.ppermute(flows.mark(values), ('dp', 'tensor'), pairs)  58 us
    unnamed x320, local copies, waits for them, and re-layouts  50.8 us
    pallas_call x9, Pallas kernels, project_back(): pl.pallas_call(kernel, grid=(tiles,), in_specs=[tile_of(h)] + weight.spec...  47 us
    pallas_call x9, Pallas kernels, project(): pl.pallas_call(kernel, grid=(weight.tiles,), in_specs=[whole(x)] + weight...  38.8 us
    pallas_call x2, Pallas kernels, attend_backward(): pl.pallas_call(kernel, grid=(heads // 2,), in_specs=[pair_of(q, q_role),...  23.2 us
    pallas_call x3, Pallas kernels, weight_grad(): pl.pallas_call(kernel, grid=(tiles,), in_specs=in_specs, out_specs=[colum...  22 us
    pallas_call x2, Pallas kernels, attend_forward(): pl.pallas_call(kernel, grid=(heads // 2,), in_specs=[pair_of(q, q_role),...  17.6 us
  transfers between devices with their start and end apart: 77, of which 31 were waited for; matrix products, arithmetic and copies ran while one was open for 17% of the time, Pallas kernels for 21%

profile of v4, /device:TPU:0, one launch (start us, length us, event | category | flops | bytes accessed | tf_op | source)
XLA Modules:
  0.0 490.6 jit_solution(16003675482044243411)
XLA Ops:
  15.4 3.0 collective-permute-start
  19.2 3.1 collective-permute-start.2
  36.6 8.0 %collective-permute-done.3 = bf16[96,1280]{1,0:T(8,128)(2,1)S(1)} collective-permute-done((bf16[96,1280]{1,0:T(8,128)(2,1)S(1)}, bf16[96,1280]{1,0:T(8,128)(2,1)S(1)}, u32[]{:S(2)}, u32[]{:S(2)}) %collective-permute-start.3) | collective-permute-done | bytes 245792 | tf_op jit(solution)/shard_map/ppermute | solution.py:628
  61.2 9.3 %collective-permute-done.6 = bf16[48,1920]{1,0:T(8,128)(2,1)} collective-permute-done((bf16[48,1920]{1,0:T(8,128)(2,1)}, bf16[48,1920]{1,0:T(8,128)(2,1)}, u32[]{:S(2)}, u32[]{:S(2)}) %collective-permute-start.6) | collective-permute-done | bytes 184352 | tf_op jit(solution)/shard_map/ppermute | solution.py:628
  76.1 6.0 %collective-permute-done.7.refs_5_ = bf16[96,1280]{1,0:T(8,128)(2,1)S(1)} collective-permute-done((bf16[96,1280]{1,0:T(8,128)(2,1)S(1)}, bf16[96,1280]{1,0:T(8,128)(2,1)S(1)}, u32[]{:S(2)}, u32[]{:S(2)}) %collective-permute-start.7) | collective-permute-done | bytes 245792 | tf_op jit(solution)/shard_map/ppermute | solution.py:628
  85.1 3.9 collective-permute-done.8.refs_6_
  95.3 4.8 shard_map.349.q_ref.k_ref.v_ref
  100.1 5.9 %collective-permute-done.15 = bf16[48,1536]{1,0:T(8,128)(2,1)} collective-permute-done((bf16[48,1536]{1,0:T(8,128)(2,1)}, bf16[48,1536]{1,0:T(8,128)(2,1)}, u32[]{:S(2)}, u32[]{:S(2)}) %collective-permute-start.15) | collective-permute-done | bytes 147488 | tf_op jit(solution)/shard_map/ppermute | solution.py:628
  107.1 9.8 %shard_map.350 = (bf16[512,768]{1,0:T(8,128)(2,1)}, bf16[12,512,512]{2,1,0:T(8,128)(2,1)S(1)}) custom-call(bf16[3,512,768]{2,1,0:T(8,128)(2,1)S(1)} %shard_map.349.q_ref.k_ref.v_ref, bf16[3,512,768]{2,1,0:T(8,128)(2,1)S(1)} %shard_map.349.q_ref.k_ref.v_ref, bf16[3,512,768]{2,1,0:T(8,128)(2,1)S(1)} %shard_map.349.q_ref.k_ref.v_ref, ...), custom_call_target="tpu_custom_call" | custom-call | flops 3221225472 | bytes 6291456 | tf_op jit(solution)/shard_map/pallas_call | solution.py:431
  116.9 2.6 copy-done.81
  119.5 7.1 %collective-permute-done.16.refs_1_ = bf16[192,1920]{1,0:T(8,128)(2,1)S(1)} collective-permute-done((bf16[192,1920]{1,0:T(8,128)(2,1)S(1)}, bf16[192,1920]{1,0:T(8,128)(2,1)S(1)}, u32[]{:S(2)}, u32[]{:S(2)}) %collective-permute-start.16) | collective-permute-done | bytes 737312 | tf_op jit(solution)/shard_map/ppermute | solution.py:628
  134.2 7.0 %collective-permute-done.18.refs_5_ = bf16[96,1920]{1,0:T(8,128)(2,1)S(1)} collective-permute-done((bf16[96,1920]{1,0:T(8,128)(2,1)S(1)}, bf16[96,1920]{1,0:T(8,128)(2,1)S(1)}, u32[]{:S(2)}, u32[]{:S(2)}) %collective-permute-start.18) | collective-permute-done | bytes 368672 | tf_op jit(solution)/shard_map/ppermute | solution.py:628
  144.8 3.6 shard_map.351
  149.1 7.1 %shard_map.352 = (bf16[4,512,768]{2,1,0:T(8,128)(2,1)S(1)}, bf16[4,512,768]{2,1,0:T(8,128)(2,1)S(1)}) custom-call(bf16[512,768]{1,0:T(8,128)(2,1)S(1)} %get-tuple-element.613.x_ref.refs_0_, bf16[192,1920]{1,0:T(8,128)(2,1)} %copy-done.92, bf16[192,1920]{1,0:T(8,128)(2,1)} %copy-done.90, bf16[192,1920]{1,0:T(8,128)(2,1)} %copy-done.93, ...), custom_call_target="tpu_custom_call" | custom-call | flops 2415919104 | bytes 11010048 | tf_op jit(solution)/shard_map/pallas_call | solution.py:155
  165.1 7.2 %collective-permute-done.28.refs_5_ = bf16[96,1536]{1,0:T(8,128)(2,1)S(1)} collective-permute-done((bf16[96,1536]{1,0:T(8,128)(2,1)}, bf16[96,1536]{1,0:T(8,128)(2,1)S(1)}, u32[]{:S(2)}, u32[]{:S(2)}) %collective-permute-start.28) | collective-permute-done | bytes 294944 | tf_op jit(solution)/shard_map/ppermute | solution.py:628
  179.2 6.3 %shard_map.353 = (f32[512,768]{1,0:T(8,128)S(1)}, f32[512,1]{1,0:T(8,128)S(1)}, bf16[512,768]{1,0:T(8,128)(2,1)S(1)}, bf16[512,384]{1,0:T(8,128)(2,1)S(1)}) custom-call(bf16[4,512,768]{2,1,0:T(8,128)(2,1)S(1)} %copy-done.9, bf16[192,1536]{1,0:T(8,128)(2,1)} %constant_dynamic-update-slice_fusion.9.refs_0_, bf16[192,1536]{1,0:T(8,128)(2,1)} %copy-done.98, ...), custom_call_target="tpu_custom_call" | custom-call | flops 2415919104 | bytes 12582912 | tf_op jit(solution)/shard_map/pallas_call | solution.py:255
  192.8 7.8 %shard_map.356 = (bf16[512,768]{1,0:T(8,128)(2,1)S(1)}, bf16[12,512,256]{2,1,0:T(8,128)(2,1)S(1)}) custom-call(bf16[1,512,768]{2,1,0:T(8,128)(2,1)S(1)} %shard_map.354.q_ref, bf16[2,256,768]{2,1,0:T(8,128)(2,1)S(1)} %shard_map.355.k_ref.v_ref, bf16[2,256,768]{2,1,0:T(8,128)(2,1)S(1)} %shard_map.355.k_ref.v_ref, bf16[512,128]{1,0:T(8,128)(2,1)S(1)} %copy-done.58, ...), custom_call_target="tpu_custom_call" | custom-call | flops 1610612736 | bytes 3145728 | tf_op jit(solution)/shard_map/pallas_call | solution.py:431
  202.2 3.6 shard_map.357
  205.9 6.4 %shard_map.358 = (bf16[4,512,768]{2,1,0:T(8,128)(2,1)S(1)}, bf16[4,512,768]{2,1,0:T(8,128)(2,1)S(1)}) custom-call(bf16[512,768]{1,0:T(8,128)(2,1)S(1)} %get-tuple-element.679.x_ref.refs_2_, s32[2,16]{1,0:T(2,128)S(1)} %broadcast_add_fusion.refs_0_.places, bf16[32,48,4608]{2,1,0:T(8,128)(2,1)} %bitcast.148), custom_call_target="tpu_custom_call" | custom-call | flops 2415919104 | bytes 11010048 | tf_op jit(solution)/shard_map/pallas_call | solution.py:155
  212.3 7.8 %shard_map.359 = (bf16[512,768]{1,0:T(8,128)(2,1)S(1)}, f32[512,768]{1,0:T(8,128)S(1)}, bf16[512,768]{1,0:T(8,128)(2,1)S(1)}, bf16[512,384]{1,0:T(8,128)(2,1)}, f32[2,768]{1,0:T(2,128)S(1)}) custom-call(bf16[4,512,768]{2,1,0:T(8,128)(2,1)S(1)} %get-tuple-element.683.h_ref.refs_1_, s32[2,16]{1,0:T(2,128)S(1)} %broadcast_add_fusion.refs_0_.places, ...), custom_call_target="tpu_custom_call" | custom-call | flops 2415919104 | bytes 12582912 | tf_op jit(solution)/shard_map/pallas_call | solution.py:255
  222.9 5.1 %shard_map.360.refs_3_.h_ref = bf16[4,512,768]{2,1,0:T(8,128)(2,1)S(1)} custom-call(bf16[512,768]{1,0:T(8,128)(2,1)S(1)} %get-tuple-element.694.x_ref.refs_0_, s32[2,16]{1,0:T(2,128)S(1)} %broadcast_add_fusion.refs_0_.places, bf16[32,48,4608]{2,1,0:T(8,128)(2,1)} %bitcast.150, bf16[4,512,768]{2,1,0:T(8,128)(2,1)S(1)} %get-tuple-element.695.refs_2_), custom_call_target="tpu_custom_call" | custom-call | flops 2415919104 | bytes 11010048 | tf_op jit(solution)/shard_map/pallas_call | solution.py:155
  228.0 6.6 %shard_map.362 = (f32[512,768]{1,0:T(8,128)S(1)}, bf16[512,768]{1,0:T(8,128)(2,1)S(1)}, bf16[512,384]{1,0:T(8,128)(2,1)S(1)}, f32[2,768]{1,0:T(2,128)S(1)}) custom-call(bf16[4,512,768]{2,1,0:T(8,128)(2,1)S(1)} %shard_map.360.refs_3_.h_ref, s32[2,16]{1,0:T(2,128)S(1)} %broadcast_add_fusion.refs_0_.places, bf16[32,48,4608]{2,1,0:T(8,128)(2,1)} %bitcast.151, ...), custom_call_target="tpu_custom_call" | custom-call | flops 2415919104 | bytes 12582912 | tf_op jit(solution)/shard_map/pallas_call | solution.py:255
  238.6 9.7 %shard_map.361 = bf16[32,48,3072]{2,1,0:T(8,128)(2,1)S(1)} custom-call(s32[2,16]{1,0:T(2,128)S(1)} %broadcast_add_fusion.refs_0_.places, bf16[512,768]{1,0:T(8,128)(2,1)S(1)} %get-tuple-element.694.x_ref.refs_0_, bf16[4,512,768]{2,1,0:T(8,128)(2,1)S(1)} %get-tuple-element.683.h_ref.refs_1_, bf16[512,768]{1,0:T(8,128)(2,1)S(1)} %get-tuple-element.679.x_ref.refs_2_, ...), custom_call_target="tpu_custom_call" | custom-call | flops 4831838208 | bytes 15728640 | tf_op jit(solution)/shard_map/pallas_call | solution.py:388
  248.3 3.7 copy-done.2
  262.6 8.7 %shard_map.364 = (bf16[1,512,768]{2,1,0:T(8,128)(2,1)S(1)}, bf16[2,256,768]{2,1,0:T(8,128)(2,1)S(1)}, f32[12,128,128]{2,1,0:T(8,128)S(1)}) custom-call(bf16[1,512,768]{2,1,0:T(8,128)(2,1)S(1)} %copy-done.31, bf16[2,256,768]{2,1,0:T(8,128)(2,1)S(1)} %copy-done.42, bf16[2,256,768]{2,1,0:T(8,128)(2,1)S(1)} %copy-done.42, bf16[512,768]{1,0:T(8,128)(2,1)S(1)} %bitcast.143, ...), custom_call_target="tpu_custom_call" | custom-call | flops 4026531840 | bytes 3145728 | tf_op jit(solution)/shard_map/pallas_call | solution.py:511
  271.4 3.1 shard_map.366
  275.7 2.8 shard_map.365
  280.2 5.7 %shard_map.367.h_ref.refs_2_ = bf16[4,512,768]{2,1,0:T(8,128)(2,1)S(1)} custom-call(bf16[512,768]{1,0:T(8,128)(2,1)S(1)} %get-tuple-element.744.x_ref.refs_12_, bf16[192,1536]{1,0:T(8,128)(2,1)} %constant_dynamic-update-slice_fusion.9.refs_0_, bf16[192,1536]{1,0:T(8,128)(2,1)} %copy-done.98, bf16[192,1536]{1,0:T(8,128)(2,1)} %copy-done.106, ...), custom_call_target="tpu_custom_call" | custom-call | flops 2415919104 | bytes 11010048 | tf_op jit(solution)/shard_map/pallas_call | solution.py:155
  287.1 2.9 collective-permute-done.41.refs_9_
  290.7 9.7 %shard_map.368 = (bf16[96,3072]{1,0:T(8,128)(2,1)S(1)}, bf16[96,3072]{1,0:T(8,128)(2,1)S(1)}, bf16[192,3072]{1,0:T(8,128)(2,1)S(1)}, bf16[192,3072]{1,0:T(8,128)(2,1)S(1)}, bf16[192,3072]{1,0:T(8,128)(2,1)S(1)}) custom-call(bf16[512,768]{1,0:T(8,128)(2,1)S(1)} %copy-done.25, bf16[512,384]{1,0:T(8,128)(2,1)} %collective-permute-done.38.refs_1_, ...), custom_call_target="tpu_custom_call" | custom-call | flops 4227858432 | bytes 18481152 | tf_op jit(solution)/shard_map/pallas_call | solution.py:336
  300.4 7.7 %shard_map.369 = (f32[512,768]{1,0:T(8,128)S(1)}, bf16[512,768]{1,0:T(8,128)(2,1)S(1)}, bf16[512,384]{1,0:T(8,128)(2,1)S(1)}, f32[2,768]{1,0:T(2,128)S(1)}) custom-call(bf16[4,512,768]{2,1,0:T(8,128)(2,1)S(1)} %shard_map.367.h_ref.refs_2_, bf16[192,1920]{1,0:T(8,128)(2,1)} %copy-done.92, bf16[192,1920]{1,0:T(8,128)(2,1)} %copy-done.90, ...), custom_call_target="tpu_custom_call" | custom-call | flops 2415919104 | bytes 12582912 | tf_op jit(solution)/shard_map/pallas_call | solution.py:255
  309.4 2.6 shard_map.370
  325.4 6.0 %collective-permute-done.45 = bf16[96,3072]{1,0:T(8,128)(2,1)} collective-permute-done((bf16[96,3072]{1,0:T(8,128)(2,1)}, bf16[96,3072]{1,0:T(8,128)(2,1)}, u32[]{:S(2)}, u32[]{:S(2)}) %collective-permute-start.45) | collective-permute-done | bytes 589856 | tf_op jit(solution)/shard_map/ppermute | solution.py:628
  332.5 2.4 add_dynamic-update-slice_fusion
  339.0 3.0 copy-done.82
  342.0 14.5 %shard_map.371 = (bf16[3,512,768]{2,1,0:T(8,128)(2,1)}, f32[12,128,128]{2,1,0:T(8,128)S(1)}) custom-call(bf16[3,512,768]{2,1,0:T(8,128)(2,1)S(1)} %copy-done.14, bf16[3,512,768]{2,1,0:T(8,128)(2,1)S(1)} %copy-done.14, bf16[3,512,768]{2,1,0:T(8,128)(2,1)S(1)} %copy-done.14, bf16[512,768]{1,0:T(8,128)(2,1)S(1)} %bitcast.144, ...), custom_call_target="tpu_custom_call" | custom-call | flops 8053063680 | bytes 6291456 | tf_op jit(solution)/shard_map/pallas_call | solution.py:511
  359.2 7.1 %shard_map.372 = (bf16[96,1920]{1,0:T(8,128)(2,1)S(1)}, bf16[96,1920]{1,0:T(8,128)(2,1)S(1)}, bf16[192,1920]{1,0:T(8,128)(2,1)S(1)}, bf16[192,1920]{1,0:T(8,128)(2,1)S(1)}, bf16[192,1920]{1,0:T(8,128)(2,1)S(1)}) custom-call(bf16[512,768]{1,0:T(8,128)(2,1)S(1)} %copy-done.71, bf16[512,384]{1,0:T(8,128)(2,1)} %collective-permute-done.48.refs_1_, ...), custom_call_target="tpu_custom_call" | custom-call | flops 3019898880 | bytes 12386304 | tf_op jit(solution)/shard_map/pallas_call | solution.py:336
  370.3 5.4 %shard_map.373 = bf16[512,768]{1,0:T(8,128)(2,1)S(1)} custom-call(bf16[3,512,768]{2,1,0:T(8,128)(2,1)} %get-tuple-element.859.h_ref.refs_2_, bf16[192,1280]{1,0:T(8,128)(2,1)} %constant_dynamic-update-slice_fusion.3.refs_0_, bf16[192,1280]{1,0:T(8,128)(2,1)} %collective-permute-done.4.refs_1_, bf16[192,1280]{1,0:T(8,128)(2,1)} %copy-done.107, ...), custom_call_target="tpu_custom_call" | custom-call | flops 1811939328 | bytes 10616832 | tf_op jit(solution)/shard_map/pallas_call | solution.py:255
  377.9 2.4 collective-permute-start.55
  380.3 4.8 collective-permute-done.56
  393.1 14.9 %collective-permute-done.55 = bf16[96,3072]{1,0:T(8,128)(2,1)} collective-permute-done((bf16[96,3072]{1,0:T(8,128)(2,1)}, bf16[96,3072]{1,0:T(8,128)(2,1)}, u32[]{:S(2)}, u32[]{:S(2)}) %collective-permute-start.55) | collective-permute-done | bytes 589856 | tf_op jit(solution)/shard_map/ppermute | solution.py:628
  410.5 5.2 %shard_map.374 = (bf16[96,1152]{1,0:T(8,128)(2,1)S(1)}, bf16[96,1152]{1,0:T(8,128)(2,1)S(1)}, bf16[192,1152]{1,0:T(8,128)(2,1)S(1)}, bf16[192,1152]{1,0:T(8,128)(2,1)S(1)}, bf16[192,1152]{1,0:T(8,128)(2,1)S(1)}) custom-call(bf16[512,768]{1,0:T(8,128)(2,1)S(1)} %copy-done.7, bf16[512,384]{1,0:T(8,128)(2,1)} %collective-permute-done.50.refs_1_, ...), custom_call_target="tpu_custom_call" | custom-call | flops 1811939328 | bytes 7274496 | tf_op jit(solution)/shard_map/pallas_call | solution.py:336
  435.5 3.9 collective-permute-done.69
  441.9 2.7 collective-permute-start.72
  445.0 4.2 collective-permute-done.66
  450.9 4.6 collective-permute-done.71
  464.1 8.2 %collective-permute-done.73 = bf16[48,1152]{1,0:T(8,128)(2,1)S(1)} collective-permute-done((bf16[48,1152]{1,0:T(8,128)(2,1)S(1)}, bf16[48,1152]{1,0:T(8,128)(2,1)S(1)}, u32[]{:S(2)}, u32[]{:S(2)}) %collective-permute-start.73) | collective-permute-done | bytes 110624 | tf_op jit(solution)/shard_map/ppermute | solution.py:628
  473.0 5.8 %reduce-scatter.2.cloned.1.call-done = bf16[48,3072]{1,0:T(8,128)(2,1)} async-done(((bf16[1536,3072]{1,0:T(8,128)(2,1)}), bf16[48,3072]{1,0:T(8,128)(2,1)}) %reduce-scatter.2.cloned.1.call-update) | async-done | bytes 294928 | tf_op jit(solution)/shard_map/reduce_scatter | solution.py:718
  (597 shorter events, 189.0 us)
Async XLA Ops:
  7.3 180.6 %all-gather.3.cloned.1.call-start = ((), (), s32[]{:S(2)}) async-start(), calls=%async_computation.2 | async-start | bytes 14598144 | tf_op jit(solution)/shard_map/all_gather | solution.py:704
  13.9 464.9 %reduce-scatter.2.cloned.1.call-start = ((), (), s32[]{:S(2)}) async-start(), calls=%async_computation.1 | async-start | bytes 9732096 | tf_op jit(solution)/shard_map/reduce_scatter | solution.py:718
  15.4 35.0 %collective-permute-start = (bf16[2,6,2,31]{3,2,1,0:T(2,128)(2,1)}, bf16[2,6,2,31]{3,2,1,0:T(2,128)(2,1)}, u32[]{:S(2)}, u32[]{:S(2)}) collective-permute-start(bf16[2,6,2,31]{3,2,1,0:T(2,128)(2,1)} %pad_maximum_fusion.7), channel_id=1, source_target_pairs={{0,1},{1,0},{2,3},{3,2},{4,5},{5,4},{6,7},{7,6},{8,9},{9,8},{10,11... | collective-permute-start | bytes 4472 | tf_op jit(solution)/shard_map/ppermute | solution.py:628
  19.2 31.3 %collective-permute-start.1 = (bf16[256,768]{1,0:T(8,128)(2,1)}, bf16[256,768]{1,0:T(8,128)(2,1)}, u32[]{:S(2)}, u32[]{:S(2)}) collective-permute-start(bf16[256,768]{1,0:T(8,128)(2,1)} %select_bitcast_fusion.4), channel_id=1, source_target_pairs={{0,1},{1,0},{2,3},{3,2},{4,5},{5,4},{6,7},{7,6},{8,9},{9,8},{10,11... | collective-permute-start | bytes 1179656 | tf_op jit(solution)/shard_map/ppermute | solution.py:628
  19.2 11.9 %collective-permute-start.2 = (bf16[48,1280]{1,0:T(8,128)(2,1)}, bf16[48,1280]{1,0:T(8,128)(2,1)}, u32[]{:S(2)}, u32[]{:S(2)}) collective-permute-start(bf16[48,1280]{1,0:T(8,128)(2,1)} %fusion.33), channel_id=1, source_target_pairs={{0,16},{1,17},{2,18},{3,19},{4,20},{5,21},{6,22},{7,23},{8,24},{9,... | collective-permute-start | bytes 368648 | tf_op jit(solution)/shard_map/ppermute | solution.py:628
  32.1 12.6 %collective-permute-start.3 = (bf16[96,1280]{1,0:T(8,128)(2,1)S(1)}, bf16[96,1280]{1,0:T(8,128)(2,1)S(1)}, u32[]{:S(2)}, u32[]{:S(2)}) collective-permute-start(bf16[96,1280]{1,0:T(8,128)(2,1)S(1)} %pad_maximum_fusion.3), channel_id=1, source_target_pairs={{0,8},{1,9},{2,10},{3,11},{4,12},{5,13},{6,14},{7,15},{8,0},{9,1},... | collective-permute-start | bytes 737288 | tf_op jit(solution)/shard_map/ppermute | solution.py:628
  46.8 25.4 %collective-permute-start.4 = (bf16[192,1280]{1,0:T(8,128)(2,1)}, bf16[192,1280]{1,0:T(8,128)(2,1)}, u32[]{:S(2)}, u32[]{:S(2)}) collective-permute-start(bf16[192,1280]{1,0:T(8,128)(2,1)} %constant_dynamic-update-slice_fusion.3.refs_0_), channel_id=1, source_target_pairs={{0,4},{1,5},{2,6},{3,7},{4,0},{5,1},{6,2},{7,3},{8,12},{9,13},{10,... | collective-permute-start | bytes 1474568 | tf_op jit(solution)/shard_map/ppermute | solution.py:628
  48.2 23.9 %collective-permute-start.5 = (bf16[192,1280]{1,0:T(8,128)(2,1)}, bf16[192,1280]{1,0:T(8,128)(2,1)}, u32[]{:S(2)}, u32[]{:S(2)}) collective-permute-start(bf16[192,1280]{1,0:T(8,128)(2,1)} %constant_dynamic-update-slice_fusion.3.refs_0_), channel_id=1, source_target_pairs={{0,1},{1,0},{2,3},{3,2},{4,5},{5,4},{6,7},{7,6},{8,9},{9,8},{10,11... | collective-permute-start | bytes 1474568 | tf_op jit(solution)/shard_map/ppermute | solution.py:628
  50.4 20.0 %collective-permute-start.6 = (bf16[48,1920]{1,0:T(8,128)(2,1)}, bf16[48,1920]{1,0:T(8,128)(2,1)}, u32[]{:S(2)}, u32[]{:S(2)}) collective-permute-start(bf16[48,1920]{1,0:T(8,128)(2,1)} %pad_maximum_fusion.4), channel_id=1, source_target_pairs={{0,16},{1,17},{2,18},{3,19},{4,20},{5,21},{6,22},{7,23},{8,24},{9,... | collective-permute-start | bytes 552968 | tf_op jit(solution)/shard_map/ppermute | solution.py:628
  75.0 14.0 %collective-permute-start.9 = (bf16[192,1280]{1,0:T(8,128)(2,1)}, bf16[192,1280]{1,0:T(8,128)(2,1)S(1)}, u32[]{:S(2)}, u32[]{:S(2)}) collective-permute-start(bf16[192,1280]{1,0:T(8,128)(2,1)} %constant_dynamic-update-slice_fusion.3.refs_0_), channel_id=1, source_target_pairs={{0,2},{1,3},{2,0},{3,1},{4,6},{5,7},{6,4},{7,5},{8,10},{9,11},{10,... | collective-permute-start | bytes 1474568 | tf_op jit(solution)/shard_map/ppermute | solution.py:628
  75.0 14.0 %collective-permute-start.10 = (bf16[192,1280]{1,0:T(8,128)(2,1)}, bf16[192,1280]{1,0:T(8,128)(2,1)}, u32[]{:S(2)}, u32[]{:S(2)}) collective-permute-start(bf16[192,1280]{1,0:T(8,128)(2,1)} %collective-permute-done.4.refs_1_), channel_id=1, source_target_pairs={{0,2},{1,3},{2,0},{3,1},{4,6},{5,7},{6,4},{7,5},{8,10},{9,11},{10,... | collective-permute-start | bytes 1474568 | tf_op jit(solution)/shard_map/ppermute | solution.py:628
  75.5 13.5 %collective-permute-start.11 = (bf16[192,1280]{1,0:T(8,128)(2,1)}, bf16[192,1280]{1,0:T(8,128)(2,1)}, u32[]{:S(2)}, u32[]{:S(2)}) collective-permute-start(bf16[192,1280]{1,0:T(8,128)(2,1)} %collective-permute-done.5.refs_4_), channel_id=1, source_target_pairs={{0,2},{1,3},{2,0},{3,1},{4,6},{5,7},{6,4},{7,5},{8,10},{9,11},{10,... | collective-permute-start | bytes 1474568 | tf_op jit(solution)/shard_map/ppermute | solution.py:628
  76.1 13.6 %collective-permute-start.14 = (bf16[96,1920]{1,0:T(8,128)(2,1)}, bf16[96,1920]{1,0:T(8,128)(2,1)}, u32[]{:S(2)}, u32[]{:S(2)}) collective-permute-start(bf16[96,1920]{1,0:T(8,128)(2,1)} %pad_maximum_fusion.1), channel_id=1, source_target_pairs={{0,8},{1,9},{2,10},{3,11},{4,12},{5,13},{6,14},{7,15},{8,0},{9,1},... | collective-permute-start | bytes 1105928 | tf_op jit(solution)/shard_map/ppermute | solution.py:628
  89.0 17.0 %collective-permute-start.15 = (bf16[48,1536]{1,0:T(8,128)(2,1)}, bf16[48,1536]{1,0:T(8,128)(2,1)}, u32[]{:S(2)}, u32[]{:S(2)}) collective-permute-start(bf16[48,1536]{1,0:T(8,128)(2,1)} %bitcast.10), channel_id=1, source_target_pairs={{0,16},{1,17},{2,18},{3,19},{4,20},{5,21},{6,22},{7,23},{8,24},{9,... | collective-permute-start | bytes 442376 | tf_op jit(solution)/shard_map/ppermute | solution.py:628
  91.8 34.9 %collective-permute-start.16 = (bf16[192,1920]{1,0:T(8,128)(2,1)S(1)}, bf16[192,1920]{1,0:T(8,128)(2,1)S(1)}, u32[]{:S(2)}, u32[]{:S(2)}) collective-permute-start(bf16[192,1920]{1,0:T(8,128)(2,1)S(1)} %constant_dynamic-update-slice_fusion.6.refs_0_), channel_id=1, source_target_pairs={{0,4},{1,5},{2,6},{3,7},{4,0},{5,1},{6,2},{7,3},{8,12},{9,13},{10,... | collective-permute-start | bytes 2211848 | tf_op jit(solution)/shard_map/ppermute | solution.py:628
  93.3 34.7 %collective-permute-start.17 = (bf16[192,1920]{1,0:T(8,128)(2,1)S(1)}, bf16[192,1920]{1,0:T(8,128)(2,1)S(1)}, u32[]{:S(2)}, u32[]{:S(2)}) collective-permute-start(bf16[192,1920]{1,0:T(8,128)(2,1)S(1)} %constant_dynamic-update-slice_fusion.6.refs_0_), channel_id=1, source_target_pairs={{0,1},{1,0},{2,3},{3,2},{4,5},{5,4},{6,7},{7,6},{8,9},{9,8},{10,11... | collective-permute-start | bytes 2211848 | tf_op jit(solution)/shard_map/ppermute | solution.py:628
  107.0 23.9 %collective-permute-start.23 = (bf16[96,1536]{1,0:T(8,128)(2,1)S(1)}, bf16[96,1536]{1,0:T(8,128)(2,1)S(1)}, u32[]{:S(2)}, u32[]{:S(2)}) collective-permute-start(bf16[96,1536]{1,0:T(8,128)(2,1)S(1)} %pad_maximum_fusion.2), channel_id=1, source_target_pairs={{0,8},{1,9},{2,10},{3,11},{4,12},{5,13},{6,14},{7,15},{8,0},{9,1},... | collective-permute-start | bytes 884744 | tf_op jit(solution)/shard_map/ppermute | solution.py:628
  128.1 13.5 %collective-permute-start.20 = (bf16[192,1920]{1,0:T(8,128)(2,1)S(1)}, bf16[192,1920]{1,0:T(8,128)(2,1)S(1)}, u32[]{:S(2)}, u32[]{:S(2)}) collective-permute-start(bf16[192,1920]{1,0:T(8,128)(2,1)S(1)} %constant_dynamic-update-slice_fusion.6.refs_0_), channel_id=1, source_target_pairs={{0,2},{1,3},{2,0},{3,1},{4,6},{5,7},{6,4},{7,5},{8,10},{9,11},{10,... | collective-permute-start | bytes 2211848 | tf_op jit(solution)/shard_map/ppermute | solution.py:628
  128.1 13.4 %collective-permute-start.21 = (bf16[192,1920]{1,0:T(8,128)(2,1)S(1)}, bf16[192,1920]{1,0:T(8,128)(2,1)S(1)}, u32[]{:S(2)}, u32[]{:S(2)}) collective-permute-start(bf16[192,1920]{1,0:T(8,128)(2,1)S(1)} %collective-permute-done.16.refs_1_), channel_id=1, source_target_pairs={{0,2},{1,3},{2,0},{3,1},{4,6},{5,7},{6,4},{7,5},{8,10},{9,11},{10,... | collective-permute-start | bytes 2211848 | tf_op jit(solution)/shard_map/ppermute | solution.py:628
  128.6 12.9 %collective-permute-start.22 = (bf16[192,1920]{1,0:T(8,128)(2,1)S(1)}, bf16[192,1920]{1,0:T(8,128)(2,1)S(1)}, u32[]{:S(2)}, u32[]{:S(2)}) collective-permute-start(bf16[192,1920]{1,0:T(8,128)(2,1)S(1)} %collective-permute-done.17.refs_4_), channel_id=1, source_target_pairs={{0,2},{1,3},{2,0},{3,1},{4,6},{5,7},{6,4},{7,5},{8,10},{9,11},{10,... | collective-permute-start | bytes 2211848 | tf_op jit(solution)/shard_map/ppermute | solution.py:628
  130.3 10.9 %collective-permute-start.18 = (bf16[96,1920]{1,0:T(8,128)(2,1)S(1)}, bf16[96,1920]{1,0:T(8,128)(2,1)S(1)}, u32[]{:S(2)}, u32[]{:S(2)}) collective-permute-start(bf16[96,1920]{1,0:T(8,128)(2,1)S(1)} %slice.252), channel_id=1, source_target_pairs={{0,4},{1,5},{2,6},{3,7},{4,0},{5,1},{6,2},{7,3},{8,12},{9,13},{10,... | collective-permute-start | bytes 1105928 | tf_op jit(solution)/shard_map/ppermute | solution.py:628
  142.1 17.4 %collective-permute-start.26 = (bf16[192,1536]{1,0:T(8,128)(2,1)}, bf16[192,1536]{1,0:T(8,128)(2,1)S(1)}, u32[]{:S(2)}, u32[]{:S(2)}) collective-permute-start(bf16[192,1536]{1,0:T(8,128)(2,1)} %constant_dynamic-update-slice_fusion.9.refs_0_), channel_id=1, source_target_pairs={{0,4},{1,5},{2,6},{3,7},{4,0},{5,1},{6,2},{7,3},{8,12},{9,13},{10,... | collective-permute-start | bytes 1769480 | tf_op jit(solution)/shard_map/ppermute | solution.py:628
  143.6 16.0 %collective-permute-start.27 = (bf16[192,1536]{1,0:T(8,128)(2,1)}, bf16[192,1536]{1,0:T(8,128)(2,1)}, u32[]{:S(2)}, u32[]{:S(2)}) collective-permute-start(bf16[192,1536]{1,0:T(8,128)(2,1)} %constant_dynamic-update-slice_fusion.9.refs_0_), channel_id=1, source_target_pairs={{0,1},{1,0},{2,3},{3,2},{4,5},{5,4},{6,7},{7,6},{8,9},{9,8},{10,11... | collective-permute-start | bytes 1769480 | tf_op jit(solution)/shard_map/ppermute | solution.py:628
  162.2 11.2 %collective-permute-start.30 = (bf16[192,1536]{1,0:T(8,128)(2,1)}, bf16[192,1536]{1,0:T(8,128)(2,1)S(1)}, u32[]{:S(2)}, u32[]{:S(2)}) collective-permute-start(bf16[192,1536]{1,0:T(8,128)(2,1)} %constant_dynamic-update-slice_fusion.9.refs_0_), channel_id=1, source_target_pairs={{0,2},{1,3},{2,0},{3,1},{4,6},{5,7},{6,4},{7,5},{8,10},{9,11},{10,... | collective-permute-start | bytes 1769480 | tf_op jit(solution)/shard_map/ppermute | solution.py:628
  162.2 11.2 %collective-permute-start.31 = (bf16[192,1536]{1,0:T(8,128)(2,1)S(1)}, bf16[192,1536]{1,0:T(8,128)(2,1)}, u32[]{:S(2)}, u32[]{:S(2)}) collective-permute-start(bf16[192,1536]{1,0:T(8,128)(2,1)S(1)} %collective-permute-done.26.refs_1_), channel_id=1, source_target_pairs={{0,2},{1,3},{2,0},{3,1},{4,6},{5,7},{6,4},{7,5},{8,10},{9,11},{10,... | collective-permute-start | bytes 1769480 | tf_op jit(solution)/shard_map/ppermute | solution.py:628
  221.9 30.2 %collective-permute-start.35 = (bf16[256,768]{1,0:T(8,128)(2,1)}, bf16[256,768]{1,0:T(8,128)(2,1)}, u32[]{:S(2)}, u32[]{:S(2)}) collective-permute-start(bf16[256,768]{1,0:T(8,128)(2,1)} %get-tuple-element.693), channel_id=1, source_target_pairs={{0,1},{1,0},{2,3},{3,2},{4,5},{5,4},{6,7},{7,6},{8,9},{9,8},{10,11... | collective-permute-start | bytes 1179656 | tf_op jit(solution)/shard_map/ppermute | solution.py:628
  252.0 19.3 %collective-permute-start.37 = (bf16[4,512,768]{2,1,0:T(8,128)(2,1)}, bf16[4,512,768]{2,1,0:T(8,128)(2,1)}, u32[]{:S(2)}, u32[]{:S(2)}) collective-permute-start(bf16[4,512,768]{2,1,0:T(8,128)(2,1)} %copy-done.8), channel_id=1, source_target_pairs={{0,2},{1,3},{2,0},{3,1},{4,6},{5,7},{6,4},{7,5},{8,10},{9,11},{10,... | collective-permute-start | bytes 9437192 | tf_op jit(solution)/shard_map/ppermute | solution.py:628
  252.0 19.3 %collective-permute-start.39 = (bf16[1,512,768]{2,1,0:T(8,128)(2,1)}, bf16[1,512,768]{2,1,0:T(8,128)(2,1)}, u32[]{:S(2)}, u32[]{:S(2)}) collective-permute-start(bf16[1,512,768]{2,1,0:T(8,128)(2,1)} %bitcast.141), channel_id=1, source_target_pairs={{0,2},{1,3},{2,0},{3,1},{4,6},{5,7},{6,4},{7,5},{8,10},{9,11},{10,... | collective-permute-start | bytes 2359304 | tf_op jit(solution)/shard_map/ppermute | solution.py:628
  252.5 18.8 %collective-permute-start.38 = (bf16[512,384]{1,0:T(8,128)(2,1)}, bf16[512,384]{1,0:T(8,128)(2,1)}, u32[]{:S(2)}, u32[]{:S(2)}) collective-permute-start(bf16[512,384]{1,0:T(8,128)(2,1)} %copy-done.78), channel_id=1, source_target_pairs={{0,2},{1,3},{2,0},{3,1},{4,6},{5,7},{6,4},{7,5},{8,10},{9,11},{10,... | collective-permute-start | bytes 1179656 | tf_op jit(solution)/shard_map/ppermute | solution.py:628
  254.2 17.1 %collective-permute-start.36 = (bf16[256,384]{1,0:T(8,128)(2,1)}, bf16[256,384]{1,0:T(8,128)(2,1)S(1)}, u32[]{:S(2)}, u32[]{:S(2)}) collective-permute-start(bf16[256,384]{1,0:T(8,128)(2,1)} %slice.259), channel_id=1, source_target_pairs={{0,2},{1,3},{2,0},{3,1},{4,6},{5,7},{6,4},{7,5},{8,10},{9,11},{10,... | collective-permute-start | bytes 589832 | tf_op jit(solution)/shard_map/ppermute | solution.py:628
  315.4 16.0 %collective-permute-start.45 = (bf16[96,3072]{1,0:T(8,128)(2,1)}, bf16[96,3072]{1,0:T(8,128)(2,1)}, u32[]{:S(2)}, u32[]{:S(2)}) collective-permute-start(bf16[96,3072]{1,0:T(8,128)(2,1)} %copy-done.73), channel_id=1, source_target_pairs={{0,4},{1,5},{2,6},{3,7},{4,0},{5,1},{6,2},{7,3},{8,12},{9,13},{10,... | collective-permute-start | bytes 1769480 | tf_op jit(solution)/shard_map/ppermute | solution.py:628
  316.8 15.6 %collective-permute-start.46 = (bf16[96,3072]{1,0:T(8,128)(2,1)}, bf16[96,3072]{1,0:T(8,128)(2,1)}, u32[]{:S(2)}, u32[]{:S(2)}) collective-permute-start(bf16[96,3072]{1,0:T(8,128)(2,1)} %copy-done.72), channel_id=1, source_target_pairs={{0,1},{1,0},{2,3},{3,2},{4,5},{5,4},{6,7},{7,6},{8,9},{9,8},{10,11... | collective-permute-start | bytes 1769480 | tf_op jit(solution)/shard_map/ppermute | solution.py:628
  337.3 31.6 %collective-permute-start.51 = (bf16[192,3072]{1,0:T(8,128)(2,1)}, bf16[192,3072]{1,0:T(8,128)(2,1)S(1)}, u32[]{:S(2)}, u32[]{:S(2)}) collective-permute-start(bf16[192,3072]{1,0:T(8,128)(2,1)} %add_dynamic-update-slice_fusion), channel_id=1, source_target_pairs={{0,4},{1,5},{2,6},{3,7},{4,0},{5,1},{6,2},{7,3},{8,12},{9,13},{10,... | collective-permute-start | bytes 3538952 | tf_op jit(solution)/shard_map/ppermute | solution.py:628
  337.9 31.0 %collective-permute-start.52 = (bf16[192,3072]{1,0:T(8,128)(2,1)}, bf16[192,3072]{1,0:T(8,128)(2,1)S(1)}, u32[]{:S(2)}, u32[]{:S(2)}) collective-permute-start(bf16[192,3072]{1,0:T(8,128)(2,1)} %add_dynamic-update-slice_fusion.1), channel_id=1, source_target_pairs={{0,1},{1,0},{2,3},{3,2},{4,5},{5,4},{6,7},{7,6},{8,9},{9,8},{10,11... | collective-permute-start | bytes 3538952 | tf_op jit(solution)/shard_map/ppermute | solution.py:628
  366.4 18.7 %collective-permute-start.56 = (bf16[96,1920]{1,0:T(8,128)(2,1)S(1)}, bf16[96,1920]{1,0:T(8,128)(2,1)S(1)}, u32[]{:S(2)}, u32[]{:S(2)}) collective-permute-start(bf16[96,1920]{1,0:T(8,128)(2,1)S(1)} %get-tuple-element.841), channel_id=1, source_target_pairs={{0,4},{1,5},{2,6},{3,7},{4,0},{5,1},{6,2},{7,3},{8,12},{9,13},{10,... | collective-permute-start | bytes 1105928 | tf_op jit(solution)/shard_map/ppermute | solution.py:628
  367.4 18.5 %collective-permute-start.57 = (bf16[96,1920]{1,0:T(8,128)(2,1)S(1)}, bf16[96,1920]{1,0:T(8,128)(2,1)S(1)}, u32[]{:S(2)}, u32[]{:S(2)}) collective-permute-start(bf16[96,1920]{1,0:T(8,128)(2,1)S(1)} %get-tuple-element.842), channel_id=1, source_target_pairs={{0,1},{1,0},{2,3},{3,2},{4,5},{5,4},{6,7},{7,6},{8,9},{9,8},{10,11... | collective-permute-start | bytes 1105928 | tf_op jit(solution)/shard_map/ppermute | solution.py:628
  377.4 31.7 %collective-permute-start.54 = (bf16[256,768]{1,0:T(8,128)(2,1)}, bf16[256,768]{1,0:T(8,128)(2,1)}, u32[]{:S(2)}, u32[]{:S(2)}) collective-permute-start(bf16[256,768]{1,0:T(8,128)(2,1)} %get-tuple-element.838), channel_id=1, source_target_pairs={{0,1},{1,0},{2,3},{3,2},{4,5},{5,4},{6,7},{7,6},{8,9},{9,8},{10,11... | collective-permute-start | bytes 1179656 | tf_op jit(solution)/shard_map/ppermute | solution.py:628
  377.9 30.1 %collective-permute-start.55 = (bf16[96,3072]{1,0:T(8,128)(2,1)}, bf16[96,3072]{1,0:T(8,128)(2,1)}, u32[]{:S(2)}, u32[]{:S(2)}) collective-permute-start(bf16[96,3072]{1,0:T(8,128)(2,1)} %get-tuple-element.839), channel_id=1, source_target_pairs={{0,8},{1,9},{2,10},{3,11},{4,12},{5,13},{6,14},{7,15},{8,0},{9,1},... | collective-permute-start | bytes 1769480 | tf_op jit(solution)/shard_map/ppermute | solution.py:628
  385.9 24.5 %collective-permute-start.58 = (bf16[3,512,768]{2,1,0:T(8,128)(2,1)}, bf16[3,512,768]{2,1,0:T(8,128)(2,1)}, u32[]{:S(2)}, u32[]{:S(2)}) collective-permute-start(bf16[3,512,768]{2,1,0:T(8,128)(2,1)} %get-tuple-element.859.h_ref.refs_2_), channel_id=1, source_target_pairs={{0,2},{1,3},{2,0},{3,1},{4,6},{5,7},{6,4},{7,5},{8,10},{9,11},{10,... | collective-permute-start | bytes 7077896 | tf_op jit(solution)/shard_map/ppermute | solution.py:628
  391.0 26.6 %collective-permute-start.62 = (bf16[192,1920]{1,0:T(8,128)(2,1)S(1)}, bf16[192,1920]{1,0:T(8,128)(2,1)S(1)}, u32[]{:S(2)}, u32[]{:S(2)}) collective-permute-start(bf16[192,1920]{1,0:T(8,128)(2,1)S(1)} %add_dynamic-update-slice_fusion.2), channel_id=1, source_target_pairs={{0,4},{1,5},{2,6},{3,7},{4,0},{5,1},{6,2},{7,3},{8,12},{9,13},{10,... | collective-permute-start | bytes 2211848 | tf_op jit(solution)/shard_map/ppermute | solution.py:628
  392.4 26.3 %collective-permute-start.63 = (bf16[192,1920]{1,0:T(8,128)(2,1)S(1)}, bf16[192,1920]{1,0:T(8,128)(2,1)S(1)}, u32[]{:S(2)}, u32[]{:S(2)}) collective-permute-start(bf16[192,1920]{1,0:T(8,128)(2,1)S(1)} %add_dynamic-update-slice_fusion.3), channel_id=1, source_target_pairs={{0,1},{1,0},{2,3},{3,2},{4,5},{5,4},{6,7},{7,6},{8,9},{9,8},{10,11... | collective-permute-start | bytes 2211848 | tf_op jit(solution)/shard_map/ppermute | solution.py:628
  409.1 15.0 %collective-permute-start.61 = (bf16[48,3072]{1,0:T(8,128)(2,1)S(1)}, bf16[48,3072]{1,0:T(8,128)(2,1)S(1)}, u32[]{:S(2)}, u32[]{:S(2)}) collective-permute-start(bf16[48,3072]{1,0:T(8,128)(2,1)S(1)} %fusion.14), channel_id=1, source_target_pairs={{0,16},{1,17},{2,18},{3,19},{4,20},{5,21},{6,22},{7,23},{8,24},{9,... | collective-permute-start | bytes 884744 | tf_op jit(solution)/shard_map/ppermute | solution.py:628
  422.6 16.8 %collective-permute-start.69 = (bf16[96,1920]{1,0:T(8,128)(2,1)}, bf16[96,1920]{1,0:T(8,128)(2,1)}, u32[]{:S(2)}, u32[]{:S(2)}) collective-permute-start(bf16[96,1920]{1,0:T(8,128)(2,1)} %get-tuple-element.904), channel_id=1, source_target_pairs={{0,8},{1,9},{2,10},{3,11},{4,12},{5,13},{6,14},{7,15},{8,0},{9,1},... | collective-permute-start | bytes 1105928 | tf_op jit(solution)/shard_map/ppermute | solution.py:628
  431.6 13.4 %collective-permute-start.65 = (bf16[192,1152]{1,0:T(8,128)(2,1)S(1)}, bf16[192,1152]{1,0:T(8,128)(2,1)S(1)}, u32[]{:S(2)}, u32[]{:S(2)}) collective-permute-start(bf16[192,1152]{1,0:T(8,128)(2,1)S(1)} %add_dynamic-update-slice_fusion.5), channel_id=1, source_target_pairs={{0,4},{1,5},{2,6},{3,7},{4,0},{5,1},{6,2},{7,3},{8,12},{9,13},{10,... | collective-permute-start | bytes 1327112 | tf_op jit(solution)/shard_map/ppermute | solution.py:628
  432.5 16.6 %collective-permute-start.66 = (bf16[192,1152]{1,0:T(8,128)(2,1)S(1)}, bf16[192,1152]{1,0:T(8,128)(2,1)S(1)}, u32[]{:S(2)}, u32[]{:S(2)}) collective-permute-start(bf16[192,1152]{1,0:T(8,128)(2,1)S(1)} %add_dynamic-update-slice_fusion.4), channel_id=1, source_target_pairs={{0,1},{1,0},{2,3},{3,2},{4,5},{5,4},{6,7},{7,6},{8,9},{9,8},{10,11... | collective-permute-start | bytes 1327112 | tf_op jit(solution)/shard_map/ppermute | solution.py:628
  440.3 15.1 %collective-permute-start.71 = (bf16[48,1920]{1,0:T(8,128)(2,1)S(1)}, bf16[48,1920]{1,0:T(8,128)(2,1)S(1)}, u32[]{:S(2)}, u32[]{:S(2)}) collective-permute-start(bf16[48,1920]{1,0:T(8,128)(2,1)S(1)} %fusion.18), channel_id=1, source_target_pairs={{0,16},{1,17},{2,18},{3,19},{4,20},{5,21},{6,22},{7,23},{8,24},{9,... | collective-permute-start | bytes 552968 | tf_op jit(solution)/shard_map/ppermute | solution.py:628
  449.3 11.1 %collective-permute-start.70 = (bf16[96,1152]{1,0:T(8,128)(2,1)S(1)}, bf16[96,1152]{1,0:T(8,128)(2,1)S(1)}, u32[]{:S(2)}, u32[]{:S(2)}) collective-permute-start(bf16[96,1152]{1,0:T(8,128)(2,1)S(1)} %get-tuple-element.915), channel_id=1, source_target_pairs={{0,8},{1,9},{2,10},{3,11},{4,12},{5,13},{6,14},{7,15},{8,0},{9,1},... | collective-permute-start | bytes 663560 | tf_op jit(solution)/shard_map/ppermute | solution.py:628
  460.5 11.8 %collective-permute-start.73 = (bf16[48,1152]{1,0:T(8,128)(2,1)S(1)}, bf16[48,1152]{1,0:T(8,128)(2,1)S(1)}, u32[]{:S(2)}, u32[]{:S(2)}) collective-permute-start(bf16[48,1152]{1,0:T(8,128)(2,1)S(1)} %fusion.26), channel_id=1, source_target_pairs={{0,16},{1,17},{2,18},{3,19},{4,20},{5,21},{6,22},{7,23},{8,24},{9,... | collective-permute-start | bytes 331784 | tf_op jit(solution)/shard_map/ppermute | solution.py:628
  (180 other events, 1291.0 us)
Sparse Core Ops, SparseCore 0:
  14.0 135.9 all-gather.2
  315.5 163.2 reduce-scatter.1
